TPU v7x, 32 devices: a whole 2x2x4 slice. The times are simulated.
32 devices in a mesh: lon: 8 (over z, x), lat: 4 (over y, core).
Axes of the slice: x: 2, y: 2, z: 4, core: 2. Of those that a mesh axis runs over, the one named last changes fastest.
Arguments:
- state_field: float32 [2, 137, 128, 1024], P(None, None, 'lat', 'lon'), may hold values from -6 to 6
- jacobian: bfloat16 [4, 512, 2, 137, 128], P('lat', 'lon'), may hold values from -0.375 to 0.375
- observed: bfloat16 [4, 512, 128], P('lat', 'lon'), may hold values from -6 to 6
- inverse_var: bfloat16 [4, 512, 128], P('lat', 'lon'), may hold values from 0.25 to 4
- valid_count: int32 [4, 512], P('lat', 'lon'), may hold values from 32 to 128
- destination: int32 [4, 512, 1], P('lat', 'lon'), may hold values from 0 to 7; in each aligned block of 64 rows (0 to 63, 64 to 127, ..., all dimensions but the last counted through in order) at most 16 rows name the same one
- column: int32 [4, 512], P('lat', 'lon'), may hold values from 0 to 4095
- vertical: bfloat16 [2, 137, 137], replicated, may hold values from -0.5 to 0.5
- lon_taps: float32 [2, 137, 9], replicated, may hold values from 0.05 to 0.3
- lat_taps: float32 [2, 137, 9], replicated, may hold values from 0.05 to 0.3
Outputs:
- gradient: float32 [2, 137, 128, 1024], P(None, None, 'lat', 'lon')
Inputs may be any that keep to these rules, and one draw needn't show every extreme that they name: `destination`: among the 64 records of one device no longitude tile is named more than 16 times, a bound that some block reaches.
All inputs are finite; a program needn't handle non-finite values.
Results may differ from a plain program's by a relative error of at most 0.0045.
Values may be sent and summed in bfloat16 or wider, within the bound.
No kernel may reach another device: no remote copies, remote signals or barrier semaphores. Data moves between devices by JAX's collectives and lax.ppermute only.
A program may use at most 128 MiB of HBM per device.

v0:
```python
import jax
import jax.numpy as jnp
from jax import lax
from jax.sharding import PartitionSpec as P


def padded(cells, sides, width, closed):
    for axis, dim in sides:
        count = lax.axis_size(axis)
        ends = count if closed else count - 1
        head = lax.slice_in_dim(cells, 0, width, axis=dim)
        tail = lax.slice_in_dim(cells, cells.shape[dim] - width, cells.shape[dim], axis=dim)
        cells = jnp.concatenate(
            [
                lax.ppermute(tail, axis, [(i, (i + 1) % count) for i in range(ends)]),
                cells,
                lax.ppermute(head, axis, [((i + 1) % count, i) for i in range(ends)]),
            ],
            axis=dim,
        )
    return cells


def slot_layout(dest_local, lon_devices, capacity):
    onehot = (dest_local[:, None] == jnp.arange(lon_devices, dtype=jnp.int32)[None, :]).astype(
        jnp.int32
    )
    before = jnp.cumsum(onehot, axis=0) - onehot
    ranking = jnp.sum(before * onehot, axis=1)
    return dest_local * capacity + ranking


def departures(jac_rows, state_cols, obs_rows, weight_rows):
    model = jnp.einsum("...fc,...f->...c", jac_rows, state_cols, preferred_element_type=jnp.float32)
    misfit = weight_rows.astype(jnp.float32) * (model - obs_rows.astype(jnp.float32))
    scaled = misfit.astype(jnp.bfloat16)
    return jnp.einsum("...fc,...c->...f", jac_rows, scaled, preferred_element_type=jnp.float32)


def lon_filter(extended, taps, width):
    result = jnp.zeros(extended.shape[:-1] + (width,), jnp.float32)
    for offset in range(taps.shape[-1]):
        result = (
            result + taps[:, :, offset][:, :, None, None] * extended[..., offset : offset + width]
        )
    return result


def lat_filter(extended, taps, height):
    result = jnp.zeros(extended.shape[:2] + (height, extended.shape[3]), jnp.float32)
    for offset in range(taps.shape[-1]):
        result = (
            result
            + taps[:, :, offset][:, :, None, None] * extended[:, :, offset : offset + height, :]
        )
    return result


def body(
    state_field,
    jacobian,
    observed,
    inverse_var,
    valid_count,
    destination,
    column,
    vertical,
    lon_taps,
    lat_taps,
):
    lon_devices = lax.axis_size("lon")
    var_count, level_count, row_count, col_count = state_field.shape
    features = var_count * level_count
    records = jacobian.shape[1]
    channels = jacobian.shape[-1]
    capacity = max(2, 2 * records // lon_devices)
    slot_total = lon_devices * capacity
    jac_rows = jacobian.reshape(records, features, channels)
    dest_local = destination.reshape(records)
    col_local = column.reshape(records)
    alive_mask = (
        jnp.arange(channels, dtype=jnp.int32)[None, :] < valid_count.reshape(records)[:, None]
    )
    weight_rows = jnp.where(
        alive_mask, inverse_var.reshape(records, channels), jnp.zeros((), jnp.bfloat16)
    )
    obs_rows = observed.reshape(records, channels)
    slots = slot_layout(dest_local, lon_devices, capacity)
    state_flat = state_field.astype(jnp.bfloat16).reshape(features, row_count * col_count)
    col_buffer = (
        jnp.zeros((slot_total,), jnp.int32).at[slots].set(col_local).reshape(lon_devices, capacity)
    )
    jac_buffer = jnp.zeros((slot_total, features, channels), jnp.bfloat16).at[slots].set(jac_rows)
    jac_buffer = jac_buffer.reshape(lon_devices, capacity, features, channels)
    obs_buffer = (
        jnp.zeros((slot_total, channels), jnp.bfloat16)
        .at[slots]
        .set(obs_rows)
        .reshape(lon_devices, capacity, channels)
    )
    weight_buffer = (
        jnp.zeros((slot_total, channels), jnp.bfloat16)
        .at[slots]
        .set(weight_rows)
        .reshape(lon_devices, capacity, channels)
    )
    jac_in = lax.all_to_all(jac_buffer, "lon", split_axis=0, concat_axis=0, tiled=True)
    obs_in = lax.all_to_all(obs_buffer, "lon", split_axis=0, concat_axis=0, tiled=True)
    weight_in = lax.all_to_all(weight_buffer, "lon", split_axis=0, concat_axis=0, tiled=True)
    col_in = lax.all_to_all(col_buffer, "lon", split_axis=0, concat_axis=0, tiled=True)
    state_cols = jnp.moveaxis(jnp.take(state_flat, col_in, axis=1), 0, -1)
    owner_terms = departures(jac_in, state_cols, obs_in, weight_in)
    impact = jnp.zeros((features, row_count * col_count), jnp.float32)
    impact = impact.at[:, col_in.reshape(-1)].add(owner_terms.reshape(-1, features).T)
    impact_low = impact.reshape(var_count, level_count, row_count * col_count).astype(jnp.bfloat16)
    mixed = jnp.einsum("vlm,vlp->vmp", vertical, impact_low, preferred_element_type=jnp.float32)
    mixed = mixed.reshape(var_count, level_count, row_count, col_count)
    reach = lon_taps.shape[-1] // 2
    lon_wide = padded(mixed, (("lon", 3),), reach, True)
    filtered = lon_filter(lon_wide, lon_taps, col_count)
    lat_tall = padded(filtered, (("lat", 2),), reach, False)
    return lat_filter(lat_tall, lat_taps, row_count)


def solution(mesh):
    placed = (
        P(None, None, "lat", "lon"),
        P("lat", "lon", None, None, None),
        P("lat", "lon", None),
        P("lat", "lon", None),
        P("lat", "lon"),
        P("lat", "lon", None),
        P("lat", "lon"),
        P(),
        P(),
        P(),
    )
    return jax.shard_map(
        body, mesh=mesh, in_specs=placed, out_specs=P(None, None, "lat", "lon"), check_vma=False
    )
```

profile of v0, /device:TPU:1, one launch (start us, length us, event | category | flops | bytes accessed | tf_op | source)
XLA Modules:
  0.0 392.7 jit_solution(13540438381465329415)
XLA Ops:
  0.0 0.8 fusion.54
  0.8 0.1 reduce_window_sum.11
  0.9 0.8 select_reduce_fusion
  1.7 0.7 fusion.65
  2.4 0.9 scatter_custom_fusion
  3.3 0.7 all_to_all.19
  4.0 6.4 %all-to-all-start = ((s32[8,1,16]{2,1,0:T(1,128)}), s32[8,1,16]{2,1,0:T(1,128)S(1)}, u32[]{:S(2)}, u32[]{:S(2)}) async-start(s32[8,1,16]{2,1,0:T(1,128)} %bitcast.7), calls=%async_computation | async-start | bytes 8192 | tf_op jit(solution)/shard_map/all_to_all | solution.py:110
  10.3 1.5 scatter_custom_fusion.3
  11.8 3.8 all-to-all-done
  15.6 3.3 all-to-all-start.3
  19.0 3.5 copy.35
  22.4 5.1 %copy.36 = bf16[64,274,128]{2,1,0:T(8,128)(2,1)} copy(bf16[64,274,128]{2,0,1:T(8,128)(2,1)S(1)} %bitcast.84) | data formatting | bytes 8978432 | tf_op jit(solution)/shard_map/reshape | solution.py:78
  27.5 4.7 %broadcast_in_dim.28 = bf16[128,274,128]{2,1,0:T(8,128)(2,1)} broadcast(bf16[]{:T(256)} %constant.15.clone.1), dimensions={} | broadcast | bytes 8978434 | tf_op jit(solution)/shard_map/broadcast_in_dim | solution.py:93
  32.3 12.4 %scatter_fusion = bf16[128,274,128]{2,1,0:T(8,128)(2,1)} fusion(bf16[128,274,128]{2,1,0:T(8,128)(2,1)} %broadcast_in_dim.28, s32[64]{0:T(128)S(1)} %fusion.65, bf16[64,274,128]{2,1,0:T(8,128)(2,1)} %copy.36), kind=kCustom, calls=%fused_computation.2 | custom fusion | bytes 13467904 | tf_op jit(solution)/shard_map/scatter | solution.py:93
  44.7 8.2 %copy.37 = bf16[8,16,274,128]{3,1,2,0:T(8,128)(2,1)} copy(bf16[8,16,274,128]{3,2,1,0:T(8,128)(2,1)} %bitcast.83) | data formatting | bytes 17956864 | tf_op jit(solution)/shard_map/reshape | solution.py:94
  52.9 5.5 %all-to-all-start.1 = ((bf16[8,16,274,128]{3,1,2,0:T(8,128)(2,1)}), bf16[8,16,274,128]{3,1,2,0:T(8,128)(2,1)}, u32[]{:S(2)}, u32[]{:S(2)}) async-start(bf16[8,16,274,128]{3,1,2,0:T(8,128)(2,1)} %copy.37), calls=%async_computation.1 | async-start | bytes 17956864 | tf_op jit(solution)/shard_map/all_to_all | solution.py:107
  58.4 2.8 convert_element_type.23
  61.2 0.4 pad.17
  61.6 2.5 copy.50
  64.1 3.3 copy.38
  67.4 1.4 scatter_custom_fusion.2
  68.7 0.5 broadcast.111
  69.3 0.6 reduce.3
  70.0 0.9 gather_fusion
  70.9 0.1 select_bitcast_fusion
  71.0 180.7 %all-to-all-done.1 = bf16[8,16,274,128]{3,1,2,0:T(8,128)(2,1)} async-done(((bf16[8,16,274,128]{3,1,2,0:T(8,128)(2,1)}), bf16[8,16,274,128]{3,1,2,0:T(8,128)(2,1)}, u32[]{:S(2)}, u32[]{:S(2)}) %all-to-all-start.1) | async-done | bytes 8978464 | tf_op jit(solution)/shard_map/all_to_all | solution.py:107
  251.7 6.3 %all-to-all-start.2 = ((bf16[8,16,128]{2,1,0:T(8,128)(2,1)}), bf16[8,16,128]{2,1,0:T(8,128)(2,1)S(1)}, u32[]{:S(2)}, u32[]{:S(2)}) async-start(bf16[8,16,128]{2,1,0:T(8,128)(2,1)} %bitcast.13), calls=%async_computation.2 | async-start | bytes 65536 | tf_op jit(solution)/shard_map/all_to_all | solution.py:109
  258.0 5.5 %fusion.2 = f32[8,16,1,128]{3,2,1,0:T(1,128)S(1)} fusion(bf16[8,16,274,128]{3,1,2,0:T(8,128)(2,1)} %all-to-all-done.1, bf16[8,16,274,1]{2,1,0,3:T(8,128)(2,1)S(1)} %select_bitcast_fusion), kind=kOutput, calls=%fused_computation.26 | convolution fusion | flops 8978432 | bytes 9114112 | tf_op jit(solution)/shard_map/...fc,...f->...c/dot_general | solution.py:34
  263.6 6.2 %fusion = f32[8,16,1,274]{3,2,1,0:T(1,128)S(1)} fusion(bf16[8,16,274,128]{3,1,2,0:T(8,128)(2,1)} %all-to-all-done.1, bf16[8,16,128,1]{2,1,0,3:T(8,128)(2,1)S(1)} %fusion.53), kind=kOutput, calls=%fused_computation.24 | convolution fusion | flops 8978432 | bytes 9151488 | tf_op jit(solution)/shard_map/...fc,...c->...f/dot_general | solution.py:37
  269.8 4.4 %scatter_custom_fusion.4 = f32[274,4096]{0,1:T(8,128)} fusion(s32[128]{0:T(128)S(1)} %fusion.66, f32[128,274]{1,0:T(8,128)S(1)} %bitcast.89, f32[]{:T(128)} %constant.9.clone.1), kind=kCustom, calls=%fused_computation.83 | custom fusion | flops 35072 | bytes 4489220 | tf_op jit(solution)/shard_map/scatter-add | solution.py:114
  274.2 5.1 %copy.39 = bf16[274,4096]{1,0:T(8,128)(2,1)} copy(f32[274,4096]{0,1:T(8,128)} %scatter_custom_fusion.4) | data formatting | bytes 6733824 | tf_op jit(solution)/shard_map/scatter-add | solution.py:114
  279.3 2.1 convert_element_type.27
  281.4 2.9 convolution_bitcast_fusion
  284.3 4.1 %reshape.161 = f32[2,137,32,128]{3,2,1,0:T(8,128)} reshape(f32[2,137,4096]{2,1,0:T(8,128)} %convolution_bitcast_fusion) | data formatting | bytes 8978432 | tf_op jit(solution)/shard_map/reshape | solution.py:117
  288.4 8.4 %fusion.70 = (f32[2,137,32,4]{3,2,1,0:T(8,128)}, f32[2,137,32,4]{3,2,1,0:T(8,128)}) fusion(f32[2,137,32,128]{3,2,1,0:T(8,128)} %reshape.161), kind=kLoop, calls=%fused_computation.134 | loop fusion | bytes 561152 | tf_op jit(solution)/shard_map/slice | solution.py:12
  296.9 5.1 %copy.43 = f32[2,137,32,4]{1,2,3,0:T(8,128)S(1)} copy(f32[2,137,32,4]{3,2,1,0:T(8,128)} %get-tuple-element.8) | data formatting | bytes 280576 | tf_op jit(solution)/shard_map/slice | solution.py:11
  302.0 4.4 %collective-permute-start.1 = (f32[2,137,32,4]{1,2,3,0:T(8,128)S(1)}, f32[2,137,32,4]{1,2,3,0:T(8,128)S(1)}, u32[]{:S(2)}, u32[]{:S(2)}) collective-permute-start(f32[2,137,32,4]{1,2,3,0:T(8,128)S(1)} %copy.43), channel_id=1, source_target_pairs={{4,0},{8,4},{12,8},{16,12},{20,16},{24,20},{28,24},{0,28},{5,1},{9... | collective-permute-start | bytes 420872 | tf_op jit(solution)/shard_map/ppermute | solution.py:17
  306.4 5.1 %copy.41 = f32[2,137,32,4]{1,2,3,0:T(8,128)S(1)} copy(f32[2,137,32,4]{3,2,1,0:T(8,128)} %get-tuple-element.7) | data formatting | bytes 280576 | tf_op jit(solution)/shard_map/slice | solution.py:12
  311.6 6.1 %copy.44 = f32[2,137,32,4]{3,2,1,0:T(8,128)} copy(f32[2,137,32,4]{1,2,3,0:T(8,128)S(1)} %collective-permute-done.1) | data formatting | bytes 280576 | tf_op jit(solution)/shard_map/ppermute | solution.py:17
  317.7 3.0 collective-permute-done
  320.7 6.2 %copy.42 = f32[2,137,32,4]{3,2,1,0:T(8,128)} copy(f32[2,137,32,4]{1,2,3,0:T(8,128)S(1)} %collective-permute-done) | data formatting | bytes 280576 | tf_op jit(solution)/shard_map/ppermute | solution.py:15
  326.8 44.0 %fusion.27 = f32[2,137,32,128]{3,2,1,0:T(8,128)S(1)} fusion(f32[2,137,32,128]{3,2,1,0:T(8,128)} %reshape.161, f32[2,137,32,4]{3,2,1,0:T(8,128)} %copy.44, f32[2,137,32,4]{3,2,1,0:T(8,128)} %copy.42, f32[2,137]{1,0:T(2,128)S(1)} %get-tuple-element.25, f32[2,137]{1,0:T(2,128)S(1)} %get-tuple-element.26, f32[2,137]{1,0:T(2,128)S(1)} %get-tuple-element.19, ...), kind=kLoop, calls=%fused_computation.58 | loop fusion | flops 28057600 | bytes 9268872 | tf_op jit(solution)/shard_map/add | solution.py:44
  370.9 0.2 fusion.69
  371.1 4.2 %collective-permute-start.3 = (f32[2,137,4,128]{3,2,1,0:T(4,128)S(1)}, f32[2,137,4,128]{3,2,1,0:T(4,128)S(1)}, u32[]{:S(2)}, u32[]{:S(2)}) collective-permute-start(f32[2,137,4,128]{3,2,1,0:T(4,128)S(1)} %get-tuple-element.6), channel_id=1, source_target_pairs={{1,0},{2,1},{3,2},{5,4},{6,5},{7,6},{9,8},{10,9},{11,10},{13,12},{... | collective-permute-start | bytes 1683464 | tf_op jit(solution)/shard_map/ppermute | solution.py:17
  375.2 3.0 collective-permute-start.2
  378.2 5.3 %collective-permute-done.3 = f32[2,137,4,128]{3,2,1,0:T(4,128)S(1)} collective-permute-done((f32[2,137,4,128]{3,2,1,0:T(4,128)S(1)}, f32[2,137,4,128]{3,2,1,0:T(4,128)S(1)}, u32[]{:S(2)}, u32[]{:S(2)}) %collective-permute-start.3) | collective-permute-done | bytes 561184 | tf_op jit(solution)/shard_map/ppermute | solution.py:17
  383.5 1.2 collective-permute-done.2
  384.7 7.9 %fusion.7 = f32[2,137,32,128]{3,2,1,0:T(8,128)} fusion(f32[2,137,32,128]{3,2,1,0:T(8,128)S(1)} %fusion.27, f32[2,137,4,128]{3,2,1,0:T(4,128)S(1)} %collective-permute-done.3, f32[2,137,4,128]{3,2,1,0:T(4,128)S(1)} %collective-permute-done.2, f32[2,137]{1,0:T(2,128)S(1)} %get-tuple-element.16, f32[2,137]{1,0:T(2,128)S(1)} %get-tuple-element.17, ...), kind=kLoop, calls=%fused_computation.38 | loop fusion | flops 28057600 | bytes 10110600 | tf_op jit(solution)/shard_map/add | solution.py:53
  (24 shorter events, 0.4 us)
Async XLA Ops:
  0.0 281.4 %copy-start = (bf16[2,137,137]{2,0,1:T(2,128)(2,1)S(1)}, bf16[2,137,137]{2,0,1:T(2,128)(2,1)}, u32[]{:S(2)}) copy-start(bf16[2,137,137]{2,0,1:T(2,128)(2,1)} %param.17) | copy-start | bytes 225232
  4.0 11.7 %all-to-all-start = ((s32[8,1,16]{2,1,0:T(1,128)}), s32[8,1,16]{2,1,0:T(1,128)S(1)}, u32[]{:S(2)}, u32[]{:S(2)}) async-start(s32[8,1,16]{2,1,0:T(1,128)} %bitcast.7), calls=%async_computation | async-start | bytes 8192 | tf_op jit(solution)/shard_map/all_to_all | solution.py:110
  15.6 37.3 %all-to-all-start.3 = ((bf16[8,16,128]{2,1,0:T(8,128)(2,1)}), bf16[8,16,128]{2,1,0:T(8,128)(2,1)S(1)}, u32[]{:S(2)}, u32[]{:S(2)}) async-start(bf16[8,16,128]{2,1,0:T(8,128)(2,1)} %bitcast.21), calls=%async_computation.3 | async-start | bytes 65536 | tf_op jit(solution)/shard_map/all_to_all | solution.py:108
  52.9 198.8 %all-to-all-start.1 = ((bf16[8,16,274,128]{3,1,2,0:T(8,128)(2,1)}), bf16[8,16,274,128]{3,1,2,0:T(8,128)(2,1)}, u32[]{:S(2)}, u32[]{:S(2)}) async-start(bf16[8,16,274,128]{3,1,2,0:T(8,128)(2,1)} %copy.37), calls=%async_computation.1 | async-start | bytes 17956864 | tf_op jit(solution)/shard_map/all_to_all | solution.py:107
  61.6 5.8 %copy-start.3 = (bf16[1,64,128]{2,1,0:T(8,128)(2,1)S(1)}, bf16[1,64,128]{2,1,0:T(8,128)(2,1)}, u32[]{:S(2)}) copy-start(bf16[1,64,128]{2,1,0:T(8,128)(2,1)} %param.13) | copy-start | bytes 49156
  61.6 5.8 %copy-start.4 = (s32[1,64]{1,0:T(1,128)S(1)}, s32[1,64]{1,0:T(1,128)}, u32[]{:S(2)}) copy-start(s32[1,64]{1,0:T(1,128)} %param.14) | copy-start | bytes 772
  251.7 11.8 %all-to-all-start.2 = ((bf16[8,16,128]{2,1,0:T(8,128)(2,1)}), bf16[8,16,128]{2,1,0:T(8,128)(2,1)S(1)}, u32[]{:S(2)}, u32[]{:S(2)}) async-start(bf16[8,16,128]{2,1,0:T(8,128)(2,1)} %bitcast.13), calls=%async_computation.2 | async-start | bytes 65536 | tf_op jit(solution)/shard_map/all_to_all | solution.py:109
  296.9 14.7 %copy-start.1 = (f32[2,137,9]{1,0,2:T(2,128)S(1)}, f32[2,137,9]{1,0,2:T(2,128)}, u32[]{:S(2)}) copy-start(f32[2,137,9]{1,0,2:T(2,128)} %param.18) | copy-start | bytes 29596
  302.0 9.6 %collective-permute-start.1 = (f32[2,137,32,4]{1,2,3,0:T(8,128)S(1)}, f32[2,137,32,4]{1,2,3,0:T(8,128)S(1)}, u32[]{:S(2)}, u32[]{:S(2)}) collective-permute-start(f32[2,137,32,4]{1,2,3,0:T(8,128)S(1)} %copy.43), channel_id=1, source_target_pairs={{4,0},{8,4},{12,8},{16,12},{20,16},{24,20},{28,24},{0,28},{5,1},{9... | collective-permute-start | bytes 420872 | tf_op jit(solution)/shard_map/ppermute | solution.py:17
  311.5 9.2 %collective-permute-start = (f32[2,137,32,4]{1,2,3,0:T(8,128)S(1)}, f32[2,137,32,4]{1,2,3,0:T(8,128)S(1)}, u32[]{:S(2)}, u32[]{:S(2)}) collective-permute-start(f32[2,137,32,4]{1,2,3,0:T(8,128)S(1)} %copy.41), channel_id=1, source_target_pairs={{0,4},{4,8},{8,12},{12,16},{16,20},{20,24},{24,28},{28,0},{1,5},{5... | collective-permute-start | bytes 420872 | tf_op jit(solution)/shard_map/ppermute | solution.py:15
  326.8 51.4 %copy-start.2 = (f32[2,137,9]{1,0,2:T(2,128)S(1)}, f32[2,137,9]{1,0,2:T(2,128)}, u32[]{:S(2)}) copy-start(f32[2,137,9]{1,0,2:T(2,128)} %param.19) | copy-start | bytes 29596
  371.1 12.5 %collective-permute-start.3 = (f32[2,137,4,128]{3,2,1,0:T(4,128)S(1)}, f32[2,137,4,128]{3,2,1,0:T(4,128)S(1)}, u32[]{:S(2)}, u32[]{:S(2)}) collective-permute-start(f32[2,137,4,128]{3,2,1,0:T(4,128)S(1)} %get-tuple-element.6), channel_id=1, source_target_pairs={{1,0},{2,1},{3,2},{5,4},{6,5},{7,6},{9,8},{10,9},{11,10},{13,12},{... | collective-permute-start | bytes 1683464 | tf_op jit(solution)/shard_map/ppermute | solution.py:17
  375.2 9.5 %collective-permute-start.2 = (f32[2,137,4,128]{3,2,1,0:T(4,128)S(1)}, f32[2,137,4,128]{3,2,1,0:T(4,128)S(1)}, u32[]{:S(2)}, u32[]{:S(2)}) collective-permute-start(f32[2,137,4,128]{3,2,1,0:T(4,128)S(1)} %get-tuple-element.5), channel_id=1, source_target_pairs={{0,1},{1,2},{2,3},{4,5},{5,6},{6,7},{8,9},{9,10},{10,11},{12,13},{... | collective-permute-start | bytes 1683464 | tf_op jit(solution)/shard_map/ppermute | solution.py:15
where the time goes:
time: 394 us; the launch traced here: 393 us
  waiting for transfers between devices  194 us (49%)
  local copies, waits for them, and re-layouts  87 us (22%)
  other arithmetic  63.6 us (16%)
  starting transfers between devices  33.1 us (8%)
  matrix products  14.7 us (4%)
    all_to_all x1, waiting for transfers between devices, body(): lax.all_to_all(jac_buffer, 'lon', split_axis=0, concat_axis=0, tiled=True)  181 us
    add x1, other arithmetic, lon_filter(): result + taps[:, :, offset][:, :, None, None] * extended[..., offset:offs...  44 us
    slice x3, local copies, waits for them, and re-layouts, padded(): lax.slice_in_dim(cells, cells.shape[dim] - width, cells.shape[dim], axis=...  13.7 us
    scatter x1, local copies, waits for them, and re-layouts, body(): jnp.zeros((slot_total, features, channels), jnp.bfloat16).at[slots]  12.4 us
    ppermute x2, starting transfers between devices, padded(): lax.ppermute(head, axis, [((i + 1) % count, i) for i in range(ends)])  8.57 us
    reshape x1, local copies, waits for them, and re-layouts, body(): jac_buffer = jac_buffer.reshape(lon_devices, capacity, features, channels)  8.25 us
    add x1, other arithmetic, lat_filter(): result + taps[:, :, offset][:, :, None, None] * extended[:, :, offset:off...  7.95 us
  transfers between devices with their start and end apart: 8, of which 5 were waited for; matrix products, arithmetic and copies ran while one was open for 16% of the time, Pallas kernels for 0%

commit v1 on v0

v1 whole, which is shorter than its diff:
```python
import functools

import jax
import jax.numpy as jnp
from jax import lax
from jax.experimental import pallas as pl
from jax.experimental.pallas import tpu as pltpu
from jax.sharding import PartitionSpec as P

LANES = 128
F32 = jnp.float32
BF16 = jnp.bfloat16
VMEM_LIMIT = 56 * 1024 * 1024


def lane_iota(shape):
    return lax.broadcasted_iota(jnp.int32, shape, 1)


def row_iota(shape):
    return lax.broadcasted_iota(jnp.int32, shape, 0)


def earlier_rows(size):
    return (lane_iota((size, size)) < row_iota((size, size))).astype(F32).astype(BF16)


def split_codes(codes_ref, records, points):
    flipped = jnp.transpose(codes_ref[...].astype(F32))[:records].astype(jnp.int32)
    tile = lax.div(flipped, points)
    return tile, flipped - tile * points


def gather_kernel(records, capacity, rows, features, codes_ref, state_ref, out_ref, held, pick, row_mask):
    step = pl.program_id(0)
    count = codes_ref.shape[0]
    slots = out_ref.shape[0]
    planes = state_ref.shape[0] // rows

    @pl.when(step == 0)
    def _():
        me = lax.axis_index("lon")
        tile, column = split_codes(codes_ref, records, rows * LANES)
        mine = (tile == me).astype(F32)
        rank = jnp.dot(earlier_rows(records), mine.astype(BF16), preferred_element_type=F32)
        slot = lane_iota(mine.shape) * capacity + rank.astype(jnp.int32)
        slot = jnp.where(tile == me, slot, -1)
        row_of = jnp.zeros((1, slots), F32)
        lon_of = jnp.zeros((1, slots), F32)
        for d in range(count):
            hit = slot[:, d : d + 1] == lane_iota((records, slots))
            row = lax.div(column[:, d : d + 1], LANES)
            lon = column[:, d : d + 1] - row * LANES
            row_of += jnp.sum(jnp.where(hit, (row + 1).astype(F32), 0.0), axis=0, keepdims=True)
            lon_of += jnp.sum(jnp.where(hit, lon.astype(F32), 0.0), axis=0, keepdims=True)
        pick[...] = (row_iota((LANES, slots)) == lon_of.astype(jnp.int32)).astype(F32).astype(BF16)
        row_mask[...] = (row_iota((rows, slots)) == row_of.astype(jnp.int32) - 1).astype(F32)

    found = jnp.dot(state_ref[...].astype(BF16), pick[...], preferred_element_type=F32)
    found = found.reshape(planes, rows, slots) * row_mask[...][None]
    held[pl.ds(pl.multiple_of(step * planes, planes), planes), :] = jnp.sum(found, axis=1)

    @pl.when(step == pl.num_programs(0) - 1)
    def _():
        for t in range(out_ref.shape[1] // LANES):
            out_ref[:, t * LANES : (t + 1) * LANES] = jnp.transpose(
                held[t * LANES : (t + 1) * LANES, :]
            ).astype(BF16)


def gather_state(codes, state, records, capacity):
    variables, levels, rows, cols = state.shape
    features = variables * levels
    wide = pl.cdiv(features, LANES) * LANES
    slots = codes.shape[0] * capacity
    planes = 32
    steps = pl.cdiv(features, planes)
    return pl.pallas_call(
        functools.partial(gather_kernel, records, capacity, rows, features),
        grid=(steps,),
        in_specs=[
            pl.BlockSpec(codes.shape, lambda s: (0, 0)),
            pl.BlockSpec((planes * rows, cols), lambda s: (s, 0)),
        ],
        out_specs=pl.BlockSpec((slots, wide), lambda s: (0, 0)),
        out_shape=jax.ShapeDtypeStruct((slots, wide), BF16),
        scratch_shapes=[
            pltpu.VMEM((wide, slots), F32),
            pltpu.VMEM((cols, slots), BF16),
            pltpu.VMEM((rows, slots), F32),
        ],
        compiler_params=pltpu.CompilerParams(vmem_limit_bytes=VMEM_LIMIT),
        cost_estimate=pl.CostEstimate(
            flops=2 * features * rows * cols * slots, bytes_accessed=features * rows * cols * 4, transcendentals=0
        ),
        name="gather_state",
    )(codes, state.reshape(features * rows, cols))


def departure_kernel(capacity, dest_ref, valid_ref, states_ref, obs_ref, inv_ref, jac_ref, out_ref, state, scaled_rows, total):
    step = pl.program_id(0)
    group, variables, levels, channels = jac_ref.shape
    records = dest_ref.shape[0]
    slots = states_ref.shape[0]

    @pl.when(step == 0)
    def _():
        dest = dest_ref[...]
        named = (dest == lane_iota((records, LANES))).astype(F32)
        before = jnp.dot(earlier_rows(records), named.astype(BF16), preferred_element_type=F32)
        rank = jnp.sum(before * named, axis=1, keepdims=True).astype(jnp.int32)
        chosen = (dest * capacity + rank == lane_iota((records, slots))).astype(F32).astype(BF16)
        columns = jnp.dot(chosen, states_ref[...], preferred_element_type=F32)
        for v in range(variables):
            state[v] = columns[:, v * levels : (v + 1) * levels].astype(BF16)
        scaled_rows[...] = jnp.zeros_like(scaled_rows)
        total[...] = jnp.zeros_like(total)

    first = pl.multiple_of(step * group, group)
    mine = [state[v, pl.ds(first, group), :] for v in range(variables)]
    model = jnp.zeros((group, channels), F32)
    for r in range(group):
        one = jnp.dot(mine[0], jac_ref[r, 0], preferred_element_type=F32)
        for v in range(1, variables):
            one += jnp.dot(mine[v], jac_ref[r, v], preferred_element_type=F32)
        model = jnp.where(row_iota(model.shape) == r, one, model)
    alive = lane_iota(model.shape) < valid_ref[pl.ds(first, group), :]
    weight = jnp.where(alive, inv_ref[pl.ds(first, group), :].astype(F32), 0.0)
    scaled = (weight * (model - obs_ref[pl.ds(first, group), :].astype(F32))).astype(BF16)
    for v in range(variables):
        scaled_rows[pl.ds(pl.multiple_of(v * records + first, group), group), :] = scaled
    against = scaled_rows[...]
    sums = total[...]
    lane = lane_iota(sums.shape)
    for r in range(group):
        for v in range(variables):
            one = lax.dot_general(
                jac_ref[r, v], against, (((1,), (1,)), ((), ())), preferred_element_type=F32
            )
            sums = jnp.where(lane == v * records + first + r, one, sums)
    total[...] = sums

    @pl.when(step == pl.num_programs(0) - 1)
    def _():
        low = sums.astype(BF16)
        for t in range(out_ref.shape[0]):
            out_ref[t] = low


def departures(dest, valid, states, obs, inv, jac, capacity, devices):
    records, variables, levels, channels = jac.shape
    group = 16

    def whole(shape):
        return pl.BlockSpec(shape, lambda s: (0,) * len(shape))

    return pl.pallas_call(
        functools.partial(departure_kernel, capacity),
        grid=(records // group,),
        in_specs=[
            whole(dest.shape),
            whole(valid.shape),
            whole(states.shape),
            whole(obs.shape),
            whole(inv.shape),
            pl.BlockSpec((group, variables, levels, channels), lambda s: (s, 0, 0, 0)),
        ],
        out_specs=whole((devices, levels, variables * records)),
        out_shape=jax.ShapeDtypeStruct((devices, levels, variables * records), BF16),
        scratch_shapes=[
            pltpu.VMEM((variables, records, levels), BF16),
            pltpu.VMEM((variables * records, channels), BF16),
            pltpu.VMEM((levels, variables * records), F32),
        ],
        compiler_params=pltpu.CompilerParams(vmem_limit_bytes=VMEM_LIMIT),
        cost_estimate=pl.CostEstimate(
            flops=4 * jac.size, bytes_accessed=jac.size * 2, transcendentals=0
        ),
        name="departures",
    )(dest, valid, states, obs, inv, jac)


def place_records(records, rows, reach, codes_ref, main, halo, wrap):
    me = lax.axis_index("lon")
    count = codes_ref.shape[0]
    right, left = lax.rem(me + 1, count), lax.rem(me + count - 1, count)
    tile, column = split_codes(codes_ref, records, rows * LANES)
    row = lax.div(column, LANES)
    lon = column - row * LANES
    far = LANES - reach
    edge = row * (2 * reach) + jnp.where(lon < reach, lon, lon - far + reach)
    near_right, near_left = lon < reach, lon >= far
    on_main = jnp.where(tile == me, column, -1)
    on_halo = jnp.where(((tile == right) & near_right) | ((tile == left) & near_left), edge, -1)
    on_wrap = jnp.where((tile == me) & (near_right | near_left), edge, -1)
    for where_to, what in ((main, on_main), (halo, on_halo), (wrap, on_wrap)):
        if where_to is None:
            continue
        for d in range(count):
            where_to[d * records : (d + 1) * records, :] = jnp.broadcast_to(
                what[:, d : d + 1], (records, LANES)
            )


def order_products(records, products_ref, terms):
    count, levels, width = products_ref.shape
    tall = terms.shape[0] * records // width
    terms[...] = jnp.zeros_like(terms)
    lane = lane_iota((levels, width))
    for pair in range(count // 2):
        one = products_ref[2 * pair].astype(F32)
        two = products_ref[2 * pair + 1].astype(F32)
        first = jnp.where(lane < records, one, pltpu.roll(two, records, 1))
        second = jnp.where(lane < records, pltpu.roll(one, records, 1), two)
        terms[0:levels, pair * width : (pair + 1) * width] = first.astype(BF16)
        terms[tall : tall + levels, pair * width : (pair + 1) * width] = second.astype(BF16)


def mix_columns(levels, place, base, width, terms, vertical_ref, mixed, at):
    tall = vertical_ref.shape[1]
    spots = [place[...] == lane_iota(place.shape) + (base + n * LANES) for n in range(width // LANES)]
    onehot = jnp.concatenate([s.astype(F32).astype(BF16) for s in spots], axis=1)
    impact = jnp.dot(terms[...], onehot, preferred_element_type=F32).astype(BF16)
    for v in range(vertical_ref.shape[0]):
        mixed[v * levels : v * levels + tall, at : at + width] = jnp.dot(
            vertical_ref[v], impact[v * tall : (v + 1) * tall], preferred_element_type=F32
        )


def edge_fix(reach, outer, inner, taps):
    gap = outer - inner
    lane = lane_iota(gap.shape) % (2 * reach)
    width = gap.shape[1]
    fix = jnp.zeros_like(gap)
    for s in range(reach):
        right = pltpu.roll(gap, s, 1) if s else gap
        left = pltpu.roll(gap, width - s, 1) if s else gap
        on_right = (lane >= s) & (lane < reach)
        on_left = (lane >= reach) & (lane < 2 * reach - s)
        fix += jnp.where(on_right, taps[2 * reach - s] * right, 0.0)
        fix += jnp.where(on_left, taps[s] * left, 0.0)
    return fix


def lon_row(reach, row, x, fix, taps, ends):
    before, after = pltpu.roll(x, 1, 1), pltpu.roll(x, LANES - 1, 1)
    parts = [taps[3 * a] * before + taps[3 * a + 1] * x + taps[3 * a + 2] * after for a in range(3)]
    total = pltpu.roll(parts[0], 3, 1) + parts[1] + pltpu.roll(parts[2], LANES - 3, 1)
    span = 2 * reach
    block, spot = divmod(row * span, LANES)
    shift = (LANES - reach - spot) % LANES
    piece = fix[:, block * LANES : (block + 1) * LANES]
    piece = pltpu.roll(piece, shift, 1) if shift else piece
    return total + jnp.where(ends, piece, 0.0)


def spread_taps(block, height):
    return [jnp.broadcast_to(block[:, k : k + 1], (height, LANES)) for k in range(block.shape[1])]


def edges_kernel(records, rows, reach, levels, codes_ref, products_ref, vertical_ref, lon_ref, out_ref, main, halo, wrap, terms, mixed):
    place_records(records, rows, reach, codes_ref, main, halo, wrap)
    order_products(records, products_ref, terms)
    span = 2 * reach
    half = reach * LANES
    mix_columns(levels, main, 0, half, terms, vertical_ref, mixed, 0)
    mix_columns(levels, main, (rows - reach) * LANES, half, terms, vertical_ref, mixed, half)
    ends = rows * span
    mix_columns(levels, halo, 0, ends, terms, vertical_ref, mixed, 2 * half)
    mix_columns(levels, wrap, 0, ends, terms, vertical_ref, mixed, 2 * half + ends)
    height = 16
    lane = lane_iota((height, LANES))
    at_ends = (lane < reach) | (lane >= LANES - reach)

    @pl.loop(0, out_ref.shape[2] // height)
    def _(g):
        here = pl.ds(pl.multiple_of(g * height, height), height)
        taps = spread_taps(lon_ref[here, :], height)
        wide_taps = [jnp.concatenate([t] * (ends // LANES), axis=1) for t in taps]
        fix = edge_fix(
            reach, mixed[here, 2 * half : 2 * half + ends], mixed[here, 2 * half + ends :], wide_taps
        )
        for side in range(2):
            for n in range(reach):
                row = n if side == 0 else rows - reach + n
                at = (side * reach + n) * LANES
                out_ref[side, n, here, :] = lon_row(
                    reach, row, mixed[here, at : at + LANES], fix, taps, at_ends
                ).astype(BF16)


def mix_kernel(records, rows, reach, levels, codes_ref, products_ref, vertical_ref, out_ref, main, halo, wrap, terms):
    place_records(records, rows, reach, codes_ref, main, halo, wrap)
    order_products(records, products_ref, terms)
    points = rows * LANES
    ends = rows * 2 * reach
    width = 2 * LANES
    for at in range(0, points, width):
        mix_columns(levels, main, at, width, terms, vertical_ref, out_ref, at)
    mix_columns(levels, halo, 0, ends, terms, vertical_ref, out_ref, points)
    mix_columns(levels, wrap, 0, ends, terms, vertical_ref, out_ref, points + ends)


def filter_kernel(rows, reach, features, mixed_ref, lon_ref, lat_ref, above_ref, below_ref, out_ref, outer):
    height = 8
    block = mixed_ref.shape[0]
    points = rows * LANES
    ends = rows * 2 * reach
    outer[0] = above_ref[...].astype(F32)
    outer[1] = below_ref[...].astype(F32)
    lane = lane_iota((height, LANES))
    at_ends = (lane < reach) | (lane >= LANES - reach)
    left = features - pl.program_id(0) * block
    groups = jnp.minimum(block // height, lax.div(left + height - 1, height))

    def one_group(g, carry):
        first = pl.multiple_of(g * height, height)
        here = pl.ds(first, height)
        lon = spread_taps(lon_ref[here, :], height)
        lat = spread_taps(lat_ref[here, :], height)
        wide = [jnp.concatenate([t] * (ends // LANES), axis=1) for t in lon]
        fix = edge_fix(reach, mixed_ref[here, points : points + ends], mixed_ref[here, points + ends :], wide)
        pending = {}
        for row in range(-reach, rows + reach):
            if row < 0:
                along = outer[0, row + reach, here, :]
            elif row >= rows:
                along = outer[1, row - rows, here, :]
            else:
                along = lon_row(reach, row, mixed_ref[here, row * LANES : (row + 1) * LANES], fix, lon, at_ends)
            for k in range(2 * reach + 1):
                target = row - k + reach
                if 0 <= target < rows:
                    term = lat[k] * along
                    pending[target] = pending[target] + term if target in pending else term
            done = row - reach
            if done >= 0:
                out_ref[pl.ds(first * rows + done, height, stride=rows), :] = pending.pop(done)
        return carry

    lax.fori_loop(0, groups, one_group, 0)


def solution(mesh):
    lon_devices, lat_devices = mesh.shape["lon"], mesh.shape["lat"]

    def body(state_field, jacobian, observed, inverse_var, valid_count, destination, column, vertical, lon_taps, lat_taps):
        variables, levels, rows, cols = state_field.shape
        features = variables * levels
        records, channels = jacobian.shape[1], jacobian.shape[-1]
        capacity = max(2, 2 * records // lon_devices)
        reach = lon_taps.shape[-1] // 2
        points = rows * cols
        span = records * lon_devices
        tall = pl.cdiv(levels, 16) * 16
        height = pl.cdiv((variables - 1) * levels + tall, 48) * 48
        ends = rows * 2 * reach

        dest = destination.reshape(records, 1)
        codes = destination.reshape(1, records) * points + column.reshape(1, records)
        codes = jnp.broadcast_to(jnp.pad(codes, ((0, 0), (0, LANES - records))), (lon_devices, LANES))
        codes = lax.all_to_all(codes, "lon", split_axis=0, concat_axis=0, tiled=True)

        found = gather_state(codes, state_field, records, capacity)
        found = found.reshape(lon_devices, capacity, found.shape[-1])
        found = lax.all_to_all(found, "lon", split_axis=0, concat_axis=0, tiled=True)
        found = found.reshape(lon_devices * capacity, found.shape[-1])

        products = departures(
            dest,
            valid_count.reshape(records, 1),
            found,
            observed.reshape(records, channels),
            inverse_var.reshape(records, channels),
            jacobian.reshape(records, variables, levels, channels),
            capacity,
            lon_devices,
        )
        products = lax.all_to_all(products, "lon", split_axis=0, concat_axis=0, tiled=True)

        mixing = jnp.pad(jnp.swapaxes(vertical, 1, 2), ((0, 0), (0, tall - levels), (0, tall - levels)))
        lon_flat = jnp.pad(lon_taps.reshape(features, -1), ((0, height - features), (0, 0)))
        lat_flat = jnp.pad(lat_taps.reshape(features, -1), ((0, height - features), (0, 0)))

        params = pltpu.CompilerParams(vmem_limit_bytes=VMEM_LIMIT)
        placing = [
            pltpu.VMEM((span, LANES), jnp.int32),
            pltpu.VMEM((span, LANES), jnp.int32),
            pltpu.VMEM((span, LANES), jnp.int32),
            pltpu.VMEM((variables * tall, span), BF16),
        ]
        edges = pl.pallas_call(
            functools.partial(edges_kernel, records, rows, reach, levels),
            out_shape=jax.ShapeDtypeStruct((2, reach, height, cols), BF16),
            scratch_shapes=placing + [pltpu.VMEM((height, 2 * reach * cols + 2 * ends), F32)],
            compiler_params=params,
            name="edge_rows",
        )(codes, products, mixing, lon_flat)
        below = lax.ppermute(edges[0], "lat", [(i + 1, i) for i in range(lat_devices - 1)])
        above = lax.ppermute(edges[1], "lat", [(i, i + 1) for i in range(lat_devices - 1)])
        mixed = pl.pallas_call(
            functools.partial(mix_kernel, records, rows, reach, levels),
            out_shape=jax.ShapeDtypeStruct((height, points + 2 * ends), F32),
            scratch_shapes=placing,
            compiler_params=params,
            cost_estimate=pl.CostEstimate(
                flops=2 * features * span * points, bytes_accessed=height * points * 4, transcendentals=0
            ),
            name="mix_levels",
        )(codes, products, mixing)

        block = 48
        result = pl.pallas_call(
            functools.partial(filter_kernel, rows, reach, features),
            grid=(pl.cdiv(features, block),),
            in_specs=[
                pl.BlockSpec((block, mixed.shape[1]), lambda s: (s, 0)),
                pl.BlockSpec((block, lon_flat.shape[1]), lambda s: (s, 0)),
                pl.BlockSpec((block, lat_flat.shape[1]), lambda s: (s, 0)),
                pl.BlockSpec((reach, block, cols), lambda s: (0, s, 0)),
                pl.BlockSpec((reach, block, cols), lambda s: (0, s, 0)),
            ],
            out_specs=pl.BlockSpec((block * rows, cols), lambda s: (s, 0)),
            out_shape=jax.ShapeDtypeStruct((features * rows, cols), F32),
            scratch_shapes=[pltpu.VMEM((2, reach, block, cols), F32)],
            compiler_params=params,
            name="filters",
        )(mixed, lon_flat, lat_flat, above, below)
        return result.reshape(variables, levels, rows, cols)

    placed = (
        P(None, None, "lat", "lon"),
        P("lat", "lon", None, None, None),
        P("lat", "lon", None),
        P("lat", "lon", None),
        P("lat", "lon"),
        P("lat", "lon", None),
        P("lat", "lon"),
        P(),
        P(),
        P(),
    )
    return jax.shard_map(
        body, mesh=mesh, in_specs=placed, out_specs=P(None, None, "lat", "lon"), check_vma=False
    )
```

time: 394 us -> 117 us (0.30)
  waiting for transfers between devices: 194 us -> 5.66 us
  local copies, waits for them, and re-layouts: 87 us -> 13 us
  Pallas kernels: 0 us -> 67.7 us
  other arithmetic: 63.6 us -> 0.73 us
  starting transfers between devices: 33.1 us -> 17.6 us
  matrix products: 14.7 us -> 0 us
  blocking collectives: 0 us -> 11.4 us
    all_to_all x4 -> x2, waiting for transfers between devices: 185 us -> 5.65 us  [the longest x1 5.65 us: body(): lax.all_to_all(products, 'lon', split_axis=0, concat_axis=0, tiled=True)]
    pallas_call x0 -> x5, Pallas kernels: none -> 67.7 us  [the longest x1 34.5 us: body(): pl.pallas_call(functools.partial(filter_kernel, rows, reach, features), g...]
    add x2 -> x1, other arithmetic: 52 us -> 0.73 us  [body(): destination.reshape(1, records) * points + column.reshape(1, records)]
    reshape x5 -> x6, local copies, waits for them, and re-layouts: 20.8 us -> 1.78 us  [the longest x1 0.7 us: body(): dest = destination.reshape(records, 1)]
    slice x4 -> x0, local copies, waits for them, and re-layouts: 18.8 us -> none  [the longest x3 13.7 us: padded(): lax.slice_in_dim(cells, cells.shape[dim] - width, cells.shape[dim], axis=...]
    scatter x3 -> x0, local copies, waits for them, and re-layouts: 14.8 us -> none  [the longest x1 12.4 us: body(): jnp.zeros((slot_total, features, channels), jnp.bfloat16).at[slots]]
    dot_general x3 -> x0, matrix products: 14.7 us -> none  [the longest x1 6.24 us: departures(): jnp.einsum('...fc,...c->...f', jac_rows, scaled, preferred_element_type=j...]
    all_to_all x4 -> x2, starting transfers between devices: 21.5 us -> 8.73 us  [the longest x1 5.37 us: body(): lax.all_to_all(products, 'lon', split_axis=0, concat_axis=0, tiled=True)]
  transfers between devices with their start and end apart: 8 -> 4, of which waited for: 5 -> 1; matrix products, arithmetic and copies ran while one was open for 16% -> 8% of each run, Pallas kernels for 0% -> 8%
where the time goes in v1:
time: 117 us; the launch traced here: 116 us
  Pallas kernels  67.7 us (58%)
  starting transfers between devices  17.6 us (15%)
  local copies, waits for them, and re-layouts  13 us (11%)
  blocking collectives  11.4 us (10%)
  waiting for transfers between devices  5.66 us (5%)
    pallas_call x1, Pallas kernels, body(): pl.pallas_call(functools.partial(filter_kernel, rows, reach, features), g...  34.5 us
    all_to_all x1, blocking collectives, body(): lax.all_to_all(codes, 'lon', split_axis=0, concat_axis=0, tiled=True)  11.4 us
    pallas_call x1, Pallas kernels, body(): pl.pallas_call(functools.partial(mix_kernel, records, rows, reach, levels...  9.09 us
    pallas_call x1, Pallas kernels, body(): pl.pallas_call(functools.partial(edges_kernel, records, rows, reach, leve...  9 us
    unnamed x20, local copies, waits for them, and re-layouts  8.05 us
    pallas_call x1, Pallas kernels, gather_state(): pl.pallas_call(functools.partial(gather_kernel, records, capacity, rows,...  7.55 us
    pallas_call x1, Pallas kernels, departures(): pl.pallas_call(functools.partial(departure_kernel, capacity), grid=(recor...  7.52 us
    ppermute x1, starting transfers between devices, body(): lax.ppermute(edges[0], 'lat', [(i + 1, i) for i in range(lat_devices - 1)])  5.77 us
  transfers between devices with their start and end apart: 4, of which 1 were waited for; matrix products, arithmetic and copies ran while one was open for 8% of the time, Pallas kernels for 8%

profile of v1, /device:TPU:1, one launch (start us, length us, event | category | flops | bytes accessed | tf_op | source)
XLA Modules:
  0.0 116.1 jit_solution(4335308878630987035)
XLA Ops:
  0.0 0.0 copy-start.8
  0.0 0.0 copy-start.7
  0.0 0.7 bitcast_add_fusion
  0.7 11.4 %all_to_all.18 = s32[8,1,128]{2,1,0:T(1,128)} all-to-all(s32[8,1,128]{2,1,0:T(1,128)S(1)} %broadcast_in_dim.2), channel_id=1, replica_groups=mesh['lon'=8,'lat'=4] {'lon'}, dimensions={0} | all-to-all | bytes 8192 | tf_op jit(solution)/shard_map/all_to_all | solution.py:362
  12.2 7.5 %gather_state.1 = bf16[128,384]{1,0:T(8,128)(2,1)} custom-call(s32[8,128]{1,0:T(8,128)} %bitcast.30, f32[8768,128]{1,0:T(8,128)} %bitcast.26), custom_call_target="tpu_custom_call" | custom-call | flops 287309824 | bytes 4489216 | tf_op jit(solution)/shard_map/gather_state/pallas_call | solution.py:78
  19.7 3.4 %all-to-all-start.1 = ((bf16[8,16,384]{2,1,0:T(8,128)(2,1)}), bf16[8,16,384]{2,1,0:T(8,128)(2,1)S(1)}, u32[]{:S(2)}, u32[]{:S(2)}) async-start(bf16[8,16,384]{2,1,0:T(8,128)(2,1)} %bitcast.29), calls=%async_computation.1 | async-start | bytes 196608 | tf_op jit(solution)/shard_map/all_to_all | solution.py:366
  23.1 0.0 copy-done.7
  23.1 0.7 copy.25.valid_ref
  23.8 0.0 copy-done.8
  23.8 0.7 copy.24.dest_ref
  24.5 5.1 %copy.30 = bf16[1,64,2,137,128]{4,3,2,1,0:T(8,128)(2,1)} copy(bf16[1,64,2,137,128]{4,2,3,1,0:T(2,128)(2,1)} %param.11) | data formatting | bytes 8978432 | tf_op args[1]
  29.6 0.0 copy-start.5
  29.6 0.0 copy-start.4
  29.6 0.0 all-to-all-done.1
  29.6 0.0 copy-start.1
  29.6 0.6 copy-done.1
  30.2 0.0 copy-start.6
  30.2 7.5 %departures.1 = bf16[8,137,128]{2,1,0:T(8,128)(2,1)} custom-call(s32[64,1]{1,0:T(8,128)} %copy.24.dest_ref, s32[64,1]{1,0:T(8,128)} %copy.25.valid_ref, bf16[128,384]{1,0:T(8,128)(2,1)} %bitcast.28, bf16[64,128]{1,0:T(8,128)(2,1)} %bitcast.33, bf16[64,128]{1,0:T(8,128)(2,1)} %bitcast.34, bf16[64,2,137,128]{3,2,1,0:T(8,128)(2,1)} %bitcast.25), custom_call_target="tpu_custom_call" | custom-call | flops 8978432 | bytes 4489216 | tf_op jit(solution)/shard_map/departures/pallas_call | solution.py:157
  37.7 5.4 %all-to-all-start.2 = ((bf16[8,137,128]{2,1,0:T(8,128)(2,1)}), bf16[8,137,128]{2,1,0:T(8,128)(2,1)S(1)}, u32[]{:S(2)}, u32[]{:S(2)}) async-start(bf16[8,137,128]{2,1,0:T(8,128)(2,1)} %departures.1), calls=%async_computation.2 | async-start | bytes 589824 | tf_op jit(solution)/shard_map/all_to_all | solution.py:379
  43.1 0.0 copy-done.5
  43.1 0.1 reshape.62
  43.2 0.1 copy.27
  43.3 0.0 copy-done.4
  43.3 0.2 copy.26
  43.5 0.7 pad.20.lon_ref
  44.2 0.7 pad.19.vertical_ref
  44.8 5.6 %all-to-all-done.2.products_ref = bf16[8,137,128]{2,1,0:T(8,128)(2,1)S(1)} async-done(((bf16[8,137,128]{2,1,0:T(8,128)(2,1)}), bf16[8,137,128]{2,1,0:T(8,128)(2,1)S(1)}, u32[]{:S(2)}, u32[]{:S(2)}) %all-to-all-start.2) | async-done | bytes 280608 | tf_op jit(solution)/shard_map/all_to_all | solution.py:379
  50.5 0.0 copy-start
  50.5 0.7 copy-done
  51.2 9.0 %edge_rows.1 = bf16[2,4,288,128]{3,2,1,0:T(8,128)(2,1)} custom-call(s32[8,128]{1,0:T(8,128)} %bitcast.31, bf16[8,137,128]{2,1,0:T(8,128)(2,1)} %copy-done, bf16[2,144,144]{2,1,0:T(8,128)(2,1)} %pad.19.vertical_ref, f32[288,9]{1,0:T(8,128)} %pad.20.lon_ref), custom_call_target="tpu_custom_call" | custom-call | tf_op jit(solution)/shard_map/edge_rows/pallas_call | solution.py:392
  60.2 1.1 slice_bitcast_fusion
  61.3 5.8 %collective-permute-start.1 = (bf16[4,288,128]{2,1,0:T(8,128)(2,1)S(1)}, bf16[4,288,128]{2,1,0:T(8,128)(2,1)S(1)}, u32[]{:S(2)}, u32[]{:S(2)}) collective-permute-start(bf16[4,288,128]{2,1,0:T(8,128)(2,1)S(1)} %get-tuple-element.5), channel_id=1, source_target_pairs={{1,0},{2,1},{3,2},{5,4},{6,5},{7,6},{9,8},{10,9},{11,10},{13,12},{... | collective-permute-start | bytes 884744 | tf_op jit(solution)/shard_map/ppermute | solution.py:399
  67.1 3.1 %collective-permute-start = (bf16[4,288,128]{2,1,0:T(8,128)(2,1)S(1)}, bf16[4,288,128]{2,1,0:T(8,128)(2,1)S(1)}, u32[]{:S(2)}, u32[]{:S(2)}) collective-permute-start(bf16[4,288,128]{2,1,0:T(8,128)(2,1)S(1)} %get-tuple-element.6), channel_id=1, source_target_pairs={{0,1},{1,2},{2,3},{4,5},{5,6},{6,7},{8,9},{9,10},{10,11},{12,13},{... | collective-permute-start | bytes 884744 | tf_op jit(solution)/shard_map/ppermute | solution.py:400
  70.2 0.0 copy-done.6
  70.2 0.1 reshape.63
  70.3 0.1 copy.28
  70.4 0.7 pad.21.lat_ref
  71.1 9.1 %mix_levels.1.mixed_ref = f32[288,4608]{1,0:T(8,128)} custom-call(s32[8,128]{1,0:T(8,128)} %bitcast.32, bf16[8,137,128]{2,1,0:T(8,128)(2,1)} %copy-done, bf16[2,144,144]{2,1,0:T(8,128)(2,1)} %pad.19.vertical_ref), custom_call_target="tpu_custom_call" | custom-call | flops 1149239296 | bytes 4718592 | tf_op jit(solution)/shard_map/mix_levels/pallas_call | solution.py:401
  80.2 0.0 collective-permute-done.1.below_ref
  80.2 0.0 copy-start.2
  80.2 0.0 collective-permute-done.above_ref
  80.2 0.7 copy-done.2
  80.9 0.0 copy-start.3
  80.9 0.7 copy-done.3
  81.6 34.5 %filters.1 = f32[8768,128]{1,0:T(8,128)} custom-call(f32[288,4608]{1,0:T(8,128)} %mix_levels.1.mixed_ref, f32[288,9]{1,0:T(8,128)} %pad.20.lon_ref, f32[288,9]{1,0:T(8,128)} %pad.21.lat_ref, bf16[4,288,128]{2,1,0:T(8,128)(2,1)} %copy-done.3, bf16[4,288,128]{2,1,0:T(8,128)(2,1)} %copy-done.2), custom_call_target="tpu_custom_call" | custom-call | tf_op jit(solution)/shard_map/filters/pallas_call | solution.py:413
  (2 shorter events, 0.0 us)
Async XLA Ops:
  0.0 23.8 %copy-start.8 = (s32[1,64,1]{1,2,0:T(1,128)S(1)}, s32[1,64,1]{1,2,0:T(1,128)}, u32[]{:S(2)}) copy-start(s32[1,64,1]{1,2,0:T(1,128)} %param.15) | copy-start | bytes 772
  0.0 23.1 %copy-start.7 = (s32[1,64]{1,0:T(1,128)S(1)}, s32[1,64]{1,0:T(1,128)}, u32[]{:S(2)}) copy-start(s32[1,64]{1,0:T(1,128)} %param.14) | copy-start | bytes 772
  19.7 9.9 %all-to-all-start.1 = ((bf16[8,16,384]{2,1,0:T(8,128)(2,1)}), bf16[8,16,384]{2,1,0:T(8,128)(2,1)S(1)}, u32[]{:S(2)}, u32[]{:S(2)}) async-start(bf16[8,16,384]{2,1,0:T(8,128)(2,1)} %bitcast.29), calls=%async_computation.1 | async-start | bytes 196608 | tf_op jit(solution)/shard_map/all_to_all | solution.py:366
  29.6 13.5 %copy-start.5 = (f32[2,137,9]{1,0,2:T(2,128)S(1)}, f32[2,137,9]{1,0,2:T(2,128)}, u32[]{:S(2)}) copy-start(f32[2,137,9]{1,0,2:T(2,128)} %param.18) | copy-start | bytes 29596
  29.6 13.7 %copy-start.4 = (bf16[2,137,137]{2,0,1:T(2,128)(2,1)S(1)}, bf16[2,137,137]{2,0,1:T(2,128)(2,1)}, u32[]{:S(2)}) copy-start(bf16[2,137,137]{2,0,1:T(2,128)(2,1)} %param.17) | copy-start | bytes 225232
  29.6 0.6 copy-start.1
  30.2 40.0 %copy-start.6 = (f32[2,137,9]{1,0,2:T(2,128)S(1)}, f32[2,137,9]{1,0,2:T(2,128)}, u32[]{:S(2)}) copy-start(f32[2,137,9]{1,0,2:T(2,128)} %param.19) | copy-start | bytes 29596
  37.7 12.8 %all-to-all-start.2 = ((bf16[8,137,128]{2,1,0:T(8,128)(2,1)}), bf16[8,137,128]{2,1,0:T(8,128)(2,1)S(1)}, u32[]{:S(2)}, u32[]{:S(2)}) async-start(bf16[8,137,128]{2,1,0:T(8,128)(2,1)} %departures.1), calls=%async_computation.2 | async-start | bytes 589824 | tf_op jit(solution)/shard_map/all_to_all | solution.py:379
  50.5 0.7 copy-start
  61.3 18.8 %collective-permute-start.1 = (bf16[4,288,128]{2,1,0:T(8,128)(2,1)S(1)}, bf16[4,288,128]{2,1,0:T(8,128)(2,1)S(1)}, u32[]{:S(2)}, u32[]{:S(2)}) collective-permute-start(bf16[4,288,128]{2,1,0:T(8,128)(2,1)S(1)} %get-tuple-element.5), channel_id=1, source_target_pairs={{1,0},{2,1},{3,2},{5,4},{6,5},{7,6},{9,8},{10,9},{11,10},{13,12},{... | collective-permute-start | bytes 884744 | tf_op jit(solution)/shard_map/ppermute | solution.py:399
  67.1 13.1 %collective-permute-start = (bf16[4,288,128]{2,1,0:T(8,128)(2,1)S(1)}, bf16[4,288,128]{2,1,0:T(8,128)(2,1)S(1)}, u32[]{:S(2)}, u32[]{:S(2)}) collective-permute-start(bf16[4,288,128]{2,1,0:T(8,128)(2,1)S(1)} %get-tuple-element.6), channel_id=1, source_target_pairs={{0,1},{1,2},{2,3},{4,5},{5,6},{6,7},{8,9},{9,10},{10,11},{12,13},{... | collective-permute-start | bytes 884744 | tf_op jit(solution)/shard_map/ppermute | solution.py:400
  80.2 0.7 copy-start.2
  80.9 0.7 copy-start.3

commit v2 on v1

v2 whole, which is shorter than its diff:
```python
import functools

import jax
import jax.numpy as jnp
from jax import lax
from jax.experimental import pallas as pl
from jax.experimental.pallas import tpu as pltpu
from jax.sharding import PartitionSpec as P

LANES = 128
F32 = jnp.float32
BF16 = jnp.bfloat16
VMEM_LIMIT = 56 * 1024 * 1024


def lane_iota(shape):
    return lax.broadcasted_iota(jnp.int32, shape, 1)


def row_iota(shape):
    return lax.broadcasted_iota(jnp.int32, shape, 0)


def earlier_rows(size):
    return (lane_iota((size, size)) < row_iota((size, size))).astype(F32).astype(BF16)


def split_codes(codes_ref, records, points):
    flipped = jnp.transpose(codes_ref[...].astype(F32))[:records].astype(jnp.int32)
    tile = lax.div(flipped, points)
    return tile, flipped - tile * points


def gather_kernel(records, capacity, rows, features, codes_ref, state_ref, out_ref, held, pick, row_mask):
    step = pl.program_id(0)
    count = codes_ref.shape[0]
    slots = out_ref.shape[0]
    planes = state_ref.shape[0] // rows

    @pl.when(step == 0)
    def _():
        me = lax.axis_index("lon")
        tile, column = split_codes(codes_ref, records, rows * LANES)
        mine = (tile == me).astype(F32)
        rank = jnp.dot(earlier_rows(records), mine.astype(BF16), preferred_element_type=F32)
        slot = lane_iota(mine.shape) * capacity + rank.astype(jnp.int32)
        slot = jnp.where(tile == me, slot, -1)
        row_of = jnp.zeros((1, slots), F32)
        lon_of = jnp.zeros((1, slots), F32)
        for d in range(count):
            hit = slot[:, d : d + 1] == lane_iota((records, slots))
            row = lax.div(column[:, d : d + 1], LANES)
            lon = column[:, d : d + 1] - row * LANES
            row_of += jnp.sum(jnp.where(hit, (row + 1).astype(F32), 0.0), axis=0, keepdims=True)
            lon_of += jnp.sum(jnp.where(hit, lon.astype(F32), 0.0), axis=0, keepdims=True)
        pick[...] = (row_iota((LANES, slots)) == lon_of.astype(jnp.int32)).astype(F32).astype(BF16)
        row_mask[...] = (row_iota((rows, slots)) == row_of.astype(jnp.int32) - 1).astype(F32)

    found = jnp.dot(state_ref[...].astype(BF16), pick[...], preferred_element_type=F32)
    found = found.reshape(planes, rows, slots) * row_mask[...][None]
    held[pl.ds(pl.multiple_of(step * planes, planes), planes), :] = jnp.sum(found, axis=1)

    @pl.when(step == pl.num_programs(0) - 1)
    def _():
        for t in range(out_ref.shape[1] // LANES):
            out_ref[:, t * LANES : (t + 1) * LANES] = jnp.transpose(
                held[t * LANES : (t + 1) * LANES, :]
            ).astype(BF16)


def gather_state(codes, state, records, capacity):
    variables, levels, rows, cols = state.shape
    features = variables * levels
    wide = pl.cdiv(features, LANES) * LANES
    slots = codes.shape[0] * capacity
    planes = 32
    steps = pl.cdiv(features, planes)
    return pl.pallas_call(
        functools.partial(gather_kernel, records, capacity, rows, features),
        grid=(steps,),
        in_specs=[
            pl.BlockSpec(codes.shape, lambda s: (0, 0)),
            pl.BlockSpec((planes * rows, cols), lambda s: (s, 0)),
        ],
        out_specs=pl.BlockSpec((slots, wide), lambda s: (0, 0)),
        out_shape=jax.ShapeDtypeStruct((slots, wide), BF16),
        scratch_shapes=[
            pltpu.VMEM((wide, slots), F32),
            pltpu.VMEM((cols, slots), BF16),
            pltpu.VMEM((rows, slots), F32),
        ],
        compiler_params=pltpu.CompilerParams(vmem_limit_bytes=VMEM_LIMIT),
        cost_estimate=pl.CostEstimate(
            flops=2 * features * rows * cols * slots, bytes_accessed=features * rows * cols * 4, transcendentals=0
        ),
        name="gather_state",
    )(codes, state.reshape(features * rows, cols))


def departure_kernel(capacity, dest_ref, valid_ref, states_ref, obs_ref, inv_ref, jac_ref, out_ref, state, scaled_rows, total):
    step = pl.program_id(0)
    group, variables, levels, channels = jac_ref.shape
    records = dest_ref.shape[0]
    slots = states_ref.shape[0]

    @pl.when(step == 0)
    def _():
        dest = dest_ref[...]
        named = (dest == lane_iota((records, LANES))).astype(F32)
        before = jnp.dot(earlier_rows(records), named.astype(BF16), preferred_element_type=F32)
        rank = jnp.sum(before * named, axis=1, keepdims=True).astype(jnp.int32)
        chosen = (dest * capacity + rank == lane_iota((records, slots))).astype(F32).astype(BF16)
        columns = jnp.dot(chosen, states_ref[...], preferred_element_type=F32)
        for v in range(variables):
            state[v] = columns[:, v * levels : (v + 1) * levels].astype(BF16)
        scaled_rows[...] = jnp.zeros_like(scaled_rows)
        total[...] = jnp.zeros_like(total)

    first = pl.multiple_of(step * group, group)
    mine = [state[v, pl.ds(first, group), :] for v in range(variables)]
    model = jnp.zeros((group, channels), F32)
    for r in range(group):
        one = jnp.dot(mine[0], jac_ref[r, 0], preferred_element_type=F32)
        for v in range(1, variables):
            one += jnp.dot(mine[v], jac_ref[r, v], preferred_element_type=F32)
        model = jnp.where(row_iota(model.shape) == r, one, model)
    alive = lane_iota(model.shape) < valid_ref[pl.ds(first, group), :]
    weight = jnp.where(alive, inv_ref[pl.ds(first, group), :].astype(F32), 0.0)
    scaled = (weight * (model - obs_ref[pl.ds(first, group), :].astype(F32))).astype(BF16)
    for v in range(variables):
        scaled_rows[pl.ds(pl.multiple_of(v * records + first, group), group), :] = scaled
    against = scaled_rows[...]
    sums = total[...]
    lane = lane_iota(sums.shape)
    for r in range(group):
        for v in range(variables):
            one = lax.dot_general(
                jac_ref[r, v], against, (((1,), (1,)), ((), ())), preferred_element_type=F32
            )
            sums = jnp.where(lane == v * records + first + r, one, sums)
    total[...] = sums

    @pl.when(step == pl.num_programs(0) - 1)
    def _():
        low = sums.astype(BF16)
        for t in range(out_ref.shape[0]):
            out_ref[t] = low


def departures(dest, valid, states, obs, inv, jac, capacity, devices):
    records, variables, levels, channels = jac.shape
    group = 16

    def whole(shape):
        return pl.BlockSpec(shape, lambda s: (0,) * len(shape))

    return pl.pallas_call(
        functools.partial(departure_kernel, capacity),
        grid=(records // group,),
        in_specs=[
            whole(dest.shape),
            whole(valid.shape),
            whole(states.shape),
            whole(obs.shape),
            whole(inv.shape),
            pl.BlockSpec((group, variables, levels, channels), lambda s: (s, 0, 0, 0)),
        ],
        out_specs=whole((devices, levels, variables * records)),
        out_shape=jax.ShapeDtypeStruct((devices, levels, variables * records), BF16),
        scratch_shapes=[
            pltpu.VMEM((variables, records, levels), BF16),
            pltpu.VMEM((variables * records, channels), BF16),
            pltpu.VMEM((levels, variables * records), F32),
        ],
        compiler_params=pltpu.CompilerParams(vmem_limit_bytes=VMEM_LIMIT),
        cost_estimate=pl.CostEstimate(
            flops=4 * jac.size, bytes_accessed=jac.size * 2, transcendentals=0
        ),
        name="departures",
    )(dest, valid, states, obs, inv, jac)


STRIDE = 256
NOWHERE = 1 << 20


def point_key(tile, column, count, reach):
    me = lax.axis_index("lon")
    right, left = lax.rem(me + 1, count), lax.rem(me + count - 1, count)
    row = lax.div(column, LANES)
    lon = column - row * LANES
    key = jnp.where(tile == me, lon + reach, NOWHERE)
    key = jnp.where((tile == right) & (lon < reach), lon + LANES + reach, key)
    key = jnp.where((tile == left) & (lon >= LANES - reach), lon - LANES + reach, key)
    return jnp.where(key == NOWHERE, NOWHERE, key + row * STRIDE)


def plan_kernel(records, points, reach, codes_ref, same_ref, info_ref, down, first):
    count = codes_ref.shape[0]
    span, listed = count * records, same_ref.shape[0]
    tile, column = split_codes(codes_ref, records, points)
    key = point_key(tile, column, count, reach)
    for d in range(count):
        down[d * records : (d + 1) * records, :] = jnp.broadcast_to(key[:, d : d + 1], (records, LANES))
    codes = codes_ref[...]
    tile = lax.div(codes, points)
    key = point_key(tile, codes - tile * points, count, reach)
    per = LANES // records
    across = []
    for t in range(span // LANES):
        lane = lane_iota((1, LANES))
        one = key[per * t : per * t + 1, :]
        for h in range(1, per):
            one = jnp.where(
                lane < h * records, one, pltpu.roll(key[per * t + h : per * t + h + 1, :], h * records, 1)
            )
        across.append(one)
    repeats = jnp.zeros((span, LANES), F32)
    for t, one in enumerate(across):
        before = lane_iota((span, LANES)) + t * LANES < row_iota((span, LANES))
        repeats += ((down[...] == one) & before).astype(F32)
    fresh = jnp.sum(repeats, axis=1, keepdims=True) == 0.0
    first[...] = (fresh & (down[...] < NOWHERE)).astype(F32)
    found = jnp.zeros((listed, LANES), jnp.int32)
    for t, one in enumerate(across):
        rank = jnp.sum(jnp.where(down[...] < one, first[...], 0.0), axis=0, keepdims=True)
        rank = jnp.where(one < NOWHERE, rank.astype(jnp.int32), -1)
        same = rank == row_iota((listed, LANES))
        same_ref[:, t * LANES : (t + 1) * LANES] = same.astype(F32).astype(BF16)
        found = jnp.maximum(found, jnp.where(same, one, 0))
    found = jnp.max(found, axis=1, keepdims=True).astype(F32)
    for b in range(listed // LANES):
        wide = jnp.broadcast_to(found[b * LANES : (b + 1) * LANES], (LANES, LANES))
        info_ref[0:1, b * LANES : (b + 1) * LANES] = jnp.transpose(wide)[0:1].astype(jnp.int32)
    starts = jnp.where(down[...] < lane_iota((span, LANES)) * STRIDE, first[...], 0.0)
    info_ref[0:1, listed:] = jnp.sum(starts, axis=0, keepdims=True).astype(jnp.int32)


def impact_kernel(records, products_ref, same_ref, out_ref, terms):
    count, levels, width = products_ref.shape
    listed = same_ref.shape[0]
    tall = out_ref.shape[0]
    variables = out_ref.shape[1] // listed
    terms[...] = jnp.zeros_like(terms)
    lane = lane_iota((levels, width))
    for pair in range(count // variables):
        one = products_ref[2 * pair].astype(F32)
        two = products_ref[2 * pair + 1].astype(F32)
        first = jnp.where(lane < records, one, pltpu.roll(two, records, 1))
        second = jnp.where(lane < records, pltpu.roll(one, records, 1), two)
        terms[0, 0:levels, pair * width : (pair + 1) * width] = first.astype(BF16)
        terms[1, 0:levels, pair * width : (pair + 1) * width] = second.astype(BF16)
    for v in range(variables):
        out_ref[:, v * listed : (v + 1) * listed] = lax.dot_general(
            terms[v], same_ref[...], (((1,), (1,)), ((), ())), preferred_element_type=F32
        ).astype(BF16)


def filter_kernel(block_of, reach, rows, *refs):
    (*lists, vertical_ref, lon_ref, lat_ref, out_ref, mixed, along, mean) = refs
    lists = [(lists[n], lists[n + 1]) for n in range(0, len(lists) // 2 * 2, 2)]
    listed = lists[0][1].shape[1] // vertical_ref.shape[0]
    features = out_ref.shape[0]
    wide = vertical_ref.shape[2]
    height = out_ref.shape[1]
    window = height + 2 * reach
    pitch = along.shape[0] // window
    step = pl.program_id(0)
    base = block_of(step) * height - reach

    @pl.when(step == 0)
    def _():
        for n, (_, impact) in enumerate(lists):
            total = 0.0
            for v in range(vertical_ref.shape[0]):
                total += lax.dot_general(
                    impact[:, v * listed : (v + 1) * listed],
                    vertical_ref[v],
                    (((0,), (0,)), ((), ())),
                    preferred_element_type=F32,
                )
            mixed[n * listed : (n + 1) * listed, :] = total

    along[...] = jnp.zeros_like(along)
    for n, (info, _) in enumerate(lists):
        offset = (0, -rows, rows)[n] - base
        low = jnp.clip(-offset, 0, rows)
        high = jnp.clip(window - offset, 0, rows)

        def add(s, carry, info=info, n=n, offset=offset):
            key = info[0, s]
            row = lax.shift_right_logical(key, 8) + offset
            place = jnp.bitwise_and(key, STRIDE - 1)
            spot = jnp.bitwise_and(place, 7)
            at = pl.ds(pl.multiple_of(row * pitch + place - spot, 8), 16)
            taps = lon_ref[pl.ds(pl.multiple_of(spot * 16, 16), 16), :]
            along[at, :] += taps * mixed[pl.ds(n * listed + s, 1), :]
            return carry

        lax.fori_loop(info[0, listed + low], info[0, listed + high], add, 0)

    flat = out_ref.reshape(features * height, LANES)
    for t in range(wide // LANES):
        here = slice(t * LANES, (t + 1) * LANES)
        lat = [jnp.broadcast_to(lat_ref[k : k + 1, here], (8, LANES)) for k in range(2 * reach + 1)]

        @pl.loop(0, LANES // 8, unroll=2)
        def _(j):
            sums = [None] * height
            for w in range(window):
                part = along[pl.ds(pl.multiple_of(w * pitch + 8 + j * 8, 8), 8), here]
                for row in range(max(0, w - 2 * reach), min(height, w + 1)):
                    term = lat[w - row] * part
                    sums[row] = term if sums[row] is None else sums[row] + term
            for row in range(height):
                mean[row, pl.ds(pl.multiple_of(j * 8, 8), 8), :] = sums[row]

        kept = min(LANES, features - t * LANES)
        for row in range(height):
            turned = jnp.transpose(mean[row])
            flat[pl.ds(t * LANES * height + row, kept, stride=height), :] = turned[0:kept]


def solution(mesh):
    lon_devices, lat_devices = mesh.shape["lon"], mesh.shape["lat"]

    def body(state_field, jacobian, observed, inverse_var, valid_count, destination, column, vertical, lon_taps, lat_taps):
        variables, levels, rows, cols = state_field.shape
        features = variables * levels
        records, channels = jacobian.shape[1], jacobian.shape[-1]
        capacity = max(2, 2 * records // lon_devices)
        reach = lon_taps.shape[-1] // 2
        points = rows * cols
        span = records * lon_devices
        tall = pl.cdiv(levels, 16) * 16

        dest = destination.reshape(records, 1)
        codes = destination.reshape(1, records) * points + column.reshape(1, records)
        codes = jnp.broadcast_to(jnp.pad(codes, ((0, 0), (0, LANES - records))), (lon_devices, LANES))
        codes = lax.all_to_all(codes, "lon", split_axis=0, concat_axis=0, tiled=True)

        found = gather_state(codes, state_field, records, capacity)
        found = found.reshape(lon_devices, capacity, found.shape[-1])
        found = lax.all_to_all(found, "lon", split_axis=0, concat_axis=0, tiled=True)
        found = found.reshape(lon_devices * capacity, found.shape[-1])

        products = departures(
            dest,
            valid_count.reshape(records, 1),
            found,
            observed.reshape(records, channels),
            inverse_var.reshape(records, channels),
            jacobian.reshape(records, variables, levels, channels),
            capacity,
            lon_devices,
        )
        products = lax.all_to_all(products, "lon", split_axis=0, concat_axis=0, tiled=True)

        listed = 3 * lon_devices * capacity
        wide = pl.cdiv(features, LANES) * LANES
        plan = pl.pallas_call(
            functools.partial(plan_kernel, records, points, reach),
            out_shape=(
                jax.ShapeDtypeStruct((listed, span), BF16),
                jax.ShapeDtypeStruct((1, listed + LANES), jnp.int32),
            ),
            scratch_shapes=[pltpu.VMEM((span, LANES), jnp.int32), pltpu.VMEM((span, LANES), F32)],
            compiler_params=pltpu.CompilerParams(vmem_limit_bytes=16 * 1024 * 1024),
            cost_estimate=pl.CostEstimate(flops=8 * span * span, bytes_accessed=span * listed * 2, transcendentals=0),
            name="plan_points",
        )
        same, info = plan(codes)
        down = [(i, i + 1) for i in range(lat_devices - 1)]
        up = [(i + 1, i) for i in range(lat_devices - 1)]
        info_above, info_below = lax.ppermute(info, "lat", down), lax.ppermute(info, "lat", up)

        impact = pl.pallas_call(
            functools.partial(impact_kernel, records),
            out_shape=jax.ShapeDtypeStruct((tall, variables * listed), BF16),
            scratch_shapes=[pltpu.VMEM((variables, tall, span), BF16)],
            compiler_params=pltpu.CompilerParams(vmem_limit_bytes=16 * 1024 * 1024),
            name="impact_columns",
        )(products, same)
        above, below = lax.ppermute(impact, "lat", down), lax.ppermute(impact, "lat", up)

        mixing = jnp.stack(
            [
                jnp.pad(vertical[v], ((0, tall - levels), (v * levels, wide - (v + 1) * levels)))
                for v in range(variables)
            ]
        )
        lon_flat = jnp.pad(lon_taps.reshape(features, -1).T[::-1], ((0, 0), (0, wide - features)))
        taps = lon_flat.shape[0]
        lon_table = jnp.concatenate([jnp.pad(lon_flat, ((b, 16 - taps - b), (0, 0))) for b in range(8)])
        lat_flat = jnp.pad(lat_taps.reshape(features, -1).T, ((0, 0), (0, wide - features)))

        height = 8
        blocks = rows // height
        pitch = LANES + 16

        def filtered(lists, steps, block_of, before, name):
            held = [pl.BlockSpec(memory_space=pltpu.SMEM), pl.BlockSpec(memory_space=pltpu.VMEM)] * (len(lists) // 2)
            held += [pl.BlockSpec(memory_space=pltpu.VMEM)] * 3
            given = list(lists) + [mixing, lon_table, lat_flat]
            kernel = functools.partial(filter_kernel, block_of, reach, rows)
            if before is not None:
                given.append(before)
                held.append(pl.BlockSpec(memory_space=pl.ANY))
                at = len(lists) + 3
                inner = kernel
                kernel = lambda *refs: inner(*refs[:at], *refs[at + 1 :])
            return pl.pallas_call(
                kernel,
                grid=(steps,),
                in_specs=held,
                out_specs=pl.BlockSpec((features, height, cols), lambda s: (0, block_of(s), 0)),
                out_shape=jax.ShapeDtypeStruct((features, rows, cols), F32),
                scratch_shapes=[
                    pltpu.VMEM((len(lists) // 2 * listed, wide), F32),
                    pltpu.VMEM(((height + 2 * reach) * pitch, wide), F32),
                    pltpu.VMEM((height, cols, LANES), F32),
                ],
                input_output_aliases={} if before is None else {len(given) - 1: 0},
                compiler_params=pltpu.CompilerParams(vmem_limit_bytes=24 * 1024 * 1024),
                cost_estimate=pl.CostEstimate(
                    flops=40 * features * rows * cols, bytes_accessed=features * rows * cols * 2, transcendentals=0
                ),
                name=name,
            )(*given)

        inner = filtered([info, impact], blocks - 2, lambda s: s + 1, None, "inner_rows")
        result = filtered(
            [info, impact, info_above, above, info_below, below],
            2,
            lambda s: s * (blocks - 1),
            inner,
            "outer_rows",
        )
        return result.reshape(variables, levels, rows, cols)

    placed = (
        P(None, None, "lat", "lon"),
        P("lat", "lon", None, None, None),
        P("lat", "lon", None),
        P("lat", "lon", None),
        P("lat", "lon"),
        P("lat", "lon", None),
        P("lat", "lon"),
        P(),
        P(),
        P(),
    )
    return jax.shard_map(
        body, mesh=mesh, in_specs=placed, out_specs=P(None, None, "lat", "lon"), check_vma=False
    )
```

time: 117 us -> 84.9 us (0.73)
  Pallas kernels: 67.7 us -> 29.6 us
  starting transfers between devices: 17.6 us -> 29.6 us
  blocking collectives: 11.4 us -> 0 us
  waiting for transfers between devices: 5.66 us -> 12.1 us
    pallas_call x3 -> x4, Pallas kernels: 52.6 us -> 14.5 us  [the longest x2 13.2 us: filtered(): pl.pallas_call(kernel, grid=(steps,), in_specs=held, out_specs=pl.BlockSp...]
    all_to_all x1 -> x0, blocking collectives: 11.4 us -> none  [body(): lax.all_to_all(codes, 'lon', split_axis=0, concat_axis=0, tiled=True)]
    all_to_all x0 -> x1, starting transfers between devices: none -> 6.35 us  [body(): lax.all_to_all(codes, 'lon', split_axis=0, concat_axis=0, tiled=True)]
    all_to_all x1, waiting for transfers between devices: 0.01 us -> 5.95 us  [body(): lax.all_to_all(found, 'lon', split_axis=0, concat_axis=0, tiled=True)]
    ppermute x2 -> x4, starting transfers between devices: 8.84 us -> 14.3 us  [the longest x1 5.65 us: body(): lax.ppermute(impact, 'lat', up)]
    all_to_all x1, starting transfers between devices: 3.36 us -> 5.59 us  [body(): lax.all_to_all(found, 'lon', split_axis=0, concat_axis=0, tiled=True)]
    pad x3 -> x2, local copies, waits for them, and re-layouts: 2.03 us -> 0.02 us  [the longest x1 0.01 us: body(): jnp.pad(lat_taps.reshape(features, -1).T, ((0, 0), (0, wide - features)))]
    all_to_all x1, starting transfers between devices: 5.37 us -> 3.42 us  [body(): lax.all_to_all(products, 'lon', split_axis=0, concat_axis=0, tiled=True)]
  transfers between devices with their start and end apart: 4 -> 7, of which waited for: 1 -> 2; matrix products, arithmetic and copies ran while one was open for 8% -> 12% of each run, Pallas kernels for 8% -> 9%
where the time goes in v2:
time: 84.9 us; the launch traced here: 84.2 us
  starting transfers between devices  29.6 us (35%)
  Pallas kernels  29.6 us (35%)
  waiting for transfers between devices  12.1 us (14%)
  local copies, waits for them, and re-layouts  12 us (14%)
    pallas_call x2, Pallas kernels, filtered(): pl.pallas_call(kernel, grid=(steps,), in_specs=held, out_specs=pl.BlockSp...  13.2 us
    pallas_call x1, Pallas kernels, gather_state(): pl.pallas_call(functools.partial(gather_kernel, records, capacity, rows,...  7.56 us
    pallas_call x1, Pallas kernels, departures(): pl.pallas_call(functools.partial(departure_kernel, capacity), grid=(recor...  7.51 us
    unnamed x16, local copies, waits for them, and re-layouts  6.39 us
    all_to_all x1, starting transfers between devices, body(): lax.all_to_all(codes, 'lon', split_axis=0, concat_axis=0, tiled=True)  6.35 us
    all_to_all x1, waiting for transfers between devices, body(): lax.all_to_all(products, 'lon', split_axis=0, concat_axis=0, tiled=True)  6.11 us
    all_to_all x1, waiting for transfers between devices, body(): lax.all_to_all(found, 'lon', split_axis=0, concat_axis=0, tiled=True)  5.95 us
    ppermute x1, starting transfers between devices, body(): lax.ppermute(impact, 'lat', up)  5.65 us
  transfers between devices with their start and end apart: 7, of which 2 were waited for; matrix products, arithmetic and copies ran while one was open for 12% of the time, Pallas kernels for 9%

profile of v2, /device:TPU:1, one launch (start us, length us, event | category | flops | bytes accessed | tf_op | source)
XLA Modules:
  0.0 84.2 jit_solution(18247681544403731572)
XLA Ops:
  0.0 0.7 bitcast_add_fusion
  0.7 0.6 broadcast_in_dim.2
  1.3 6.4 %all-to-all-start = ((s32[8,1,128]{2,1,0:T(1,128)}), s32[8,1,128]{2,1,0:T(1,128)S(1)}, u32[]{:S(2)}, u32[]{:S(2)}) async-start(s32[8,1,128]{2,1,0:T(1,128)} %broadcast_in_dim.2), calls=%async_computation | async-start | bytes 8192 | tf_op jit(solution)/shard_map/all_to_all | solution.py:340
  7.6 0.8 reshape.62
  8.4 0.1 rev.3
  8.6 1.2 %fusion = (bf16[1,137,137]{2,0,1:T(2,128)(2,1)S(1)}, bf16[1,137,137]{2,0,1:T(2,128)(2,1)S(1)}) fusion(bf16[2,137,137]{2,0,1:T(2,128)(2,1)} %param.17), kind=kLoop, calls=%fused_computation.16 | loop fusion | bytes 150152 | tf_op jit(solution)/shard_map/slice | solution.py:388
  9.8 1.4 %copy.19.valid_ref = s32[64,1]{1,0:T(8,128)} copy(s32[64,1]{0,1:T(1,128)} %bitcast.40) | data formatting | bytes 512 | tf_op jit(solution)/shard_map/reshape | solution.py:349
  11.2 1.4 %copy.18.dest_ref = s32[64,1]{1,0:T(8,128)} copy(s32[64,1]{0,1:T(1,128)} %bitcast.41) | data formatting | bytes 512 | tf_op jit(solution)/shard_map/reshape | solution.py:337
  12.5 5.1 %copy.27 = bf16[1,64,2,137,128]{4,3,2,1,0:T(8,128)(2,1)} copy(bf16[1,64,2,137,128]{4,2,3,1,0:T(2,128)(2,1)} %param.11) | data formatting | bytes 8978432 | tf_op args[1]
  17.6 0.0 all-to-all-done
  17.6 0.0 copy-start
  17.6 0.6 copy-done
  18.2 0.0 copy-start.3
  18.2 7.6 %gather_state.1 = bf16[128,384]{1,0:T(8,128)(2,1)} custom-call(s32[8,128]{1,0:T(8,128)} %bitcast.30, f32[8768,128]{1,0:T(8,128)} %bitcast.33), custom_call_target="tpu_custom_call" | custom-call | flops 287309824 | bytes 4489216 | tf_op jit(solution)/shard_map/gather_state/pallas_call | solution.py:78
  25.8 0.0 copy-start.1
  25.8 5.6 %all-to-all-start.1 = ((bf16[8,16,384]{2,1,0:T(8,128)(2,1)}), bf16[8,16,384]{2,1,0:T(8,128)(2,1)S(1)}, u32[]{:S(2)}, u32[]{:S(2)}) async-start(bf16[8,16,384]{2,1,0:T(8,128)(2,1)} %bitcast.35), calls=%async_computation.1 | async-start | bytes 196608 | tf_op jit(solution)/shard_map/all_to_all | solution.py:344
  31.4 6.0 %all-to-all-done.1 = bf16[8,16,384]{2,1,0:T(8,128)(2,1)S(1)} async-done(((bf16[8,16,384]{2,1,0:T(8,128)(2,1)}), bf16[8,16,384]{2,1,0:T(8,128)(2,1)S(1)}, u32[]{:S(2)}, u32[]{:S(2)}) %all-to-all-start.1) | async-done | bytes 98336 | tf_op jit(solution)/shard_map/all_to_all | solution.py:344
  37.3 0.0 copy-start.2
  37.4 0.6 copy-done.2
  38.0 7.5 %departures.1 = bf16[8,137,128]{2,1,0:T(8,128)(2,1)} custom-call(s32[64,1]{1,0:T(8,128)} %copy.18.dest_ref, s32[64,1]{1,0:T(8,128)} %copy.19.valid_ref, bf16[128,384]{1,0:T(8,128)(2,1)} %bitcast.34, bf16[64,128]{1,0:T(8,128)(2,1)} %bitcast.38, bf16[64,128]{1,0:T(8,128)(2,1)} %bitcast.39, bf16[64,2,137,128]{3,2,1,0:T(8,128)(2,1)} %bitcast.32), custom_call_target="tpu_custom_call" | custom-call | flops 8978432 | bytes 4489216 | tf_op jit(solution)/shard_map/departures/pallas_call | solution.py:157
  45.5 3.4 %all-to-all-start.2 = ((bf16[8,137,128]{2,1,0:T(8,128)(2,1)}), bf16[8,137,128]{2,1,0:T(8,128)(2,1)S(1)}, u32[]{:S(2)}, u32[]{:S(2)}) async-start(bf16[8,137,128]{2,1,0:T(8,128)(2,1)} %departures.1), calls=%async_computation.2 | async-start | bytes 589824 | tf_op jit(solution)/shard_map/all_to_all | solution.py:357
  49.0 0.0 copy-done.3
  49.0 0.1 reshape.63
  49.1 0.1 pad_bitcast_fusion
  49.2 0.0 copy-done.1
  49.2 0.9 %plan_points.1 = (bf16[384,512]{1,0:T(8,128)(2,1)S(1)}, s32[1,512]{1,0:T(1,128)S(1)}) custom-call(s32[8,128]{1,0:T(8,128)S(1)} %bitcast.31), custom_call_target="tpu_custom_call" | custom-call | flops 2097152 | bytes 393216 | tf_op jit(solution)/shard_map/plan_points/pallas_call | solution.py:372
  50.1 6.1 %all-to-all-done.2.products_ref = bf16[8,137,128]{2,1,0:T(8,128)(2,1)S(1)} async-done(((bf16[8,137,128]{2,1,0:T(8,128)(2,1)}), bf16[8,137,128]{2,1,0:T(8,128)(2,1)S(1)}, u32[]{:S(2)}, u32[]{:S(2)}) %all-to-all-start.2) | async-done | bytes 280608 | tf_op jit(solution)/shard_map/all_to_all | solution.py:357
  56.2 0.4 impact_columns.1.refs_1_
  56.7 5.7 %collective-permute-start.3 = (bf16[144,768]{1,0:T(8,128)(2,1)S(1)}, bf16[144,768]{1,0:T(8,128)(2,1)S(1)}, u32[]{:S(2)}, u32[]{:S(2)}) collective-permute-start(bf16[144,768]{1,0:T(8,128)(2,1)S(1)} %impact_columns.1.refs_1_), channel_id=1, source_target_pairs={{1,0},{2,1},{3,2},{5,4},{6,5},{7,6},{9,8},{10,9},{11,10},{13,12},{... | collective-permute-start | bytes 663560 | tf_op jit(solution)/shard_map/ppermute | solution.py:384
  62.3 3.1 %collective-permute-start.1 = (bf16[144,768]{1,0:T(8,128)(2,1)S(1)}, bf16[144,768]{1,0:T(8,128)(2,1)S(1)}, u32[]{:S(2)}, u32[]{:S(2)}) collective-permute-start(bf16[144,768]{1,0:T(8,128)(2,1)S(1)} %impact_columns.1.refs_1_), channel_id=1, source_target_pairs={{0,1},{1,2},{2,3},{4,5},{5,6},{6,7},{8,9},{9,10},{10,11},{12,13},{... | collective-permute-start | bytes 663560 | tf_op jit(solution)/shard_map/ppermute | solution.py:384
  65.4 1.9 %collective-permute-start.2 = (s32[1,512]{1,0:T(1,128)S(1)}, s32[1,512]{1,0:T(1,128)S(1)}, u32[]{:S(2)}, u32[]{:S(2)}) collective-permute-start(s32[1,512]{1,0:T(1,128)S(1)} %get-tuple-element.7.refs_0_), channel_id=1, source_target_pairs={{1,0},{2,1},{3,2},{5,4},{6,5},{7,6},{9,8},{10,9},{11,10},{13,12},{... | collective-permute-start | bytes 6152 | tf_op jit(solution)/shard_map/ppermute | solution.py:375
  67.4 3.6 %collective-permute-start = (s32[1,512]{1,0:T(1,128)S(1)}, s32[1,512]{1,0:T(1,128)S(1)}, u32[]{:S(2)}, u32[]{:S(2)}) collective-permute-start(s32[1,512]{1,0:T(1,128)S(1)} %get-tuple-element.7.refs_0_), channel_id=1, source_target_pairs={{0,1},{1,2},{2,3},{4,5},{5,6},{6,7},{8,9},{9,10},{10,11},{12,13},{... | collective-permute-start | bytes 6152 | tf_op jit(solution)/shard_map/ppermute | solution.py:375
  71.0 6.3 %inner_rows.1.refs_9_ = f32[274,32,128]{2,1,0:T(8,128)} custom-call(s32[1,512]{1,0:T(1,128)S(1)} %get-tuple-element.7.refs_0_, bf16[144,768]{1,0:T(8,128)(2,1)S(1)} %impact_columns.1.refs_1_, bf16[2,144,384]{2,1,0:T(8,128)(2,1)S(1)} %pad_maximum_fusion.refs_2_.refs_6_, f32[128,384]{1,0:T(8,128)S(1)} %pad_dynamic-update-slice_fusion.refs_3_.refs_7_, ...), custom_call_target="tpu_custom_call" | custom-call | flops 44892160 | bytes 2244608 | tf_op jit(solution)/shard_map/inner_rows/pallas_call | solution.py:412
  77.3 0.0 collective-permute-done.2.refs_4_
  77.3 0.0 collective-permute-done.refs_2_
  77.3 0.0 collective-permute-done.3.refs_5_
  77.3 0.0 collective-permute-done.1.refs_3_
  77.3 6.9 %outer_rows.1 = f32[274,32,128]{2,1,0:T(8,128)} custom-call(s32[1,512]{1,0:T(1,128)S(1)} %get-tuple-element.7.refs_0_, bf16[144,768]{1,0:T(8,128)(2,1)S(1)} %impact_columns.1.refs_1_, s32[1,512]{1,0:T(1,128)S(1)} %collective-permute-done.refs_2_, bf16[144,768]{1,0:T(8,128)(2,1)S(1)} %collective-permute-done.1.refs_3_, ...), custom_call_target="tpu_custom_call", output_to_operand_aliasing={{}: (9, {})} | custom-call | flops 44892160 | bytes 2244608 | tf_op jit(solution)/shard_map/outer_rows/pallas_call | solution.py:412
  (14 shorter events, 0.2 us)
Async XLA Ops:
  1.3 16.4 %all-to-all-start = ((s32[8,1,128]{2,1,0:T(1,128)}), s32[8,1,128]{2,1,0:T(1,128)S(1)}, u32[]{:S(2)}, u32[]{:S(2)}) async-start(s32[8,1,128]{2,1,0:T(1,128)} %broadcast_in_dim.2), calls=%async_computation | async-start | bytes 8192 | tf_op jit(solution)/shard_map/all_to_all | solution.py:340
  17.6 0.6 copy-start
  18.2 30.7 %copy-start.3 = (f32[2,137,9]{1,0,2:T(2,128)S(1)}, f32[2,137,9]{1,0,2:T(2,128)}, u32[]{:S(2)}) copy-start(f32[2,137,9]{1,0,2:T(2,128)} %param.19) | copy-start | bytes 29596
  25.8 23.4 %copy-start.1 = (s32[8,1,128]{2,1,0:T(1,128)S(1)}, s32[8,1,128]{2,1,0:T(1,128)}, u32[]{:S(2)}) copy-start(s32[8,1,128]{2,1,0:T(1,128)} %copy-done) | copy-start | bytes 12292
  25.8 11.6 %all-to-all-start.1 = ((bf16[8,16,384]{2,1,0:T(8,128)(2,1)}), bf16[8,16,384]{2,1,0:T(8,128)(2,1)S(1)}, u32[]{:S(2)}, u32[]{:S(2)}) async-start(bf16[8,16,384]{2,1,0:T(8,128)(2,1)} %bitcast.35), calls=%async_computation.1 | async-start | bytes 196608 | tf_op jit(solution)/shard_map/all_to_all | solution.py:344
  37.3 0.6 copy-start.2
  45.5 10.7 %all-to-all-start.2 = ((bf16[8,137,128]{2,1,0:T(8,128)(2,1)}), bf16[8,137,128]{2,1,0:T(8,128)(2,1)S(1)}, u32[]{:S(2)}, u32[]{:S(2)}) async-start(bf16[8,137,128]{2,1,0:T(8,128)(2,1)} %departures.1), calls=%async_computation.2 | async-start | bytes 589824 | tf_op jit(solution)/shard_map/all_to_all | solution.py:357
  56.7 20.7 %collective-permute-start.3 = (bf16[144,768]{1,0:T(8,128)(2,1)S(1)}, bf16[144,768]{1,0:T(8,128)(2,1)S(1)}, u32[]{:S(2)}, u32[]{:S(2)}) collective-permute-start(bf16[144,768]{1,0:T(8,128)(2,1)S(1)} %impact_columns.1.refs_1_), channel_id=1, source_target_pairs={{1,0},{2,1},{3,2},{5,4},{6,5},{7,6},{9,8},{10,9},{11,10},{13,12},{... | collective-permute-start | bytes 663560 | tf_op jit(solution)/shard_map/ppermute | solution.py:384
  62.3 15.0 %collective-permute-start.1 = (bf16[144,768]{1,0:T(8,128)(2,1)S(1)}, bf16[144,768]{1,0:T(8,128)(2,1)S(1)}, u32[]{:S(2)}, u32[]{:S(2)}) collective-permute-start(bf16[144,768]{1,0:T(8,128)(2,1)S(1)} %impact_columns.1.refs_1_), channel_id=1, source_target_pairs={{0,1},{1,2},{2,3},{4,5},{5,6},{6,7},{8,9},{9,10},{10,11},{12,13},{... | collective-permute-start | bytes 663560 | tf_op jit(solution)/shard_map/ppermute | solution.py:384
  65.4 11.9 %collective-permute-start.2 = (s32[1,512]{1,0:T(1,128)S(1)}, s32[1,512]{1,0:T(1,128)S(1)}, u32[]{:S(2)}, u32[]{:S(2)}) collective-permute-start(s32[1,512]{1,0:T(1,128)S(1)} %get-tuple-element.7.refs_0_), channel_id=1, source_target_pairs={{1,0},{2,1},{3,2},{5,4},{6,5},{7,6},{9,8},{10,9},{11,10},{13,12},{... | collective-permute-start | bytes 6152 | tf_op jit(solution)/shard_map/ppermute | solution.py:375
  67.4 10.0 %collective-permute-start = (s32[1,512]{1,0:T(1,128)S(1)}, s32[1,512]{1,0:T(1,128)S(1)}, u32[]{:S(2)}, u32[]{:S(2)}) collective-permute-start(s32[1,512]{1,0:T(1,128)S(1)} %get-tuple-element.7.refs_0_), channel_id=1, source_target_pairs={{0,1},{1,2},{2,3},{4,5},{5,6},{6,7},{8,9},{9,10},{10,11},{12,13},{... | collective-permute-start | bytes 6152 | tf_op jit(solution)/shard_map/ppermute | solution.py:375

commit v3 on v2

--- a/solution.py
+++ b/solution.py
@@ -31,41 +31,46 @@
     return tile, flipped - tile * points
 
 
-def gather_kernel(records, capacity, rows, features, codes_ref, state_ref, out_ref, held, pick, row_mask):
-    step = pl.program_id(0)
+def gather_kernel(records, capacity, rows, levels, chunk, codes_ref, state_ref, out_ref, state, held, arrived):
     count = codes_ref.shape[0]
     slots = out_ref.shape[0]
-    planes = state_ref.shape[0] // rows
-
-    @pl.when(step == 0)
-    def _():
-        me = lax.axis_index("lon")
-        tile, column = split_codes(codes_ref, records, rows * LANES)
-        mine = (tile == me).astype(F32)
-        rank = jnp.dot(earlier_rows(records), mine.astype(BF16), preferred_element_type=F32)
-        slot = lane_iota(mine.shape) * capacity + rank.astype(jnp.int32)
-        slot = jnp.where(tile == me, slot, -1)
-        row_of = jnp.zeros((1, slots), F32)
-        lon_of = jnp.zeros((1, slots), F32)
-        for d in range(count):
-            hit = slot[:, d : d + 1] == lane_iota((records, slots))
-            row = lax.div(column[:, d : d + 1], LANES)
-            lon = column[:, d : d + 1] - row * LANES
-            row_of += jnp.sum(jnp.where(hit, (row + 1).astype(F32), 0.0), axis=0, keepdims=True)
-            lon_of += jnp.sum(jnp.where(hit, lon.astype(F32), 0.0), axis=0, keepdims=True)
-        pick[...] = (row_iota((LANES, slots)) == lon_of.astype(jnp.int32)).astype(F32).astype(BF16)
-        row_mask[...] = (row_iota((rows, slots)) == row_of.astype(jnp.int32) - 1).astype(F32)
-
-    found = jnp.dot(state_ref[...].astype(BF16), pick[...], preferred_element_type=F32)
-    found = found.reshape(planes, rows, slots) * row_mask[...][None]
-    held[pl.ds(pl.multiple_of(step * planes, planes), planes), :] = jnp.sum(found, axis=1)
-
-    @pl.when(step == pl.num_programs(0) - 1)
-    def _():
-        for t in range(out_ref.shape[1] // LANES):
-            out_ref[:, t * LANES : (t + 1) * LANES] = jnp.transpose(
-                held[t * LANES : (t + 1) * LANES, :]
-            ).astype(BF16)
+    variables = state_ref.shape[0] // (rows * levels)
+    parts = []
+    for first in range(0, levels, chunk):
+        size = min(chunk, levels - first)
+        for v in range(variables):
+            here = pl.ds((v * levels + first) * rows, size * rows)
+            copy = pltpu.make_async_copy(state_ref.at[here], state.at[here], arrived.at[len(parts)])
+            copy.start()
+            parts.append((v, first, size, here, copy))
+
+    held[...] = jnp.zeros_like(held)
+    me = lax.axis_index("lon")
+    tile, column = split_codes(codes_ref, records, rows * LANES)
+    mine = (tile == me).astype(F32)
+    rank = jnp.dot(earlier_rows(records), mine.astype(BF16), preferred_element_type=F32)
+    slot = lane_iota(mine.shape) * capacity + rank.astype(jnp.int32)
+    slot = jnp.where(tile == me, slot, -1)
+    row_of = jnp.zeros((1, slots), F32)
+    lon_of = jnp.zeros((1, slots), F32)
+    for d in range(count):
+        hit = slot[:, d : d + 1] == lane_iota((records, slots))
+        row = lax.div(column[:, d : d + 1], LANES)
+        lon = column[:, d : d + 1] - row * LANES
+        row_of += jnp.sum(jnp.where(hit, (row + 1).astype(F32), 0.0), axis=0, keepdims=True)
+        lon_of += jnp.sum(jnp.where(hit, lon.astype(F32), 0.0), axis=0, keepdims=True)
+    pick = (row_iota((LANES, slots)) == lon_of.astype(jnp.int32)).astype(F32).astype(BF16)
+    row_mask = (row_iota((rows, slots)) == row_of.astype(jnp.int32) - 1).astype(F32)
+
+    for v, first, size, here, copy in parts:
+        copy.wait()
+        found = jnp.dot(state[here, :].astype(BF16), pick, preferred_element_type=F32)
+        found = found.reshape(size, rows, slots) * row_mask[None]
+        held[pl.ds(variables * first + v, size, stride=variables), :] = jnp.sum(found, axis=1)
+    for t in range(out_ref.shape[1] // LANES):
+        out_ref[:, t * LANES : (t + 1) * LANES] = jnp.transpose(
+            held[t * LANES : (t + 1) * LANES, :]
+        ).astype(BF16)
 
 
 def gather_state(codes, state, records, capacity):
@@ -73,23 +78,17 @@
     features = variables * levels
     wide = pl.cdiv(features, LANES) * LANES
     slots = codes.shape[0] * capacity
-    planes = 32
-    steps = pl.cdiv(features, planes)
+    chunk = 32
     return pl.pallas_call(
-        functools.partial(gather_kernel, records, capacity, rows, features),
-        grid=(steps,),
-        in_specs=[
-            pl.BlockSpec(codes.shape, lambda s: (0, 0)),
-            pl.BlockSpec((planes * rows, cols), lambda s: (s, 0)),
-        ],
-        out_specs=pl.BlockSpec((slots, wide), lambda s: (0, 0)),
+        functools.partial(gather_kernel, records, capacity, rows, levels, chunk),
+        in_specs=[pl.BlockSpec(memory_space=pltpu.VMEM), pl.BlockSpec(memory_space=pl.ANY)],
         out_shape=jax.ShapeDtypeStruct((slots, wide), BF16),
         scratch_shapes=[
+            pltpu.VMEM((features * rows, cols), F32),
             pltpu.VMEM((wide, slots), F32),
-            pltpu.VMEM((cols, slots), BF16),
-            pltpu.VMEM((rows, slots), F32),
+            pltpu.SemaphoreType.DMA((variables * pl.cdiv(levels, chunk),)),
         ],
-        compiler_params=pltpu.CompilerParams(vmem_limit_bytes=VMEM_LIMIT),
+        compiler_params=pltpu.CompilerParams(vmem_limit_bytes=20 * 1024 * 1024),
         cost_estimate=pl.CostEstimate(
             flops=2 * features * rows * cols * slots, bytes_accessed=features * rows * cols * 4, transcendentals=0
         ),
@@ -97,82 +96,97 @@
     )(codes, state.reshape(features * rows, cols))
 
 
-def departure_kernel(capacity, dest_ref, valid_ref, states_ref, obs_ref, inv_ref, jac_ref, out_ref, state, scaled_rows, total):
-    step = pl.program_id(0)
-    group, variables, levels, channels = jac_ref.shape
+def departure_kernel(capacity, group, dest_ref, valid_ref, states_ref, obs_ref, inv_ref, jac_ref, out_ref, jac, scaled_rows, sums, total, arrived):
     records = dest_ref.shape[0]
     slots = states_ref.shape[0]
-
-    @pl.when(step == 0)
-    def _():
-        dest = dest_ref[...]
-        named = (dest == lane_iota((records, LANES))).astype(F32)
-        before = jnp.dot(earlier_rows(records), named.astype(BF16), preferred_element_type=F32)
-        rank = jnp.sum(before * named, axis=1, keepdims=True).astype(jnp.int32)
-        chosen = (dest * capacity + rank == lane_iota((records, slots))).astype(F32).astype(BF16)
-        columns = jnp.dot(chosen, states_ref[...], preferred_element_type=F32)
-        for v in range(variables):
-            state[v] = columns[:, v * levels : (v + 1) * levels].astype(BF16)
-        scaled_rows[...] = jnp.zeros_like(scaled_rows)
-        total[...] = jnp.zeros_like(total)
-
-    first = pl.multiple_of(step * group, group)
-    mine = [state[v, pl.ds(first, group), :] for v in range(variables)]
-    model = jnp.zeros((group, channels), F32)
-    for r in range(group):
-        one = jnp.dot(mine[0], jac_ref[r, 0], preferred_element_type=F32)
-        for v in range(1, variables):
-            one += jnp.dot(mine[v], jac_ref[r, v], preferred_element_type=F32)
-        model = jnp.where(row_iota(model.shape) == r, one, model)
-    alive = lane_iota(model.shape) < valid_ref[pl.ds(first, group), :]
-    weight = jnp.where(alive, inv_ref[pl.ds(first, group), :].astype(F32), 0.0)
-    scaled = (weight * (model - obs_ref[pl.ds(first, group), :].astype(F32))).astype(BF16)
-    for v in range(variables):
-        scaled_rows[pl.ds(pl.multiple_of(v * records + first, group), group), :] = scaled
-    against = scaled_rows[...]
-    sums = total[...]
-    lane = lane_iota(sums.shape)
-    for r in range(group):
-        for v in range(variables):
-            one = lax.dot_general(
-                jac_ref[r, v], against, (((1,), (1,)), ((), ())), preferred_element_type=F32
+    channels = jac_ref.shape[1]
+    features = jac_ref.shape[0] // records
+    span = group * features
+    copies = []
+    for g in range(records // group):
+        here = pl.ds(g * span, span)
+        copies.append(pltpu.make_async_copy(jac_ref.at[here], jac.at[here], arrived.at[g]))
+        copies[g].start()
+
+    dest = dest_ref[...]
+    named = (dest == lane_iota((records, LANES))).astype(F32)
+    before = jnp.dot(earlier_rows(records), named.astype(BF16), preferred_element_type=F32)
+    rank = jnp.sum(before * named, axis=1, keepdims=True).astype(jnp.int32)
+    chosen = (dest * capacity + rank == lane_iota((records, slots))).astype(F32).astype(BF16)
+    columns = jnp.dot(chosen, states_ref[...], preferred_element_type=F32)
+    alive = lane_iota((records, channels)) < valid_ref[...]
+    weight = jnp.where(alive, inv_ref[...].astype(F32), 0.0)
+    scaled_rows[...] = jnp.zeros_like(scaled_rows)
+    total[...] = jnp.zeros_like(total)
+
+    tiles, skip = divmod(features, LANES)
+    wide = columns.shape[1]
+    reach = pl.cdiv(skip * (group - 1) + features, LANES)
+    row = row_iota((group, LANES))
+    half = total.shape[0] // 2
+    for g in range(records // group):
+        mine = columns[g * group : (g + 1) * group]
+        mine = jnp.concatenate([mine, jnp.zeros((group, reach * LANES - wide), F32)], axis=1)
+        bit = 1
+        while bit < group:
+            moved = pltpu.roll(mine, skip * bit, 1)
+            mine = jnp.where(jnp.bitwise_and(row_iota(mine.shape), bit) > 0, moved, mine)
+            bit *= 2
+        spread = []
+        for t in range(pl.cdiv(span, LANES)):
+            piece = jnp.zeros((group, LANES), F32)
+            for r in range(group):
+                at = t - tiles * r
+                if 0 <= at < reach:
+                    piece = jnp.where(row == r, mine[:, at * LANES : (at + 1) * LANES], piece)
+            spread.append(piece.astype(BF16))
+        spread = jnp.concatenate(spread, axis=1)[:, :span]
+        copies[g].wait()
+        here = slice(g * span, (g + 1) * span)
+        model = jnp.dot(spread, jac[here, :], preferred_element_type=F32)
+        own = slice(g * group, (g + 1) * group)
+        misfit = weight[own] * (model - obs_ref[own, :].astype(F32))
+        scaled_rows[own, :] = misfit.astype(BF16)
+        against = scaled_rows[...]
+        for h in range(2):
+            part = span // 2
+            sums[...] = lax.dot_general(
+                jac[g * span + h * part : g * span + (h + 1) * part, :],
+                against,
+                (((1,), (1,)), ((), ())),
+                preferred_element_type=F32,
             )
-            sums = jnp.where(lane == v * records + first + r, one, sums)
-    total[...] = sums
-
-    @pl.when(step == pl.num_programs(0) - 1)
-    def _():
-        low = sums.astype(BF16)
-        for t in range(out_ref.shape[0]):
-            out_ref[t] = low
-
-
-def departures(dest, valid, states, obs, inv, jac, capacity, devices):
-    records, variables, levels, channels = jac.shape
+            kept = total[0:features, :]
+            lane = lane_iota(kept.shape)
+            for r in range(group // 2):
+                kept = jnp.where(
+                    lane == g * group + h * (group // 2) + r, sums[r * features : (r + 1) * features, :], kept
+                )
+            total[0:features, :] = kept
+    lane = lane_iota((half, LANES))
+    low = jnp.where(lane < records, total[0:half, :], pltpu.roll(total[half:, :], records, 1)).astype(BF16)
+    for t in range(out_ref.shape[0]):
+        out_ref[t] = low
+
+
+def departures(dest, valid, states, obs, inv, jac, capacity, devices, tall):
+    records = dest.shape[0]
+    channels = jac.shape[1]
+    features = jac.shape[0] // records
     group = 16
-
-    def whole(shape):
-        return pl.BlockSpec(shape, lambda s: (0,) * len(shape))
-
+    vmem = pl.BlockSpec(memory_space=pltpu.VMEM)
     return pl.pallas_call(
-        functools.partial(departure_kernel, capacity),
-        grid=(records // group,),
-        in_specs=[
-            whole(dest.shape),
-            whole(valid.shape),
-            whole(states.shape),
-            whole(obs.shape),
-            whole(inv.shape),
-            pl.BlockSpec((group, variables, levels, channels), lambda s: (s, 0, 0, 0)),
+        functools.partial(departure_kernel, capacity, group),
+        in_specs=[vmem] * 5 + [pl.BlockSpec(memory_space=pl.ANY)],
+        out_shape=jax.ShapeDtypeStruct((devices, tall, 2 * records), BF16),
+        scratch_shapes=[
+            pltpu.VMEM(jac.shape, BF16),
+            pltpu.VMEM((2 * records, channels), BF16),
+            pltpu.VMEM((group // 2 * features, 2 * records), F32),
+            pltpu.VMEM((2 * tall, 2 * records), F32),
+            pltpu.SemaphoreType.DMA((records // group,)),
         ],
-        out_specs=whole((devices, levels, variables * records)),
-        out_shape=jax.ShapeDtypeStruct((devices, levels, variables * records), BF16),
-        scratch_shapes=[
-            pltpu.VMEM((variables, records, levels), BF16),
-            pltpu.VMEM((variables * records, channels), BF16),
-            pltpu.VMEM((levels, variables * records), F32),
-        ],
-        compiler_params=pltpu.CompilerParams(vmem_limit_bytes=VMEM_LIMIT),
+        compiler_params=pltpu.CompilerParams(vmem_limit_bytes=20 * 1024 * 1024),
         cost_estimate=pl.CostEstimate(
             flops=4 * jac.size, bytes_accessed=jac.size * 2, transcendentals=0
         ),
@@ -237,22 +251,19 @@
 
 
 def impact_kernel(records, products_ref, same_ref, out_ref, terms):
-    count, levels, width = products_ref.shape
+    count, tall, width = products_ref.shape
     listed = same_ref.shape[0]
-    tall = out_ref.shape[0]
-    variables = out_ref.shape[1] // listed
-    terms[...] = jnp.zeros_like(terms)
-    lane = lane_iota((levels, width))
-    for pair in range(count // variables):
+    lane = lane_iota((tall, width))
+    for pair in range(count // 2):
         one = products_ref[2 * pair].astype(F32)
         two = products_ref[2 * pair + 1].astype(F32)
         first = jnp.where(lane < records, one, pltpu.roll(two, records, 1))
         second = jnp.where(lane < records, pltpu.roll(one, records, 1), two)
-        terms[0, 0:levels, pair * width : (pair + 1) * width] = first.astype(BF16)
-        terms[1, 0:levels, pair * width : (pair + 1) * width] = second.astype(BF16)
-    for v in range(variables):
-        out_ref[:, v * listed : (v + 1) * listed] = lax.dot_general(
-            terms[v], same_ref[...], (((1,), (1,)), ((), ())), preferred_element_type=F32
+        terms[0, :, pair * width : (pair + 1) * width] = first.astype(BF16)
+        terms[1, :, pair * width : (pair + 1) * width] = second.astype(BF16)
+    for h in range(2):
+        out_ref[:, h * listed : (h + 1) * listed] = lax.dot_general(
+            terms[h], same_ref[...], (((1,), (1,)), ((), ())), preferred_element_type=F32
         ).astype(BF16)
 
 
@@ -332,7 +343,7 @@
         reach = lon_taps.shape[-1] // 2
         points = rows * cols
         span = records * lon_devices
-        tall = pl.cdiv(levels, 16) * 16
+        tall = pl.cdiv(features, 32) * 16
 
         dest = destination.reshape(records, 1)
         codes = destination.reshape(1, records) * points + column.reshape(1, records)
@@ -350,9 +361,10 @@
             found,
             observed.reshape(records, channels),
             inverse_var.reshape(records, channels),
-            jacobian.reshape(records, variables, levels, channels),
+            jnp.swapaxes(jacobian.reshape(records, variables, levels, channels), 1, 2).reshape(-1, channels),
             capacity,
             lon_devices,
+            tall,
         )
         products = lax.all_to_all(products, "lon", split_axis=0, concat_axis=0, tiled=True)
 
@@ -376,8 +388,8 @@
 
         impact = pl.pallas_call(
             functools.partial(impact_kernel, records),
-            out_shape=jax.ShapeDtypeStruct((tall, variables * listed), BF16),
-            scratch_shapes=[pltpu.VMEM((variables, tall, span), BF16)],
+            out_shape=jax.ShapeDtypeStruct((tall, 2 * listed), BF16),
+            scratch_shapes=[pltpu.VMEM((2, tall, span), BF16)],
             compiler_params=pltpu.CompilerParams(vmem_limit_bytes=16 * 1024 * 1024),
             name="impact_columns",
         )(products, same)
@@ -385,10 +397,12 @@
 
         mixing = jnp.stack(
             [
-                jnp.pad(vertical[v], ((0, tall - levels), (v * levels, wide - (v + 1) * levels)))
+                jnp.pad(vertical[v], ((0, 0), (v * levels, wide - (v + 1) * levels)))
                 for v in range(variables)
-            ]
-        )
+            ],
+            axis=1,
+        ).reshape(features, wide)
+        mixing = jnp.pad(mixing, ((0, 2 * tall - features), (0, 0))).reshape(2, tall, wide)
         lon_flat = jnp.pad(lon_taps.reshape(features, -1).T[::-1], ((0, 0), (0, wide - features)))
         taps = lon_flat.shape[0]
         lon_table = jnp.concatenate([jnp.pad(lon_flat, ((b, 16 - taps - b), (0, 0))) for b in range(8)])

time: 84.9 us -> 80.6 us (0.949)
  local copies, waits for them, and re-layouts: 12 us -> 10.3 us
  Pallas kernels: 29.6 us -> 28.1 us
    pallas_call x1, Pallas kernels: 7.56 us -> 4.5 us  [gather_state(): pl.pallas_call(functools.partial(gather_kernel, records, capacity, rows,...]
    pallas_call x2, Pallas kernels: 13.2 us -> 15.3 us  [filtered(): pl.pallas_call(kernel, grid=(steps,), in_specs=held, out_specs=pl.BlockSp...]
    unnamed x16 -> x15, local copies, waits for them, and re-layouts: 6.39 us -> 4.61 us
  transfers between devices with their start and end apart: 7 -> 7, of which waited for: 2 -> 3; matrix products, arithmetic and copies ran while one was open for 12% -> 6% of each run, Pallas kernels for 9% -> 10%
where the time goes in v3:
time: 80.6 us
  starting transfers between devices  28.9 us (36%)
  Pallas kernels  28.1 us (35%)
  waiting for transfers between devices  12.4 us (15%)
  local copies, waits for them, and re-layouts  10.3 us (13%)
    pallas_call x2, Pallas kernels, filtered(): pl.pallas_call(kernel, grid=(steps,), in_specs=held, out_specs=pl.BlockSp...  15.3 us
    pallas_call x1, Pallas kernels, departures(): pl.pallas_call(functools.partial(departure_kernel, capacity, group), in_s...  7.01 us
    all_to_all x1, starting transfers between devices, body(): lax.all_to_all(codes, 'lon', split_axis=0, concat_axis=0, tiled=True)  6.35 us
    all_to_all x1, waiting for transfers between devices, body(): lax.all_to_all(products, 'lon', split_axis=0, concat_axis=0, tiled=True)  6.31 us
    ppermute x1, starting transfers between devices, body(): lax.ppermute(impact, 'lat', up)  5.68 us
    all_to_all x1, waiting for transfers between devices, body(): lax.all_to_all(found, 'lon', split_axis=0, concat_axis=0, tiled=True)  5.41 us
    all_to_all x1, starting transfers between devices, body(): lax.all_to_all(found, 'lon', split_axis=0, concat_axis=0, tiled=True)  4.8 us
    unnamed x15, local copies, waits for them, and re-layouts  4.61 us
  transfers between devices with their start and end apart: 7, of which 3 were waited for; matrix products, arithmetic and copies ran while one was open for 6% of the time, Pallas kernels for 10%

profile of v3, /device:TPU:1, one launch (start us, length us, event | category | flops | bytes accessed | tf_op | source)
XLA Modules:
  0.0 80.6 jit_solution(8055165461401215717)
XLA Ops:
  0.0 0.0 copy-start.3
  0.0 0.0 copy-start.2
  0.0 0.7 bitcast_add_fusion
  0.7 0.6 broadcast_in_dim.2
  1.3 6.4 %all-to-all-start = ((s32[8,1,128]{2,1,0:T(1,128)}), s32[8,1,128]{2,1,0:T(1,128)S(1)}, u32[]{:S(2)}, u32[]{:S(2)}) async-start(s32[8,1,128]{2,1,0:T(1,128)} %broadcast_in_dim.2), calls=%async_computation | async-start | bytes 8192 | tf_op jit(solution)/shard_map/all_to_all | solution.py:351
  7.7 1.2 %fusion = (bf16[1,137,137]{2,0,1:T(2,128)(2,1)S(1)}, bf16[1,137,137]{2,0,1:T(2,128)(2,1)S(1)}) fusion(bf16[2,137,137]{2,0,1:T(2,128)(2,1)} %param.17), kind=kLoop, calls=%fused_computation.15 | loop fusion | bytes 150152 | tf_op jit(solution)/shard_map/slice | solution.py:400
  8.9 0.1 pad_bitcast_fusion
  9.0 0.8 %reshape.74 = f32[274,9]{0,1:T(8,128)S(1)} reshape(f32[2,137,9]{1,0,2:T(2,128)} %param.18) | data formatting | bytes 19728 | tf_op jit(solution)/shard_map/reshape | solution.py:406
  9.8 0.1 rev.3
  9.9 0.8 %reshape.75 = f32[274,9]{0,1:T(8,128)S(1)} reshape(f32[2,137,9]{1,0,2:T(2,128)} %param.19) | data formatting | bytes 19728 | tf_op jit(solution)/shard_map/reshape | solution.py:409
  10.8 0.7 copy.21.valid_ref
  11.5 0.7 copy.20.dest_ref
  12.2 0.7 all-to-all-done
  12.9 0.0 copy-start.1
  12.9 2.3 %copy-done.1 = f32[2,137,32,128]{3,2,1,0:T(8,128)S(1)} copy-done((f32[2,137,32,128]{3,2,1,0:T(8,128)S(1)}, f32[2,137,32,128]{3,2,1,0:T(8,128)}, u32[]{:S(2)}) %copy-start.1) | copy-done | bytes 4489240
  15.2 4.5 %gather_state.1 = bf16[128,384]{1,0:T(8,128)(2,1)} custom-call(s32[8,128]{1,0:T(8,128)S(1)} %bitcast.40, f32[8768,128]{1,0:T(8,128)S(1)} %bitcast.34), custom_call_target="tpu_custom_call" | custom-call | flops 287309824 | bytes 4489216 | tf_op jit(solution)/shard_map/gather_state/pallas_call | solution.py:82
  19.7 4.8 %all-to-all-start.1 = ((bf16[8,16,384]{2,1,0:T(8,128)(2,1)}), bf16[8,16,384]{2,1,0:T(8,128)(2,1)S(1)}, u32[]{:S(2)}, u32[]{:S(2)}) async-start(bf16[8,16,384]{2,1,0:T(8,128)(2,1)} %bitcast.6), calls=%async_computation.1 | async-start | bytes 196608 | tf_op jit(solution)/shard_map/all_to_all | solution.py:355
  24.5 0.2 copy.24
  24.7 0.3 reshape.72
  25.1 5.4 %all-to-all-done.1 = bf16[8,16,384]{2,1,0:T(8,128)(2,1)S(1)} async-done(((bf16[8,16,384]{2,1,0:T(8,128)(2,1)}), bf16[8,16,384]{2,1,0:T(8,128)(2,1)S(1)}, u32[]{:S(2)}, u32[]{:S(2)}) %all-to-all-start.1) | async-done | bytes 98336 | tf_op jit(solution)/shard_map/all_to_all | solution.py:355
  30.5 0.0 copy-done.3
  30.5 0.0 copy-done.2
  30.5 0.0 copy-start
  30.5 2.3 %copy-done = bf16[1,64,2,137,128]{4,2,3,1,0:T(2,128)(2,1)S(1)} copy-done((bf16[1,64,2,137,128]{4,2,3,1,0:T(2,128)(2,1)S(1)}, bf16[1,64,2,137,128]{4,2,3,1,0:T(2,128)(2,1)}, u32[]{:S(2)}) %copy-start) | copy-done | bytes 4489240
  32.7 7.0 %departures.1 = bf16[8,144,128]{2,1,0:T(8,128)(2,1)} custom-call(s32[64,1]{1,0:T(8,128)S(1)} %copy.20.dest_ref, s32[64,1]{1,0:T(8,128)S(1)} %copy.21.valid_ref, bf16[128,384]{1,0:T(8,128)(2,1)S(1)} %bitcast.37, bf16[64,128]{1,0:T(8,128)(2,1)S(1)} %bitcast.38, bf16[64,128]{1,0:T(8,128)(2,1)S(1)} %bitcast.39, bf16[17536,128]{1,0:T(8,128)(2,1)S(1)} %bitcast.33), custom_call_target="tpu_custom_call" | custom-call | flops 8978432 | bytes 4489216 | tf_op jit(solution)/shard_map/departures/pallas_call | solution.py:178
  39.8 3.4 %all-to-all-start.2 = ((bf16[8,144,128]{2,1,0:T(8,128)(2,1)}), bf16[8,144,128]{2,1,0:T(8,128)(2,1)S(1)}, u32[]{:S(2)}, u32[]{:S(2)}) async-start(bf16[8,144,128]{2,1,0:T(8,128)(2,1)} %departures.1), calls=%async_computation.2 | async-start | bytes 589824 | tf_op jit(solution)/shard_map/all_to_all | solution.py:369
  43.3 0.9 %plan_points.1 = (bf16[384,512]{1,0:T(8,128)(2,1)S(1)}, s32[1,512]{1,0:T(1,128)S(1)}) custom-call(s32[8,128]{1,0:T(8,128)S(1)} %bitcast.41), custom_call_target="tpu_custom_call" | custom-call | flops 2097152 | bytes 393216 | tf_op jit(solution)/shard_map/plan_points/pallas_call | solution.py:384
  44.2 6.3 %all-to-all-done.2.products_ref = bf16[8,144,128]{2,1,0:T(8,128)(2,1)S(1)} async-done(((bf16[8,144,128]{2,1,0:T(8,128)(2,1)}), bf16[8,144,128]{2,1,0:T(8,128)(2,1)S(1)}, u32[]{:S(2)}, u32[]{:S(2)}) %all-to-all-start.2) | async-done | bytes 294944 | tf_op jit(solution)/shard_map/all_to_all | solution.py:369
  50.5 0.4 impact_columns.1.refs_1_
  50.9 5.7 %collective-permute-start.3 = (bf16[144,768]{1,0:T(8,128)(2,1)S(1)}, bf16[144,768]{1,0:T(8,128)(2,1)S(1)}, u32[]{:S(2)}, u32[]{:S(2)}) collective-permute-start(bf16[144,768]{1,0:T(8,128)(2,1)S(1)} %impact_columns.1.refs_1_), channel_id=1, source_target_pairs={{1,0},{2,1},{3,2},{5,4},{6,5},{7,6},{9,8},{10,9},{11,10},{13,12},{... | collective-permute-start | bytes 663560 | tf_op jit(solution)/shard_map/ppermute | solution.py:396
  56.6 3.1 %collective-permute-start.1 = (bf16[144,768]{1,0:T(8,128)(2,1)S(1)}, bf16[144,768]{1,0:T(8,128)(2,1)S(1)}, u32[]{:S(2)}, u32[]{:S(2)}) collective-permute-start(bf16[144,768]{1,0:T(8,128)(2,1)S(1)} %impact_columns.1.refs_1_), channel_id=1, source_target_pairs={{0,1},{1,2},{2,3},{4,5},{5,6},{6,7},{8,9},{9,10},{10,11},{12,13},{... | collective-permute-start | bytes 663560 | tf_op jit(solution)/shard_map/ppermute | solution.py:396
  59.7 1.9 %collective-permute-start.2 = (s32[1,512]{1,0:T(1,128)S(1)}, s32[1,512]{1,0:T(1,128)S(1)}, u32[]{:S(2)}, u32[]{:S(2)}) collective-permute-start(s32[1,512]{1,0:T(1,128)S(1)} %get-tuple-element.7.refs_0_), channel_id=1, source_target_pairs={{1,0},{2,1},{3,2},{5,4},{6,5},{7,6},{9,8},{10,9},{11,10},{13,12},{... | collective-permute-start | bytes 6152 | tf_op jit(solution)/shard_map/ppermute | solution.py:387
  61.6 3.6 %collective-permute-start = (s32[1,512]{1,0:T(1,128)S(1)}, s32[1,512]{1,0:T(1,128)S(1)}, u32[]{:S(2)}, u32[]{:S(2)}) collective-permute-start(s32[1,512]{1,0:T(1,128)S(1)} %get-tuple-element.7.refs_0_), channel_id=1, source_target_pairs={{0,1},{1,2},{2,3},{4,5},{5,6},{6,7},{8,9},{9,10},{10,11},{12,13},{... | collective-permute-start | bytes 6152 | tf_op jit(solution)/shard_map/ppermute | solution.py:387
  65.3 7.4 %inner_rows.1.refs_9_ = f32[274,32,128]{2,1,0:T(8,128)} custom-call(s32[1,512]{1,0:T(1,128)S(1)} %get-tuple-element.7.refs_0_, bf16[144,768]{1,0:T(8,128)(2,1)S(1)} %impact_columns.1.refs_1_, bf16[2,144,384]{2,1,0:T(8,128)(2,1)S(1)} %bitcast.35, f32[128,384]{1,0:T(8,128)S(1)} %pad_dynamic-update-slice_fusion.refs_3_.refs_7_, f32[9,384]{1,0:T(8,128)S(1)} %pad.71.refs_4_.refs_8_), custom_call_target="tpu_custom_call" | custom-call | flops 44892160 | bytes 2244608 | tf_op jit(solution)/shard_map/inner_rows/pallas_call | solution.py:426
  72.6 0.0 collective-permute-done.2.refs_4_
  72.6 0.0 collective-permute-done.refs_2_
  72.6 0.0 collective-permute-done.3.refs_5_
  72.7 0.0 collective-permute-done.1.refs_3_
  72.7 7.9 %outer_rows.1 = f32[274,32,128]{2,1,0:T(8,128)} custom-call(s32[1,512]{1,0:T(1,128)S(1)} %get-tuple-element.7.refs_0_, bf16[144,768]{1,0:T(8,128)(2,1)S(1)} %impact_columns.1.refs_1_, s32[1,512]{1,0:T(1,128)S(1)} %collective-permute-done.refs_2_, bf16[144,768]{1,0:T(8,128)(2,1)S(1)} %collective-permute-done.1.refs_3_, ...), custom_call_target="tpu_custom_call", output_to_operand_aliasing={{}: (9, {})} | custom-call | flops 44892160 | bytes 2244608 | tf_op jit(solution)/shard_map/outer_rows/pallas_call | solution.py:426
  (15 shorter events, 0.2 us)
Async XLA Ops:
  0.0 30.5 %copy-start.3 = (bf16[1,64,128]{2,1,0:T(8,128)(2,1)S(1)}, bf16[1,64,128]{2,1,0:T(8,128)(2,1)}, u32[]{:S(2)}) copy-start(bf16[1,64,128]{2,1,0:T(8,128)(2,1)} %param.13) | copy-start | bytes 49156
  0.0 30.5 %copy-start.2 = (bf16[1,64,128]{2,1,0:T(8,128)(2,1)S(1)}, bf16[1,64,128]{2,1,0:T(8,128)(2,1)}, u32[]{:S(2)}) copy-start(bf16[1,64,128]{2,1,0:T(8,128)(2,1)} %param.12) | copy-start | bytes 49156
  1.3 11.6 %all-to-all-start = ((s32[8,1,128]{2,1,0:T(1,128)}), s32[8,1,128]{2,1,0:T(1,128)S(1)}, u32[]{:S(2)}, u32[]{:S(2)}) async-start(s32[8,1,128]{2,1,0:T(1,128)} %broadcast_in_dim.2), calls=%async_computation | async-start | bytes 8192 | tf_op jit(solution)/shard_map/all_to_all | solution.py:351
  12.9 2.3 %copy-start.1 = (f32[2,137,32,128]{3,2,1,0:T(8,128)S(1)}, f32[2,137,32,128]{3,2,1,0:T(8,128)}, u32[]{:S(2)}) copy-start(f32[2,137,32,128]{3,2,1,0:T(8,128)} %param.10) | copy-start | bytes 13467652
  19.7 10.8 %all-to-all-start.1 = ((bf16[8,16,384]{2,1,0:T(8,128)(2,1)}), bf16[8,16,384]{2,1,0:T(8,128)(2,1)S(1)}, u32[]{:S(2)}, u32[]{:S(2)}) async-start(bf16[8,16,384]{2,1,0:T(8,128)(2,1)} %bitcast.6), calls=%async_computation.1 | async-start | bytes 196608 | tf_op jit(solution)/shard_map/all_to_all | solution.py:355
  30.5 2.3 %copy-start = (bf16[1,64,2,137,128]{4,2,3,1,0:T(2,128)(2,1)S(1)}, bf16[1,64,2,137,128]{4,2,3,1,0:T(2,128)(2,1)}, u32[]{:S(2)}) copy-start(bf16[1,64,2,137,128]{4,2,3,1,0:T(2,128)(2,1)} %param.11) | copy-start | bytes 13467652
  39.8 10.7 %all-to-all-start.2 = ((bf16[8,144,128]{2,1,0:T(8,128)(2,1)}), bf16[8,144,128]{2,1,0:T(8,128)(2,1)S(1)}, u32[]{:S(2)}, u32[]{:S(2)}) async-start(bf16[8,144,128]{2,1,0:T(8,128)(2,1)} %departures.1), calls=%async_computation.2 | async-start | bytes 589824 | tf_op jit(solution)/shard_map/all_to_all | solution.py:369
  50.9 21.7 %collective-permute-start.3 = (bf16[144,768]{1,0:T(8,128)(2,1)S(1)}, bf16[144,768]{1,0:T(8,128)(2,1)S(1)}, u32[]{:S(2)}, u32[]{:S(2)}) collective-permute-start(bf16[144,768]{1,0:T(8,128)(2,1)S(1)} %impact_columns.1.refs_1_), channel_id=1, source_target_pairs={{1,0},{2,1},{3,2},{5,4},{6,5},{7,6},{9,8},{10,9},{11,10},{13,12},{... | collective-permute-start | bytes 663560 | tf_op jit(solution)/shard_map/ppermute | solution.py:396
  56.6 16.1 %collective-permute-start.1 = (bf16[144,768]{1,0:T(8,128)(2,1)S(1)}, bf16[144,768]{1,0:T(8,128)(2,1)S(1)}, u32[]{:S(2)}, u32[]{:S(2)}) collective-permute-start(bf16[144,768]{1,0:T(8,128)(2,1)S(1)} %impact_columns.1.refs_1_), channel_id=1, source_target_pairs={{0,1},{1,2},{2,3},{4,5},{5,6},{6,7},{8,9},{9,10},{10,11},{12,13},{... | collective-permute-start | bytes 663560 | tf_op jit(solution)/shard_map/ppermute | solution.py:396
  59.7 13.0 %collective-permute-start.2 = (s32[1,512]{1,0:T(1,128)S(1)}, s32[1,512]{1,0:T(1,128)S(1)}, u32[]{:S(2)}, u32[]{:S(2)}) collective-permute-start(s32[1,512]{1,0:T(1,128)S(1)} %get-tuple-element.7.refs_0_), channel_id=1, source_target_pairs={{1,0},{2,1},{3,2},{5,4},{6,5},{7,6},{9,8},{10,9},{11,10},{13,12},{... | collective-permute-start | bytes 6152 | tf_op jit(solution)/shard_map/ppermute | solution.py:387
  61.6 11.0 %collective-permute-start = (s32[1,512]{1,0:T(1,128)S(1)}, s32[1,512]{1,0:T(1,128)S(1)}, u32[]{:S(2)}, u32[]{:S(2)}) collective-permute-start(s32[1,512]{1,0:T(1,128)S(1)} %get-tuple-element.7.refs_0_), channel_id=1, source_target_pairs={{0,1},{1,2},{2,3},{4,5},{5,6},{6,7},{8,9},{9,10},{10,11},{12,13},{... | collective-permute-start | bytes 6152 | tf_op jit(solution)/shard_map/ppermute | solution.py:387

commit v4 on v3

--- a/solution.py
+++ b/solution.py
@@ -31,138 +31,187 @@
     return tile, flipped - tile * points
 
 
-def gather_kernel(records, capacity, rows, levels, chunk, codes_ref, state_ref, out_ref, state, held, arrived):
-    count = codes_ref.shape[0]
-    slots = out_ref.shape[0]
+def lay_state_kernel(rows, levels, chunk, state_ref, out_ref, state, arrived):
     variables = state_ref.shape[0] // (rows * levels)
+    half = rows // 2
     parts = []
     for first in range(0, levels, chunk):
         size = min(chunk, levels - first)
         for v in range(variables):
-            here = pl.ds((v * levels + first) * rows, size * rows)
+            start = (v * levels + first) * rows
+            here = pl.ds(start, size * rows)
             copy = pltpu.make_async_copy(state_ref.at[here], state.at[here], arrived.at[len(parts)])
             copy.start()
-            parts.append((v, first, size, here, copy))
-
-    held[...] = jnp.zeros_like(held)
+            parts.append((v, first, size, start, copy))
+    for v, first, size, start, copy in parts:
+        copy.wait()
+        for odd in range(2):
+            some = state[pl.ds(start + odd, size * half, stride=2), :].astype(BF16)
+            out_ref[first : first + size, v * half : (v + 1) * half, odd * LANES : (odd + 1) * LANES] = some.reshape(
+                size, half, LANES
+            )
+
+
+def lay_state(state):
+    variables, levels, rows, cols = state.shape
+    chunk = 72
+    return pl.pallas_call(
+        functools.partial(lay_state_kernel, rows, levels, chunk),
+        in_specs=[pl.BlockSpec(memory_space=pl.ANY)],
+        out_shape=jax.ShapeDtypeStruct((levels, variables * rows // 2, 2 * cols), BF16),
+        scratch_shapes=[
+            pltpu.VMEM((variables * levels * rows, cols), F32),
+            pltpu.SemaphoreType.DMA((variables * pl.cdiv(levels, chunk),)),
+        ],
+        compiler_params=pltpu.CompilerParams(vmem_limit_bytes=24 * 1024 * 1024),
+        cost_estimate=pl.CostEstimate(flops=0, bytes_accessed=state.size * 6, transcendentals=0),
+        name="lay_state",
+    )(state.reshape(variables * levels * rows, cols))
+
+
+def gather_kernel(records, capacity, rows, codes_ref, state_ref, out_ref, held):
+    count = codes_ref.shape[0]
+    slots = out_ref.shape[0]
+    half = rows // 2
+    features = state_ref.shape[0] // half
     me = lax.axis_index("lon")
     tile, column = split_codes(codes_ref, records, rows * LANES)
     mine = (tile == me).astype(F32)
     rank = jnp.dot(earlier_rows(records), mine.astype(BF16), preferred_element_type=F32)
     slot = lane_iota(mine.shape) * capacity + rank.astype(jnp.int32)
     slot = jnp.where(tile == me, slot, -1)
-    row_of = jnp.zeros((1, slots), F32)
-    lon_of = jnp.zeros((1, slots), F32)
+    place = jnp.zeros((records, slots), F32)
     for d in range(count):
         hit = slot[:, d : d + 1] == lane_iota((records, slots))
-        row = lax.div(column[:, d : d + 1], LANES)
-        lon = column[:, d : d + 1] - row * LANES
-        row_of += jnp.sum(jnp.where(hit, (row + 1).astype(F32), 0.0), axis=0, keepdims=True)
-        lon_of += jnp.sum(jnp.where(hit, lon.astype(F32), 0.0), axis=0, keepdims=True)
-    pick = (row_iota((LANES, slots)) == lon_of.astype(jnp.int32)).astype(F32).astype(BF16)
-    row_mask = (row_iota((rows, slots)) == row_of.astype(jnp.int32) - 1).astype(F32)
-
-    for v, first, size, here, copy in parts:
-        copy.wait()
-        found = jnp.dot(state[here, :].astype(BF16), pick, preferred_element_type=F32)
-        found = found.reshape(size, rows, slots) * row_mask[None]
-        held[pl.ds(variables * first + v, size, stride=variables), :] = jnp.sum(found, axis=1)
+        place += jnp.where(hit, (column[:, d : d + 1] + 1).astype(F32), 0.0)
+    place = jnp.sum(place, axis=0, keepdims=True).astype(jnp.int32) - 1
+    row = lax.shift_right_arithmetic(place, LANES.bit_length() - 1)
+    in_pair = jnp.where(place < 0, -1, jnp.bitwise_and(place, 2 * LANES - 1))
+    pick = (row_iota((2 * LANES, slots)) == in_pair).astype(F32).astype(BF16)
+    mask = (row_iota((half, slots)) == lax.shift_right_arithmetic(row, 1)).astype(F32)
+
+    held[...] = jnp.zeros_like(held)
+    chunk = 72
+    for first in range(0, features, chunk):
+        size = min(chunk, features - first)
+        found = jnp.dot(
+            state_ref[first * half : (first + size) * half, :], pick, preferred_element_type=F32
+        )
+        found = found.reshape(size, half, slots) * mask[None]
+        held[first : first + size, :] = jnp.sum(found, axis=1)
     for t in range(out_ref.shape[1] // LANES):
         out_ref[:, t * LANES : (t + 1) * LANES] = jnp.transpose(
             held[t * LANES : (t + 1) * LANES, :]
         ).astype(BF16)
 
 
-def gather_state(codes, state, records, capacity):
-    variables, levels, rows, cols = state.shape
-    features = variables * levels
+def gather_state(codes, laid, records, capacity, rows):
+    features = laid.shape[0] * laid.shape[1] * 2 // rows
     wide = pl.cdiv(features, LANES) * LANES
     slots = codes.shape[0] * capacity
-    chunk = 32
+    vmem = pl.BlockSpec(memory_space=pltpu.VMEM)
     return pl.pallas_call(
-        functools.partial(gather_kernel, records, capacity, rows, levels, chunk),
-        in_specs=[pl.BlockSpec(memory_space=pltpu.VMEM), pl.BlockSpec(memory_space=pl.ANY)],
+        functools.partial(gather_kernel, records, capacity, rows),
+        in_specs=[vmem, vmem],
         out_shape=jax.ShapeDtypeStruct((slots, wide), BF16),
-        scratch_shapes=[
-            pltpu.VMEM((features * rows, cols), F32),
-            pltpu.VMEM((wide, slots), F32),
-            pltpu.SemaphoreType.DMA((variables * pl.cdiv(levels, chunk),)),
-        ],
-        compiler_params=pltpu.CompilerParams(vmem_limit_bytes=20 * 1024 * 1024),
-        cost_estimate=pl.CostEstimate(
-            flops=2 * features * rows * cols * slots, bytes_accessed=features * rows * cols * 4, transcendentals=0
-        ),
+        scratch_shapes=[pltpu.VMEM((wide, slots), F32)],
+        compiler_params=pltpu.CompilerParams(vmem_limit_bytes=12 * 1024 * 1024),
+        cost_estimate=pl.CostEstimate(flops=2 * laid.size * slots, bytes_accessed=laid.size * 2, transcendentals=0),
         name="gather_state",
-    )(codes, state.reshape(features * rows, cols))
-
-
-def departure_kernel(capacity, group, dest_ref, valid_ref, states_ref, obs_ref, inv_ref, jac_ref, out_ref, jac, scaled_rows, sums, total, arrived):
-    records = dest_ref.shape[0]
+    )(codes, laid.reshape(-1, laid.shape[2]))
+
+
+def fetch_kernel(from_ref, after_ref, out_ref, arrived):
+    copy = pltpu.make_async_copy(from_ref, out_ref, arrived)
+    copy.start()
+    copy.wait()
+
+
+def fetch(array, after):
+    anywhere = pl.BlockSpec(memory_space=pl.ANY)
+    return pl.pallas_call(
+        fetch_kernel,
+        in_specs=[anywhere, anywhere],
+        out_specs=pl.BlockSpec(memory_space=pltpu.VMEM),
+        out_shape=jax.ShapeDtypeStruct(array.shape, array.dtype),
+        scratch_shapes=[pltpu.SemaphoreType.DMA],
+        compiler_params=pltpu.CompilerParams(vmem_limit_bytes=12 * 1024 * 1024),
+        cost_estimate=pl.CostEstimate(flops=0, bytes_accessed=array.size * 4, transcendentals=0),
+        name="fetch_jacobian",
+    )(array, after)
+
+
+def to_column(row):
+    size = row.shape[1]
+    wide = jnp.broadcast_to(row, (size, size))
+    return jnp.sum(jnp.where(row_iota(wide.shape) == lane_iota(wide.shape), wide, 0), axis=1, keepdims=True)
+
+
+def departure_kernel(capacity, group, dest_ref, valid_ref, states_ref, obs_ref, inv_ref, jac_ref, out_ref, total):
+    records = dest_ref.shape[1]
     slots = states_ref.shape[0]
     channels = jac_ref.shape[1]
     features = jac_ref.shape[0] // records
-    span = group * features
-    copies = []
-    for g in range(records // group):
-        here = pl.ds(g * span, span)
-        copies.append(pltpu.make_async_copy(jac_ref.at[here], jac.at[here], arrived.at[g]))
-        copies[g].start()
-
-    dest = dest_ref[...]
+    part = group // 2
+    span = part * features
+
+    dest = to_column(dest_ref[...])
     named = (dest == lane_iota((records, LANES))).astype(F32)
     before = jnp.dot(earlier_rows(records), named.astype(BF16), preferred_element_type=F32)
     rank = jnp.sum(before * named, axis=1, keepdims=True).astype(jnp.int32)
     chosen = (dest * capacity + rank == lane_iota((records, slots))).astype(F32).astype(BF16)
     columns = jnp.dot(chosen, states_ref[...], preferred_element_type=F32)
-    alive = lane_iota((records, channels)) < valid_ref[...]
+    alive = lane_iota((records, channels)) < to_column(valid_ref[...])
     weight = jnp.where(alive, inv_ref[...].astype(F32), 0.0)
-    scaled_rows[...] = jnp.zeros_like(scaled_rows)
-    total[...] = jnp.zeros_like(total)
 
     tiles, skip = divmod(features, LANES)
     wide = columns.shape[1]
-    reach = pl.cdiv(skip * (group - 1) + features, LANES)
+    reach = pl.cdiv(skip * (part - 1) + features, LANES)
+    tall = total.shape[0]
+    total[...] = jnp.zeros_like(total)
     row = row_iota((group, LANES))
-    half = total.shape[0] // 2
+    index = jnp.bitwise_and(row, part - 1)
     for g in range(records // group):
+        first = g * group * features
         mine = columns[g * group : (g + 1) * group]
-        mine = jnp.concatenate([mine, jnp.zeros((group, reach * LANES - wide), F32)], axis=1)
+        if reach * LANES > wide:
+            mine = jnp.concatenate([mine, jnp.zeros((group, reach * LANES - wide), F32)], axis=1)
         bit = 1
-        while bit < group:
+        while bit < part:
             moved = pltpu.roll(mine, skip * bit, 1)
             mine = jnp.where(jnp.bitwise_and(row_iota(mine.shape), bit) > 0, moved, mine)
             bit *= 2
         spread = []
         for t in range(pl.cdiv(span, LANES)):
             piece = jnp.zeros((group, LANES), F32)
-            for r in range(group):
+            for r in range(part):
                 at = t - tiles * r
                 if 0 <= at < reach:
-                    piece = jnp.where(row == r, mine[:, at * LANES : (at + 1) * LANES], piece)
+                    piece = jnp.where(index == r, mine[:, at * LANES : (at + 1) * LANES], piece)
             spread.append(piece.astype(BF16))
         spread = jnp.concatenate(spread, axis=1)[:, :span]
-        copies[g].wait()
-        here = slice(g * span, (g + 1) * span)
-        model = jnp.dot(spread, jac[here, :], preferred_element_type=F32)
+        pair = jnp.concatenate([jac_ref[first : first + span, :], jac_ref[first + span : first + 2 * span, :]], axis=1)
+        both = jnp.dot(spread, pair, preferred_element_type=F32)
+        model = jnp.where(row < part, both[:, :channels], both[:, channels:])
         own = slice(g * group, (g + 1) * group)
         misfit = weight[own] * (model - obs_ref[own, :].astype(F32))
-        scaled_rows[own, :] = misfit.astype(BF16)
-        against = scaled_rows[...]
-        for h in range(2):
-            part = span // 2
-            sums[...] = lax.dot_general(
-                jac[g * span + h * part : g * span + (h + 1) * part, :],
-                against,
+        low = misfit.astype(BF16).astype(F32)
+        for r in range(part):
+            against = jnp.concatenate([jnp.where(row == r, low, 0.0), jnp.where(row == r + part, low, 0.0)], axis=1)
+            start = first + r * features
+            lead = start % 16
+            size = pl.cdiv(features + lead, 16) * 16
+            rows = [jac_ref[start - lead + h * span : start - lead + h * span + size, :] for h in range(2)]
+            one = lax.dot_general(
+                jnp.concatenate(rows, axis=1),
+                against.astype(BF16),
                 (((1,), (1,)), ((), ())),
                 preferred_element_type=F32,
             )
-            kept = total[0:features, :]
-            lane = lane_iota(kept.shape)
-            for r in range(group // 2):
-                kept = jnp.where(
-                    lane == g * group + h * (group // 2) + r, sums[r * features : (r + 1) * features, :], kept
-                )
-            total[0:features, :] = kept
+            one = one[lead : lead + features]
+            sums = one if r == 0 else sums + one
+        total[0:features, g * group : (g + 1) * group] = sums
+    half = tall // 2
     lane = lane_iota((half, LANES))
     low = jnp.where(lane < records, total[0:half, :], pltpu.roll(total[half:, :], records, 1)).astype(BF16)
     for t in range(out_ref.shape[0]):
@@ -170,22 +219,13 @@
 
 
 def departures(dest, valid, states, obs, inv, jac, capacity, devices, tall):
-    records = dest.shape[0]
-    channels = jac.shape[1]
-    features = jac.shape[0] // records
-    group = 16
+    records, channels = obs.shape
     vmem = pl.BlockSpec(memory_space=pltpu.VMEM)
     return pl.pallas_call(
-        functools.partial(departure_kernel, capacity, group),
-        in_specs=[vmem] * 5 + [pl.BlockSpec(memory_space=pl.ANY)],
+        functools.partial(departure_kernel, capacity, 16),
+        in_specs=[vmem] * 6,
         out_shape=jax.ShapeDtypeStruct((devices, tall, 2 * records), BF16),
-        scratch_shapes=[
-            pltpu.VMEM(jac.shape, BF16),
-            pltpu.VMEM((2 * records, channels), BF16),
-            pltpu.VMEM((group // 2 * features, 2 * records), F32),
-            pltpu.VMEM((2 * tall, 2 * records), F32),
-            pltpu.SemaphoreType.DMA((records // group,)),
-        ],
+        scratch_shapes=[pltpu.VMEM((2 * tall, 2 * records), F32)],
         compiler_params=pltpu.CompilerParams(vmem_limit_bytes=20 * 1024 * 1024),
         cost_estimate=pl.CostEstimate(
             flops=4 * jac.size, bytes_accessed=jac.size * 2, transcendentals=0
@@ -209,7 +249,7 @@
     return jnp.where(key == NOWHERE, NOWHERE, key + row * STRIDE)
 
 
-def plan_kernel(records, points, reach, codes_ref, same_ref, info_ref, down, first):
+def plan_kernel(records, points, reach, codes_ref, vertical_ref, lon_ref, lat_ref, after_ref, same_ref, info_ref, mixing_ref, table_ref, taps_ref, down, first):
     count = codes_ref.shape[0]
     span, listed = count * records, same_ref.shape[0]
     tile, column = split_codes(codes_ref, records, points)
@@ -249,8 +289,27 @@
     starts = jnp.where(down[...] < lane_iota((span, LANES)) * STRIDE, first[...], 0.0)
     info_ref[0:1, listed:] = jnp.sum(starts, axis=0, keepdims=True).astype(jnp.int32)
 
-
-def impact_kernel(records, products_ref, same_ref, out_ref, terms):
+    features, levels = vertical_ref.shape
+    wide = mixing_ref.shape[2]
+    tall = mixing_ref.shape[1]
+    variables = features // levels
+    mixing_ref[...] = jnp.zeros_like(mixing_ref)
+    rows = jnp.concatenate([vertical_ref[...].astype(F32), jnp.zeros((features, wide - levels), F32)], axis=1)
+    spread = rows
+    for v in range(1, variables):
+        spread = jnp.where(row_iota(rows.shape) % variables == v, pltpu.roll(rows, v * levels, 1), spread)
+    mixing_ref[0] = spread[:tall].astype(BF16)
+    mixing_ref[1, 0 : features - tall, :] = spread[tall:].astype(BF16)
+    taps = lon_ref.shape[0]
+    spare = jnp.zeros((taps, wide - features), F32)
+    lon = jnp.concatenate([lon_ref[...], spare], axis=1)
+    lon = jnp.concatenate([lon[k : k + 1] for k in reversed(range(taps))] + [jnp.zeros((16 - taps, wide), F32)], axis=0)
+    for b in range(8):
+        table_ref[16 * b : 16 * (b + 1), :] = pltpu.roll(lon, b, 0) if b else lon
+    taps_ref[...] = jnp.concatenate([lat_ref[...], spare], axis=1)
+
+
+def impact_kernel(records, products_ref, same_ref, near_ref, far_ref, out_ref, terms):
     count, tall, width = products_ref.shape
     listed = same_ref.shape[0]
     lane = lane_iota((tall, width))
@@ -294,7 +353,10 @@
 
     along[...] = jnp.zeros_like(along)
     for n, (info, _) in enumerate(lists):
-        offset = (0, -rows, rows)[n] - base
+        offset = -base
+        if n:
+            side = 1 - 2 * lax.rem(lax.axis_index("lat"), 2)
+            offset += (rows if n == 1 else -rows) * side
         low = jnp.clip(-offset, 0, rows)
         high = jnp.clip(window - offset, 0, rows)
 
@@ -315,7 +377,7 @@
         here = slice(t * LANES, (t + 1) * LANES)
         lat = [jnp.broadcast_to(lat_ref[k : k + 1, here], (8, LANES)) for k in range(2 * reach + 1)]
 
-        @pl.loop(0, LANES // 8, unroll=2)
+        @pl.loop(0, LANES // 8, unroll=LANES // 8)
         def _(j):
             sums = [None] * height
             for w in range(window):
@@ -345,68 +407,70 @@
         span = records * lon_devices
         tall = pl.cdiv(features, 32) * 16
 
-        dest = destination.reshape(records, 1)
         codes = destination.reshape(1, records) * points + column.reshape(1, records)
         codes = jnp.broadcast_to(jnp.pad(codes, ((0, 0), (0, LANES - records))), (lon_devices, LANES))
         codes = lax.all_to_all(codes, "lon", split_axis=0, concat_axis=0, tiled=True)
-
-        found = gather_state(codes, state_field, records, capacity)
-        found = found.reshape(lon_devices, capacity, found.shape[-1])
-        found = lax.all_to_all(found, "lon", split_axis=0, concat_axis=0, tiled=True)
-        found = found.reshape(lon_devices * capacity, found.shape[-1])
-
+        laid = lay_state(state_field)
+
+        found = gather_state(codes, laid, records, capacity, rows)
+        found_in = lax.all_to_all(
+            found.reshape(lon_devices, capacity, found.shape[-1]), "lon", split_axis=0, concat_axis=0, tiled=True
+        )
+        own = jnp.swapaxes(jacobian.reshape(records, variables, levels, channels), 1, 2).reshape(-1, channels)
         products = departures(
-            dest,
-            valid_count.reshape(records, 1),
-            found,
+            destination.reshape(1, records),
+            valid_count.reshape(1, records),
+            found_in.reshape(lon_devices * capacity, found.shape[-1]),
             observed.reshape(records, channels),
             inverse_var.reshape(records, channels),
-            jnp.swapaxes(jacobian.reshape(records, variables, levels, channels), 1, 2).reshape(-1, channels),
+            fetch(own, found),
             capacity,
             lon_devices,
             tall,
         )
-        products = lax.all_to_all(products, "lon", split_axis=0, concat_axis=0, tiled=True)
+        products_in = lax.all_to_all(products, "lon", split_axis=0, concat_axis=0, tiled=True)
 
         listed = 3 * lon_devices * capacity
         wide = pl.cdiv(features, LANES) * LANES
-        plan = pl.pallas_call(
+        taps = lon_taps.shape[-1]
+        vmem, anywhere = pl.BlockSpec(memory_space=pltpu.VMEM), pl.BlockSpec(memory_space=pl.ANY)
+        same, info, mixing, lon_table, lat_flat = pl.pallas_call(
             functools.partial(plan_kernel, records, points, reach),
+            in_specs=[vmem] * 4 + [anywhere],
             out_shape=(
                 jax.ShapeDtypeStruct((listed, span), BF16),
                 jax.ShapeDtypeStruct((1, listed + LANES), jnp.int32),
+                jax.ShapeDtypeStruct((2, tall, wide), BF16),
+                jax.ShapeDtypeStruct((8 * 16, wide), F32),
+                jax.ShapeDtypeStruct((taps, wide), F32),
             ),
             scratch_shapes=[pltpu.VMEM((span, LANES), jnp.int32), pltpu.VMEM((span, LANES), F32)],
             compiler_params=pltpu.CompilerParams(vmem_limit_bytes=16 * 1024 * 1024),
             cost_estimate=pl.CostEstimate(flops=8 * span * span, bytes_accessed=span * listed * 2, transcendentals=0),
             name="plan_points",
+        )(
+            codes,
+            jnp.swapaxes(vertical, 0, 1).reshape(features, levels),
+            jnp.moveaxis(lon_taps, 2, 0).reshape(taps, features),
+            jnp.moveaxis(lat_taps, 2, 0).reshape(taps, features),
+            found,
         )
-        same, info = plan(codes)
-        down = [(i, i + 1) for i in range(lat_devices - 1)]
-        up = [(i + 1, i) for i in range(lat_devices - 1)]
-        info_above, info_below = lax.ppermute(info, "lat", down), lax.ppermute(info, "lat", up)
+        pairs = [(i, i + 1) for i in range(0, lat_devices - 1, 2)]
+        between = [(i, i + 1) for i in range(1, lat_devices - 1, 2)]
+        swaps = [[(a, b) for a, b in some] + [(b, a) for a, b in some] for some in (pairs, between)]
+        info_far = lax.ppermute(info, "lat", swaps[1])
+        info_near = lax.ppermute(info, "lat", swaps[0])
 
         impact = pl.pallas_call(
             functools.partial(impact_kernel, records),
+            in_specs=[vmem] * 2 + [anywhere] * 2,
             out_shape=jax.ShapeDtypeStruct((tall, 2 * listed), BF16),
             scratch_shapes=[pltpu.VMEM((2, tall, span), BF16)],
             compiler_params=pltpu.CompilerParams(vmem_limit_bytes=16 * 1024 * 1024),
             name="impact_columns",
-        )(products, same)
-        above, below = lax.ppermute(impact, "lat", down), lax.ppermute(impact, "lat", up)
-
-        mixing = jnp.stack(
-            [
-                jnp.pad(vertical[v], ((0, 0), (v * levels, wide - (v + 1) * levels)))
-                for v in range(variables)
-            ],
-            axis=1,
-        ).reshape(features, wide)
-        mixing = jnp.pad(mixing, ((0, 2 * tall - features), (0, 0))).reshape(2, tall, wide)
-        lon_flat = jnp.pad(lon_taps.reshape(features, -1).T[::-1], ((0, 0), (0, wide - features)))
-        taps = lon_flat.shape[0]
-        lon_table = jnp.concatenate([jnp.pad(lon_flat, ((b, 16 - taps - b), (0, 0))) for b in range(8)])
-        lat_flat = jnp.pad(lat_taps.reshape(features, -1).T, ((0, 0), (0, wide - features)))
+        )(products_in, same, info_near, info_far)
+        impact_far = lax.ppermute(impact, "lat", swaps[1])
+        impact_near = lax.ppermute(impact, "lat", swaps[0])
 
         height = 8
         blocks = rows // height
@@ -444,7 +508,7 @@
 
         inner = filtered([info, impact], blocks - 2, lambda s: s + 1, None, "inner_rows")
         result = filtered(
-            [info, impact, info_above, above, info_below, below],
+            [info, impact, info_near, impact_near, info_far, impact_far],
             2,
             lambda s: s * (blocks - 1),
             inner,

time: 80.6 us -> 61.4 us (0.76); the launches traced: 80.6 us -> 60.4 us
  Pallas kernels: 28.1 us -> 19.9 us
  waiting for transfers between devices: 12.4 us -> 4.63 us
  starting transfers between devices: 28.9 us -> 25.1 us
    all_to_all x1, waiting for transfers between devices: 6.31 us -> 0.01 us  [body(): lax.all_to_all(products, 'lon', split_axis=0, concat_axis=0, tiled=True)]
    pallas_call x2, Pallas kernels: 15.3 us -> 10.7 us  [filtered(): pl.pallas_call(kernel, grid=(steps,), in_specs=held, out_specs=pl.BlockSp...]
    unnamed x15 -> x22, local copies, waits for them, and re-layouts: 4.61 us -> 8.94 us
    all_to_all x1, waiting for transfers between devices: 5.41 us -> 1.28 us  [body(): lax.all_to_all(found.reshape(lon_devices, capacity, found.shape[-1]), 'lo...]
    pallas_call x4 -> x6, Pallas kernels: 12.8 us -> 9.17 us  [the longest x1 4.33 us: departures(): pl.pallas_call(functools.partial(departure_kernel, capacity, 16), in_spec...]
    ppermute x4, starting transfers between devices: 14.3 us -> 11 us  [the longest x1 5.45 us: body(): impact_far = lax.ppermute(impact, 'lat', swaps[1])]
    reshape x5 -> x3, local copies, waits for them, and re-layouts: 3.42 us -> 0.38 us  [the longest x1 0.21 us: body(): jnp.swapaxes(vertical, 0, 1).reshape(features, levels)]
    ppermute x4, waiting for transfers between devices: 0.01 us -> 1.48 us  [the longest x1 1.47 us: body(): info_far = lax.ppermute(info, 'lat', swaps[1])]
  transfers between devices with their start and end apart: 7 -> 7, of which waited for: 3 -> 3; matrix products, arithmetic and copies ran while one was open for 6% -> 1% of each run, Pallas kernels for 10% -> 13%
where the time goes in v4:
time: 61.4 us; the launch traced here: 60.4 us
  starting transfers between devices  25.1 us (41%)
  Pallas kernels  19.9 us (32%)
  local copies, waits for them, and re-layouts  9.92 us (16%)
  waiting for transfers between devices  4.63 us (8%)
  other arithmetic  0.67 us (1%)
    pallas_call x2, Pallas kernels, filtered(): pl.pallas_call(kernel, grid=(steps,), in_specs=held, out_specs=pl.BlockSp...  10.7 us
    unnamed x22, local copies, waits for them, and re-layouts  8.94 us
    all_to_all x1, starting transfers between devices, body(): lax.all_to_all(codes, 'lon', split_axis=0, concat_axis=0, tiled=True)  6.35 us
    ppermute x1, starting transfers between devices, body(): impact_far = lax.ppermute(impact, 'lat', swaps[1])  5.45 us
    ppermute x1, starting transfers between devices, body(): info_far = lax.ppermute(info, 'lat', swaps[1])  5.4 us
    pallas_call x1, Pallas kernels, departures(): pl.pallas_call(functools.partial(departure_kernel, capacity, 16), in_spec...  4.33 us
    all_to_all x1, starting transfers between devices, body(): lax.all_to_all(products, 'lon', split_axis=0, concat_axis=0, tiled=True)  4.17 us
    all_to_all x1, starting transfers between devices, body(): lax.all_to_all(found.reshape(lon_devices, capacity, found.shape[-1]), 'lo...  3.58 us
  transfers between devices with their start and end apart: 7, of which 3 were waited for; matrix products, arithmetic and copies ran while one was open for 1% of the time, Pallas kernels for 13%

profile of v4, /device:TPU:1, one launch (start us, length us, event | category | flops | bytes accessed | tf_op | source)
XLA Modules:
  0.0 60.4 jit_solution(4267491108583405193)
XLA Ops:
  0.0 0.7 %multiply_add_fusion = s32[1,64]{1,0:T(1,128)S(1)} fusion(s32[1,64]{1,0:T(1,128)} %param.16, s32[1,64,1]{1,2,0:T(1,128)} %param.15), kind=kLoop, calls=%fused_computation.1 | loop fusion | flops 128 | bytes 768 | tf_op jit(solution)/shard_map/add | solution.py:410
  0.7 0.6 broadcast_in_dim.2
  1.3 6.4 %all-to-all-start = ((s32[8,1,128]{2,1,0:T(1,128)}), s32[8,1,128]{2,1,0:T(1,128)S(1)}, u32[]{:S(2)}, u32[]{:S(2)}) async-start(s32[8,1,128]{2,1,0:T(1,128)} %broadcast_in_dim.2), calls=%async_computation | async-start | bytes 8192 | tf_op jit(solution)/shard_map/all_to_all | solution.py:412
  7.6 0.0 copy-start.2
  7.6 2.3 %copy-done.2 = f32[2,137,32,128]{3,2,1,0:T(8,128)S(1)} copy-done((f32[2,137,32,128]{3,2,1,0:T(8,128)S(1)}, f32[2,137,32,128]{3,2,1,0:T(8,128)}, u32[]{:S(2)}) %copy-start.2) | copy-done | bytes 4489240
  9.9 1.1 %lay_state.1 = bf16[137,32,256]{2,1,0:T(8,128)(2,1)S(1)} custom-call(f32[8768,128]{1,0:T(8,128)S(1)} %bitcast.21), custom_call_target="tpu_custom_call" | custom-call | bytes 6733824 | tf_op jit(solution)/shard_map/lay_state/pallas_call | solution.py:58
  11.0 1.9 %all-to-all-done = s32[8,1,128]{2,1,0:T(1,128)S(1)} async-done(((s32[8,1,128]{2,1,0:T(1,128)}), s32[8,1,128]{2,1,0:T(1,128)S(1)}, u32[]{:S(2)}, u32[]{:S(2)}) %all-to-all-start) | async-done | bytes 4128 | tf_op jit(solution)/shard_map/all_to_all | solution.py:412
  12.9 1.9 %gather_state.1.after_ref = bf16[128,384]{1,0:T(8,128)(2,1)} custom-call(s32[8,128]{1,0:T(8,128)S(1)} %bitcast.24, bf16[4384,256]{1,0:T(8,128)(2,1)S(1)} %bitcast.20), custom_call_target="tpu_custom_call" | custom-call | flops 287309824 | bytes 2244608 | tf_op jit(solution)/shard_map/gather_state/pallas_call | solution.py:113
  14.8 3.6 %all-to-all-start.1 = ((bf16[8,16,384]{2,1,0:T(8,128)(2,1)}), bf16[8,16,384]{2,1,0:T(8,128)(2,1)S(1)}, u32[]{:S(2)}, u32[]{:S(2)}) async-start(bf16[8,16,384]{2,1,0:T(8,128)(2,1)} %bitcast.8), calls=%async_computation.1 | async-start | bytes 196608 | tf_op jit(solution)/shard_map/all_to_all | solution.py:416
  18.4 0.0 copy-start.3
  18.4 2.3 %copy-done.3 = bf16[1,64,2,137,128]{4,2,3,1,0:T(2,128)(2,1)S(1)} copy-done((bf16[1,64,2,137,128]{4,2,3,1,0:T(2,128)(2,1)S(1)}, bf16[1,64,2,137,128]{4,2,3,1,0:T(2,128)(2,1)}, u32[]{:S(2)}) %copy-start.3) | copy-done | bytes 4489240
  20.6 0.0 copy-start.4
  20.6 0.0 copy-start.5
  20.6 0.0 copy-start.6
  20.7 0.0 copy-start.9
  20.7 0.0 copy-start.10
  20.7 0.0 copy-start.8
  20.7 0.4 fetch_jacobian.1.jac_ref
  21.1 0.0 copy-start
  21.1 2.1 %copy-done = bf16[17536,128]{1,0:T(8,128)(2,1)} copy-done((bf16[17536,128]{1,0:T(8,128)(2,1)}, bf16[17536,128]{1,0:T(8,128)(2,1)S(1)}, u32[]{:S(2)}) %copy-start) | copy-done | bytes 4489240
  23.2 1.3 %all-to-all-done.1 = bf16[8,16,384]{2,1,0:T(8,128)(2,1)S(1)} async-done(((bf16[8,16,384]{2,1,0:T(8,128)(2,1)}), bf16[8,16,384]{2,1,0:T(8,128)(2,1)S(1)}, u32[]{:S(2)}, u32[]{:S(2)}) %all-to-all-start.1) | async-done | bytes 98336 | tf_op jit(solution)/shard_map/all_to_all | solution.py:416
  24.5 0.0 copy-done.4
  24.5 0.0 copy-done.5
  24.5 0.0 copy-done.6
  24.5 0.0 copy-done.7
  24.5 0.0 copy-start.1
  24.5 2.3 %copy-done.1 = bf16[17536,128]{1,0:T(8,128)(2,1)S(1)} copy-done((bf16[17536,128]{1,0:T(8,128)(2,1)S(1)}, bf16[17536,128]{1,0:T(8,128)(2,1)}, u32[]{:S(2)}) %copy-start.1) | copy-done | bytes 4489240
  26.7 4.3 %departures.1 = bf16[8,144,128]{2,1,0:T(8,128)(2,1)} custom-call(s32[1,64]{1,0:T(1,128)S(1)} %bitcast.28, s32[1,64]{1,0:T(1,128)S(1)} %copy-done.7, bf16[128,384]{1,0:T(8,128)(2,1)S(1)} %bitcast.23, bf16[64,128]{1,0:T(8,128)(2,1)S(1)} %bitcast.26, bf16[64,128]{1,0:T(8,128)(2,1)S(1)} %bitcast.27, bf16[17536,128]{1,0:T(8,128)(2,1)S(1)} %copy-done.1), custom_call_target="tpu_custom_call" | custom-call | flops 8978432 | bytes 4489216 | tf_op jit(solution)/shard_map/departures/pallas_call | solution.py:224
  31.1 4.2 %all-to-all-start.2 = ((bf16[8,144,128]{2,1,0:T(8,128)(2,1)}), bf16[8,144,128]{2,1,0:T(8,128)(2,1)S(1)}, u32[]{:S(2)}, u32[]{:S(2)}) async-start(bf16[8,144,128]{2,1,0:T(8,128)(2,1)} %departures.1), calls=%async_computation.2 | async-start | bytes 589824 | tf_op jit(solution)/shard_map/all_to_all | solution.py:431
  35.2 0.0 copy-done.9
  35.3 0.1 reshape.60.lon_ref
  35.3 0.0 copy-done.10
  35.3 0.1 reshape.61.lat_ref
  35.4 0.0 copy-done.8
  35.4 0.2 reshape.59.vertical_ref
  35.6 1.0 %plan_points.1 = (bf16[384,512]{1,0:T(8,128)(2,1)S(1)}, s32[1,512]{1,0:T(1,128)S(1)}, bf16[2,144,384]{2,1,0:T(8,128)(2,1)S(1)}, f32[128,384]{1,0:T(8,128)S(1)}, f32[9,384]{1,0:T(8,128)S(1)}) custom-call(s32[8,128]{1,0:T(8,128)S(1)} %bitcast.25, bf16[274,137]{1,0:T(8,128)(2,1)S(1)} %reshape.59.vertical_ref, f32[9,274]{1,0:T(8,128)S(1)} %reshape.60.lon_ref, ...), custom_call_target="tpu_custom_call" | custom-call | flops 2097152 | bytes 393216 | tf_op jit(solution)/shard_map/plan_points/pallas_call | solution.py:437
  36.7 5.4 %collective-permute-start.1 = (s32[1,512]{1,0:T(1,128)S(1)}, s32[1,512]{1,0:T(1,128)S(1)}, u32[]{:S(2)}, u32[]{:S(2)}) collective-permute-start(s32[1,512]{1,0:T(1,128)S(1)} %get-tuple-element.10.refs_0_), channel_id=1, source_target_pairs={{1,2},{2,1},{5,6},{6,5},{9,10},{10,9},{13,14},{14,13},{17,18},{18,... | collective-permute-start | bytes 6152 | tf_op jit(solution)/shard_map/ppermute | solution.py:461
  42.1 0.1 collective-permute-start
  42.2 1.5 %collective-permute-done.1.far_ref.refs_4_ = s32[1,512]{1,0:T(1,128)S(1)} collective-permute-done((s32[1,512]{1,0:T(1,128)S(1)}, s32[1,512]{1,0:T(1,128)S(1)}, u32[]{:S(2)}, u32[]{:S(2)}) %collective-permute-start.1) | collective-permute-done | bytes 2080 | tf_op jit(solution)/shard_map/ppermute | solution.py:461
  43.6 0.0 collective-permute-done.near_ref.refs_2_
  43.6 0.0 all-to-all-done.2.products_ref
  43.6 0.4 impact_columns.1.refs_1_
  44.1 5.4 %collective-permute-start.3 = (bf16[144,768]{1,0:T(8,128)(2,1)S(1)}, bf16[144,768]{1,0:T(8,128)(2,1)S(1)}, u32[]{:S(2)}, u32[]{:S(2)}) collective-permute-start(bf16[144,768]{1,0:T(8,128)(2,1)S(1)} %impact_columns.1.refs_1_), channel_id=1, source_target_pairs={{1,2},{2,1},{5,6},{6,5},{9,10},{10,9},{13,14},{14,13},{17,18},{18,... | collective-permute-start | bytes 663560 | tf_op jit(solution)/shard_map/ppermute | solution.py:472
  49.6 0.1 collective-permute-start.2
  49.6 5.1 %inner_rows.1.refs_9_ = f32[274,32,128]{2,1,0:T(8,128)} custom-call(s32[1,512]{1,0:T(1,128)S(1)} %get-tuple-element.10.refs_0_, bf16[144,768]{1,0:T(8,128)(2,1)S(1)} %impact_columns.1.refs_1_, bf16[2,144,384]{2,1,0:T(8,128)(2,1)S(1)} %get-tuple-element.12.refs_2_.refs_6_, f32[128,384]{1,0:T(8,128)S(1)} %get-tuple-element.13.refs_3_.refs_7_, ...), custom_call_target="tpu_custom_call" | custom-call | flops 44892160 | bytes 2244608 | tf_op jit(solution)/shard_map/inner_rows/pallas_call | solution.py:490
  54.7 0.0 collective-permute-done.3.refs_5_
  54.7 0.0 collective-permute-done.2.refs_3_
  54.7 5.6 %outer_rows.1 = f32[274,32,128]{2,1,0:T(8,128)} custom-call(s32[1,512]{1,0:T(1,128)S(1)} %get-tuple-element.10.refs_0_, bf16[144,768]{1,0:T(8,128)(2,1)S(1)} %impact_columns.1.refs_1_, s32[1,512]{1,0:T(1,128)S(1)} %collective-permute-done.near_ref.refs_2_, bf16[144,768]{1,0:T(8,128)(2,1)S(1)} %collective-permute-done.2.refs_3_, ...), custom_call_target="tpu_custom_call", output_to_operand_aliasing={{}: (9, {})} | custom-call | flops 44892160 | bytes 2244608 | tf_op jit(solution)/shard_map/outer_rows/pallas_call | solution.py:490
  (2 shorter events, 0.0 us)
Async XLA Ops:
  1.3 11.6 %all-to-all-start = ((s32[8,1,128]{2,1,0:T(1,128)}), s32[8,1,128]{2,1,0:T(1,128)S(1)}, u32[]{:S(2)}, u32[]{:S(2)}) async-start(s32[8,1,128]{2,1,0:T(1,128)} %broadcast_in_dim.2), calls=%async_computation | async-start | bytes 8192 | tf_op jit(solution)/shard_map/all_to_all | solution.py:412
  7.6 2.3 %copy-start.2 = (f32[2,137,32,128]{3,2,1,0:T(8,128)S(1)}, f32[2,137,32,128]{3,2,1,0:T(8,128)}, u32[]{:S(2)}) copy-start(f32[2,137,32,128]{3,2,1,0:T(8,128)} %param.10) | copy-start | bytes 13467652
  14.8 9.7 %all-to-all-start.1 = ((bf16[8,16,384]{2,1,0:T(8,128)(2,1)}), bf16[8,16,384]{2,1,0:T(8,128)(2,1)S(1)}, u32[]{:S(2)}, u32[]{:S(2)}) async-start(bf16[8,16,384]{2,1,0:T(8,128)(2,1)} %bitcast.8), calls=%async_computation.1 | async-start | bytes 196608 | tf_op jit(solution)/shard_map/all_to_all | solution.py:416
  18.4 2.3 %copy-start.3 = (bf16[1,64,2,137,128]{4,2,3,1,0:T(2,128)(2,1)S(1)}, bf16[1,64,2,137,128]{4,2,3,1,0:T(2,128)(2,1)}, u32[]{:S(2)}) copy-start(bf16[1,64,2,137,128]{4,2,3,1,0:T(2,128)(2,1)} %param.11) | copy-start | bytes 13467652
  20.6 3.8 %copy-start.4 = (bf16[1,64,128]{2,1,0:T(8,128)(2,1)S(1)}, bf16[1,64,128]{2,1,0:T(8,128)(2,1)}, u32[]{:S(2)}) copy-start(bf16[1,64,128]{2,1,0:T(8,128)(2,1)} %param.12) | copy-start | bytes 49156
  20.6 3.8 %copy-start.5 = (bf16[1,64,128]{2,1,0:T(8,128)(2,1)S(1)}, bf16[1,64,128]{2,1,0:T(8,128)(2,1)}, u32[]{:S(2)}) copy-start(bf16[1,64,128]{2,1,0:T(8,128)(2,1)} %param.13) | copy-start | bytes 49156
  20.6 3.8 %copy-start.6 = (s32[1,64,1]{1,2,0:T(1,128)S(1)}, s32[1,64,1]{1,2,0:T(1,128)}, u32[]{:S(2)}) copy-start(s32[1,64,1]{1,2,0:T(1,128)} %param.15) | copy-start | bytes 772
  20.7 3.8 %copy-start.7 = (s32[1,64]{1,0:T(1,128)S(1)}, s32[1,64]{1,0:T(1,128)}, u32[]{:S(2)}) copy-start(s32[1,64]{1,0:T(1,128)} %valid_ref.1) | copy-start | bytes 772
  20.7 14.6 %copy-start.9 = (f32[2,137,9]{1,0,2:T(2,128)S(1)}, f32[2,137,9]{1,0,2:T(2,128)}, u32[]{:S(2)}) copy-start(f32[2,137,9]{1,0,2:T(2,128)} %param.18) | copy-start | bytes 29596
  20.7 14.7 %copy-start.10 = (f32[2,137,9]{1,0,2:T(2,128)S(1)}, f32[2,137,9]{1,0,2:T(2,128)}, u32[]{:S(2)}) copy-start(f32[2,137,9]{1,0,2:T(2,128)} %param.19) | copy-start | bytes 29596
  20.7 14.7 %copy-start.8 = (bf16[2,137,137]{2,0,1:T(2,128)(2,1)S(1)}, bf16[2,137,137]{2,0,1:T(2,128)(2,1)}, u32[]{:S(2)}) copy-start(bf16[2,137,137]{2,0,1:T(2,128)(2,1)} %param.17) | copy-start | bytes 225232
  21.1 2.1 %copy-start = (bf16[17536,128]{1,0:T(8,128)(2,1)}, bf16[17536,128]{1,0:T(8,128)(2,1)S(1)}, u32[]{:S(2)}) copy-start(bf16[17536,128]{1,0:T(8,128)(2,1)S(1)} %fetch_jacobian.1.jac_ref) | copy-start | bytes 13467652
  24.5 2.3 %copy-start.1 = (bf16[17536,128]{1,0:T(8,128)(2,1)S(1)}, bf16[17536,128]{1,0:T(8,128)(2,1)}, u32[]{:S(2)}) copy-start(bf16[17536,128]{1,0:T(8,128)(2,1)} %copy-done) | copy-start | bytes 13467652
  31.1 12.6 %all-to-all-start.2 = ((bf16[8,144,128]{2,1,0:T(8,128)(2,1)}), bf16[8,144,128]{2,1,0:T(8,128)(2,1)S(1)}, u32[]{:S(2)}, u32[]{:S(2)}) async-start(bf16[8,144,128]{2,1,0:T(8,128)(2,1)} %departures.1), calls=%async_computation.2 | async-start | bytes 589824 | tf_op jit(solution)/shard_map/all_to_all | solution.py:431
  36.7 7.0 %collective-permute-start.1 = (s32[1,512]{1,0:T(1,128)S(1)}, s32[1,512]{1,0:T(1,128)S(1)}, u32[]{:S(2)}, u32[]{:S(2)}) collective-permute-start(s32[1,512]{1,0:T(1,128)S(1)} %get-tuple-element.10.refs_0_), channel_id=1, source_target_pairs={{1,2},{2,1},{5,6},{6,5},{9,10},{10,9},{13,14},{14,13},{17,18},{18,... | collective-permute-start | bytes 6152 | tf_op jit(solution)/shard_map/ppermute | solution.py:461
  42.1 1.6 %collective-permute-start = (s32[1,512]{1,0:T(1,128)S(1)}, s32[1,512]{1,0:T(1,128)S(1)}, u32[]{:S(2)}, u32[]{:S(2)}) collective-permute-start(s32[1,512]{1,0:T(1,128)S(1)} %get-tuple-element.10.refs_0_), channel_id=1, source_target_pairs={{0,1},{2,3},{1,0},{3,2},{4,5},{6,7},{5,4},{7,6},{8,9},{10,11},{9,8... | collective-permute-start | bytes 6152 | tf_op jit(solution)/shard_map/ppermute | solution.py:462
  44.1 10.6 %collective-permute-start.3 = (bf16[144,768]{1,0:T(8,128)(2,1)S(1)}, bf16[144,768]{1,0:T(8,128)(2,1)S(1)}, u32[]{:S(2)}, u32[]{:S(2)}) collective-permute-start(bf16[144,768]{1,0:T(8,128)(2,1)S(1)} %impact_columns.1.refs_1_), channel_id=1, source_target_pairs={{1,2},{2,1},{5,6},{6,5},{9,10},{10,9},{13,14},{14,13},{17,18},{18,... | collective-permute-start | bytes 663560 | tf_op jit(solution)/shard_map/ppermute | solution.py:472
  49.6 5.2 %collective-permute-start.2 = (bf16[144,768]{1,0:T(8,128)(2,1)S(1)}, bf16[144,768]{1,0:T(8,128)(2,1)S(1)}, u32[]{:S(2)}, u32[]{:S(2)}) collective-permute-start(bf16[144,768]{1,0:T(8,128)(2,1)S(1)} %impact_columns.1.refs_1_), channel_id=1, source_target_pairs={{0,1},{2,3},{1,0},{3,2},{4,5},{6,7},{5,4},{7,6},{8,9},{10,11},{9,8... | collective-permute-start | bytes 663560 | tf_op jit(solution)/shard_map/ppermute | solution.py:473

commit v5 on v4

--- a/solution.py
+++ b/solution.py
@@ -10,7 +10,9 @@
 LANES = 128
 F32 = jnp.float32
 BF16 = jnp.bfloat16
-VMEM_LIMIT = 56 * 1024 * 1024
+STRIDE = 256
+NOWHERE = 1 << 20
+SOME = 4
 
 
 def lane_iota(shape):
@@ -25,8 +27,14 @@
     return (lane_iota((size, size)) < row_iota((size, size))).astype(F32).astype(BF16)
 
 
+def read_codes(codes_ref):
+    count, records = codes_ref.shape
+    codes = jnp.bitwise_and(codes_ref[...], NOWHERE - 1)
+    return jnp.concatenate([codes, jnp.zeros((count, LANES - records), jnp.int32)], axis=1)
+
+
 def split_codes(codes_ref, records, points):
-    flipped = jnp.transpose(codes_ref[...].astype(F32))[:records].astype(jnp.int32)
+    flipped = jnp.transpose(read_codes(codes_ref).astype(F32))[:records].astype(jnp.int32)
     tile = lax.div(flipped, points)
     return tile, flipped - tile * points
 
@@ -121,40 +129,36 @@
     )(codes, laid.reshape(-1, laid.shape[2]))
 
 
+def to_column(row):
+    size = row.shape[1]
+    wide = jnp.broadcast_to(row, (size, size))
+    return jnp.sum(jnp.where(row_iota(wide.shape) == lane_iota(wide.shape), wide, 0), axis=1, keepdims=True)
+
+
 def fetch_kernel(from_ref, after_ref, out_ref, arrived):
-    copy = pltpu.make_async_copy(from_ref, out_ref, arrived)
+    copy = pltpu.make_async_copy(from_ref.at[pl.ds(0, out_ref.shape[0])], out_ref, arrived)
     copy.start()
     copy.wait()
 
 
-def fetch(array, after):
+def fetch(array, after, rows):
     anywhere = pl.BlockSpec(memory_space=pl.ANY)
     return pl.pallas_call(
         fetch_kernel,
         in_specs=[anywhere, anywhere],
         out_specs=pl.BlockSpec(memory_space=pltpu.VMEM),
-        out_shape=jax.ShapeDtypeStruct(array.shape, array.dtype),
+        out_shape=jax.ShapeDtypeStruct((rows, array.shape[1]), array.dtype),
         scratch_shapes=[pltpu.SemaphoreType.DMA],
         compiler_params=pltpu.CompilerParams(vmem_limit_bytes=12 * 1024 * 1024),
-        cost_estimate=pl.CostEstimate(flops=0, bytes_accessed=array.size * 4, transcendentals=0),
+        cost_estimate=pl.CostEstimate(flops=0, bytes_accessed=rows * array.shape[1] * 4, transcendentals=0),
         name="fetch_jacobian",
     )(array, after)
 
 
-def to_column(row):
-    size = row.shape[1]
-    wide = jnp.broadcast_to(row, (size, size))
-    return jnp.sum(jnp.where(row_iota(wide.shape) == lane_iota(wide.shape), wide, 0), axis=1, keepdims=True)
-
-
-def departure_kernel(capacity, group, dest_ref, valid_ref, states_ref, obs_ref, inv_ref, jac_ref, out_ref, total):
+def first_departures(capacity, group, features, dest_ref, valid_ref, states_ref, obs_ref, inv_ref, jac_ref, after_ref, total_ref, columns_ref, weight_ref):
     records = dest_ref.shape[1]
     slots = states_ref.shape[0]
     channels = jac_ref.shape[1]
-    features = jac_ref.shape[0] // records
-    part = group // 2
-    span = part * features
-
     dest = to_column(dest_ref[...])
     named = (dest == lane_iota((records, LANES))).astype(F32)
     before = jnp.dot(earlier_rows(records), named.astype(BF16), preferred_element_type=F32)
@@ -162,18 +166,35 @@
     chosen = (dest * capacity + rank == lane_iota((records, slots))).astype(F32).astype(BF16)
     columns = jnp.dot(chosen, states_ref[...], preferred_element_type=F32)
     alive = lane_iota((records, channels)) < to_column(valid_ref[...])
-    weight = jnp.where(alive, inv_ref[...].astype(F32), 0.0)
-
+    columns_ref[...] = columns
+    weight_ref[...] = jnp.where(alive, inv_ref[...].astype(F32), 0.0)
+    total_ref[...] = jnp.zeros_like(total_ref)
+    product_groups(group, features, 0, columns_ref, weight_ref, obs_ref, jac_ref, total_ref)
+
+
+def last_departures(group, features, done, columns_ref, weight_ref, obs_ref, jac_ref, before_ref, out_ref, total):
+    records = obs_ref.shape[0]
+    total[...] = before_ref[...]
+    product_groups(group, features, done, columns_ref, weight_ref, obs_ref, jac_ref, total)
+    half = total.shape[0] // 2
+    lane = lane_iota((half, LANES))
+    low = jnp.where(lane < records, total[0:half, :], pltpu.roll(total[half:, :], records, 1)).astype(BF16)
+    for t in range(out_ref.shape[0]):
+        out_ref[t] = low
+
+
+def product_groups(group, features, done, columns_ref, weight_ref, obs_ref, jac_ref, total):
+    channels = jac_ref.shape[1]
+    part = group // 2
+    span = part * features
     tiles, skip = divmod(features, LANES)
-    wide = columns.shape[1]
+    wide = columns_ref.shape[1]
     reach = pl.cdiv(skip * (part - 1) + features, LANES)
-    tall = total.shape[0]
-    total[...] = jnp.zeros_like(total)
     row = row_iota((group, LANES))
     index = jnp.bitwise_and(row, part - 1)
-    for g in range(records // group):
+    for g in range(done, jac_ref.shape[0] // (group * features)):
         first = g * group * features
-        mine = columns[g * group : (g + 1) * group]
+        mine = columns_ref[g * group : (g + 1) * group, :]
         if reach * LANES > wide:
             mine = jnp.concatenate([mine, jnp.zeros((group, reach * LANES - wide), F32)], axis=1)
         bit = 1
@@ -194,7 +215,7 @@
         both = jnp.dot(spread, pair, preferred_element_type=F32)
         model = jnp.where(row < part, both[:, :channels], both[:, channels:])
         own = slice(g * group, (g + 1) * group)
-        misfit = weight[own] * (model - obs_ref[own, :].astype(F32))
+        misfit = weight_ref[own, :] * (model - obs_ref[own, :].astype(F32))
         low = misfit.astype(BF16).astype(F32)
         for r in range(part):
             against = jnp.concatenate([jnp.where(row == r, low, 0.0), jnp.where(row == r + part, low, 0.0)], axis=1)
@@ -211,31 +232,37 @@
             one = one[lead : lead + features]
             sums = one if r == 0 else sums + one
         total[0:features, g * group : (g + 1) * group] = sums
-    half = tall // 2
-    lane = lane_iota((half, LANES))
-    low = jnp.where(lane < records, total[0:half, :], pltpu.roll(total[half:, :], records, 1)).astype(BF16)
-    for t in range(out_ref.shape[0]):
-        out_ref[t] = low
-
-
-def departures(dest, valid, states, obs, inv, jac, capacity, devices, tall):
+
+
+def departures(dest, valid, states, obs, inv, jac, after, capacity, devices, tall):
     records, channels = obs.shape
-    vmem = pl.BlockSpec(memory_space=pltpu.VMEM)
+    features = jac.shape[0] // records
+    group = 16
+    done = records // group // 2
+    vmem, anywhere = pl.BlockSpec(memory_space=pltpu.VMEM), pl.BlockSpec(memory_space=pl.ANY)
+    params = pltpu.CompilerParams(vmem_limit_bytes=16 * 1024 * 1024)
+    cost = pl.CostEstimate(flops=3_000_000_000, bytes_accessed=jac.size, transcendentals=0)
+    total, columns, weight = pl.pallas_call(
+        functools.partial(first_departures, capacity, group, features),
+        in_specs=[vmem] * 6 + [anywhere],
+        out_shape=(
+            jax.ShapeDtypeStruct((2 * tall, 2 * records), F32),
+            jax.ShapeDtypeStruct((records, states.shape[1]), F32),
+            jax.ShapeDtypeStruct((records, channels), F32),
+        ),
+        compiler_params=params,
+        cost_estimate=cost,
+        name="first_departures",
+    )(dest, valid, states, obs, inv, fetch(jac, after, done * group * features), after)
     return pl.pallas_call(
-        functools.partial(departure_kernel, capacity, 16),
-        in_specs=[vmem] * 6,
+        functools.partial(last_departures, group, features, done),
+        in_specs=[vmem] * 5,
         out_shape=jax.ShapeDtypeStruct((devices, tall, 2 * records), BF16),
         scratch_shapes=[pltpu.VMEM((2 * tall, 2 * records), F32)],
-        compiler_params=pltpu.CompilerParams(vmem_limit_bytes=20 * 1024 * 1024),
-        cost_estimate=pl.CostEstimate(
-            flops=4 * jac.size, bytes_accessed=jac.size * 2, transcendentals=0
-        ),
-        name="departures",
-    )(dest, valid, states, obs, inv, jac)
-
-
-STRIDE = 256
-NOWHERE = 1 << 20
+        compiler_params=params,
+        cost_estimate=cost,
+        name="last_departures",
+    )(columns, weight, obs, jac, total)
 
 
 def point_key(tile, column, count, reach):
@@ -256,7 +283,7 @@
     key = point_key(tile, column, count, reach)
     for d in range(count):
         down[d * records : (d + 1) * records, :] = jnp.broadcast_to(key[:, d : d + 1], (records, LANES))
-    codes = codes_ref[...]
+    codes = read_codes(codes_ref)
     tile = lax.div(codes, points)
     key = point_key(tile, codes - tile * points, count, reach)
     per = LANES // records
@@ -327,12 +354,12 @@
 
 
 def filter_kernel(block_of, reach, rows, *refs):
-    (*lists, vertical_ref, lon_ref, lat_ref, out_ref, mixed, along, mean) = refs
+    (*lists, vertical_ref, lon_ref, lat_ref, out_ref, mixed, along, mean, ready, sent) = refs
     lists = [(lists[n], lists[n + 1]) for n in range(0, len(lists) // 2 * 2, 2)]
     listed = lists[0][1].shape[1] // vertical_ref.shape[0]
     features = out_ref.shape[0]
     wide = vertical_ref.shape[2]
-    height = out_ref.shape[1]
+    height = ready.shape[2]
     window = height + 2 * reach
     pitch = along.shape[0] // window
     step = pl.program_id(0)
@@ -340,18 +367,22 @@
 
     @pl.when(step == 0)
     def _():
-        for n, (_, impact) in enumerate(lists):
-            total = 0.0
-            for v in range(vertical_ref.shape[0]):
-                total += lax.dot_general(
-                    impact[:, v * listed : (v + 1) * listed],
-                    vertical_ref[v],
-                    (((0,), (0,)), ((), ())),
-                    preferred_element_type=F32,
-                )
-            mixed[n * listed : (n + 1) * listed, :] = total
-
-    along[...] = jnp.zeros_like(along)
+        along[...] = jnp.zeros_like(along)
+        for n, (info, impact) in enumerate(lists):
+            for part in range(0, listed, LANES):
+
+                @pl.when(info[0, listed + rows] > part)
+                def _(n=n, impact=impact, part=part):
+                    total = 0.0
+                    for h in range(vertical_ref.shape[0]):
+                        total += lax.dot_general(
+                            impact[:, h * listed + part : h * listed + part + LANES],
+                            vertical_ref[h],
+                            (((0,), (0,)), ((), ())),
+                            preferred_element_type=F32,
+                        )
+                    mixed[n * listed + part : n * listed + part + LANES, :] = total
+
     for n, (info, _) in enumerate(lists):
         offset = -base
         if n:
@@ -360,38 +391,62 @@
         low = jnp.clip(-offset, 0, rows)
         high = jnp.clip(window - offset, 0, rows)
 
-        def add(s, carry, info=info, n=n, offset=offset):
-            key = info[0, s]
-            row = lax.shift_right_logical(key, 8) + offset
-            place = jnp.bitwise_and(key, STRIDE - 1)
-            spot = jnp.bitwise_and(place, 7)
-            at = pl.ds(pl.multiple_of(row * pitch + place - spot, 8), 16)
-            taps = lon_ref[pl.ds(pl.multiple_of(spot * 16, 16), 16), :]
-            along[at, :] += taps * mixed[pl.ds(n * listed + s, 1), :]
+        start, stop = info[0, listed + low], info[0, listed + high]
+
+        def add_some(i, carry, info=info, n=n, offset=offset, start=start, stop=stop):
+            pieces = []
+            for u in range(SOME):
+                here = start + i * SOME + u
+                live = here < stop
+                here = jnp.where(live, here, start)
+                key = info[0, here]
+                row = lax.shift_right_logical(key, 8) + offset
+                place = jnp.bitwise_and(key, STRIDE - 1)
+                spot = jnp.bitwise_and(place, 7)
+                at = pl.ds(pl.multiple_of(row * pitch + place - spot, 8), 16)
+                taps = lon_ref[pl.ds(pl.multiple_of(spot * 16, 16), 16), :]
+                column = mixed[pl.ds(n * listed + here, 1), :] * jnp.where(live, 1.0, 0.0)
+                pieces.append((at, taps * column))
+            for at, piece in pieces:
+                along[at, :] += piece
             return carry
 
-        lax.fori_loop(info[0, listed + low], info[0, listed + high], add, 0)
-
-    flat = out_ref.reshape(features * height, LANES)
+        lax.fori_loop(0, lax.div(stop - start + SOME - 1, SOME), add_some, 0)
+
+    flat = ready.reshape(ready.shape[0] * features * height, LANES)
+
+    def leave(at, t):
+        here = pl.ds(t * LANES, min(LANES, features - t * LANES))
+        there = pl.ds(pl.multiple_of(block_of(at) * height, height), height)
+        return pltpu.make_async_copy(ready.at[at, here], out_ref.at[here, there], sent.at[at, t])
+
     for t in range(wide // LANES):
         here = slice(t * LANES, (t + 1) * LANES)
         lat = [jnp.broadcast_to(lat_ref[k : k + 1, here], (8, LANES)) for k in range(2 * reach + 1)]
 
-        @pl.loop(0, LANES // 8, unroll=LANES // 8)
-        def _(j):
+        for j in range(LANES // 8):
             sums = [None] * height
             for w in range(window):
-                part = along[pl.ds(pl.multiple_of(w * pitch + 8 + j * 8, 8), 8), here]
+                spot = pl.ds(w * pitch + 8 + j * 8, 8)
+                part = along[spot, here]
+                along[spot, here] = jnp.zeros_like(part)
                 for row in range(max(0, w - 2 * reach), min(height, w + 1)):
                     term = lat[w - row] * part
                     sums[row] = term if sums[row] is None else sums[row] + term
             for row in range(height):
-                mean[row, pl.ds(pl.multiple_of(j * 8, 8), 8), :] = sums[row]
+                mean[t % 2, row, j * 8 : (j + 1) * 8, :] = sums[row]
 
         kept = min(LANES, features - t * LANES)
         for row in range(height):
-            turned = jnp.transpose(mean[row])
-            flat[pl.ds(t * LANES * height + row, kept, stride=height), :] = turned[0:kept]
+            turned = jnp.transpose(mean[t % 2, row])
+            flat[pl.ds((step * features + t * LANES) * height + row, kept, stride=height), :] = turned[0:kept]
+        leave(step, t).start()
+
+    @pl.when(step == ready.shape[0] - 1)
+    def _():
+        for at in range(ready.shape[0]):
+            for t in range(wide // LANES):
+                leave(at, t).wait()
 
 
 def solution(mesh):
@@ -407,29 +462,16 @@
         span = records * lon_devices
         tall = pl.cdiv(features, 32) * 16
 
-        codes = destination.reshape(1, records) * points + column.reshape(1, records)
-        codes = jnp.broadcast_to(jnp.pad(codes, ((0, 0), (0, LANES - records))), (lon_devices, LANES))
+        codes = destination.reshape(1, 1, records) * points + column.reshape(1, 1, records)
+        codes = codes + lax.broadcasted_iota(jnp.int32, (lon_devices, 1, records), 0) * NOWHERE
         codes = lax.all_to_all(codes, "lon", split_axis=0, concat_axis=0, tiled=True)
+        codes = codes.reshape(lon_devices, records)
         laid = lay_state(state_field)
 
         found = gather_state(codes, laid, records, capacity, rows)
         found_in = lax.all_to_all(
             found.reshape(lon_devices, capacity, found.shape[-1]), "lon", split_axis=0, concat_axis=0, tiled=True
         )
-        own = jnp.swapaxes(jacobian.reshape(records, variables, levels, channels), 1, 2).reshape(-1, channels)
-        products = departures(
-            destination.reshape(1, records),
-            valid_count.reshape(1, records),
-            found_in.reshape(lon_devices * capacity, found.shape[-1]),
-            observed.reshape(records, channels),
-            inverse_var.reshape(records, channels),
-            fetch(own, found),
-            capacity,
-            lon_devices,
-            tall,
-        )
-        products_in = lax.all_to_all(products, "lon", split_axis=0, concat_axis=0, tiled=True)
-
         listed = 3 * lon_devices * capacity
         wide = pl.cdiv(features, LANES) * LANES
         taps = lon_taps.shape[-1]
@@ -455,11 +497,26 @@
             jnp.moveaxis(lat_taps, 2, 0).reshape(taps, features),
             found,
         )
+        own = jnp.swapaxes(jacobian.reshape(records, variables, levels, channels), 1, 2).reshape(-1, channels)
+        products = departures(
+            destination.reshape(1, records),
+            valid_count.reshape(1, records),
+            found_in.reshape(lon_devices * capacity, found.shape[-1]),
+            observed.reshape(records, channels),
+            inverse_var.reshape(records, channels),
+            own,
+            info,
+            capacity,
+            lon_devices,
+            tall,
+        )
+        products_in = lax.all_to_all(products, "lon", split_axis=0, concat_axis=0, tiled=True)
+
         pairs = [(i, i + 1) for i in range(0, lat_devices - 1, 2)]
         between = [(i, i + 1) for i in range(1, lat_devices - 1, 2)]
         swaps = [[(a, b) for a, b in some] + [(b, a) for a, b in some] for some in (pairs, between)]
+        info_near = lax.ppermute(info, "lat", swaps[0])
         info_far = lax.ppermute(info, "lat", swaps[1])
-        info_near = lax.ppermute(info, "lat", swaps[0])
 
         impact = pl.pallas_call(
             functools.partial(impact_kernel, records),
@@ -469,8 +526,8 @@
             compiler_params=pltpu.CompilerParams(vmem_limit_bytes=16 * 1024 * 1024),
             name="impact_columns",
         )(products_in, same, info_near, info_far)
+        impact_near = lax.ppermute(impact, "lat", swaps[0])
         impact_far = lax.ppermute(impact, "lat", swaps[1])
-        impact_near = lax.ppermute(impact, "lat", swaps[0])
 
         height = 8
         blocks = rows // height
@@ -491,12 +548,14 @@
                 kernel,
                 grid=(steps,),
                 in_specs=held,
-                out_specs=pl.BlockSpec((features, height, cols), lambda s: (0, block_of(s), 0)),
+                out_specs=pl.BlockSpec(memory_space=pl.ANY),
                 out_shape=jax.ShapeDtypeStruct((features, rows, cols), F32),
                 scratch_shapes=[
                     pltpu.VMEM((len(lists) // 2 * listed, wide), F32),
                     pltpu.VMEM(((height + 2 * reach) * pitch, wide), F32),
-                    pltpu.VMEM((height, cols, LANES), F32),
+                    pltpu.VMEM((2, height, cols, LANES), F32),
+                    pltpu.VMEM((steps, features, height, cols), F32),
+                    pltpu.SemaphoreType.DMA((steps, wide // LANES)),
                 ],
                 input_output_aliases={} if before is None else {len(given) - 1: 0},
                 compiler_params=pltpu.CompilerParams(vmem_limit_bytes=24 * 1024 * 1024),

time: 61.4 us -> 58 us (0.945)
  local copies, waits for them, and re-layouts: 9.92 us -> 4.95 us
  starting transfers between devices: 25.1 us -> 26.3 us
  other arithmetic: 0.67 us -> 1.35 us
  waiting for transfers between devices: 4.63 us -> 5.29 us
    unnamed x22, local copies, waits for them, and re-layouts: 8.94 us -> 4.57 us
    ppermute x1, starting transfers between devices: 5.45 us -> 6.89 us  [body(): impact_far = lax.ppermute(impact, 'lat', swaps[1])]
    pallas_call x2, Pallas kernels: 10.7 us -> 9.65 us  [filtered(): pl.pallas_call(kernel, grid=(steps,), in_specs=held, out_specs=pl.BlockSp...]
    all_to_all x1, waiting for transfers between devices: 1.28 us -> 2.02 us  [body(): lax.all_to_all(found.reshape(lon_devices, capacity, found.shape[-1]), 'lo...]
    all_to_all x1, starting transfers between devices: 4.17 us -> 3.45 us  [body(): lax.all_to_all(products, 'lon', split_axis=0, concat_axis=0, tiled=True)]
    add x1 -> x2, other arithmetic: 0.67 us -> 1.34 us  [the longest x1 0.67 us: body(): destination.reshape(1, 1, records) * points + column.reshape(1, 1, records)]
    pallas_call x1 -> x2, Pallas kernels: 4.33 us -> 4.86 us  [the longest x1 2.63 us: departures(): pl.pallas_call(functools.partial(last_departures, group, features, done),...]
  transfers between devices with their start and end apart: 7 -> 7, of which waited for: 3 -> 4; matrix products, arithmetic and copies ran while one was open for 1% -> 1% of each run, Pallas kernels for 13% -> 12%
where the time goes in v5:
time: 58 us; the launch traced here: 57.4 us
  starting transfers between devices  26.3 us (45%)
  Pallas kernels  19.3 us (33%)
  waiting for transfers between devices  5.29 us (9%)
  local copies, waits for them, and re-layouts  4.95 us (9%)
  other arithmetic  1.35 us (2%)
    pallas_call x2, Pallas kernels, filtered(): pl.pallas_call(kernel, grid=(steps,), in_specs=held, out_specs=pl.BlockSp...  9.65 us
    ppermute x1, starting transfers between devices, body(): impact_far = lax.ppermute(impact, 'lat', swaps[1])  6.89 us
    all_to_all x1, starting transfers between devices, body(): lax.all_to_all(codes, 'lon', split_axis=0, concat_axis=0, tiled=True)  6.35 us
    ppermute x1, starting transfers between devices, body(): info_far = lax.ppermute(info, 'lat', swaps[1])  5.85 us
    unnamed x22, local copies, waits for them, and re-layouts  4.57 us
    all_to_all x1, starting transfers between devices, body(): lax.all_to_all(found.reshape(lon_devices, capacity, found.shape[-1]), 'lo...  3.62 us
    all_to_all x1, starting transfers between devices, body(): lax.all_to_all(products, 'lon', split_axis=0, concat_axis=0, tiled=True)  3.45 us
    pallas_call x1, Pallas kernels, departures(): pl.pallas_call(functools.partial(last_departures, group, features, done),...  2.63 us
  transfers between devices with their start and end apart: 7, of which 4 were waited for; matrix products, arithmetic and copies ran while one was open for 1% of the time, Pallas kernels for 12%

profile of v5, /device:TPU:1, one launch (start us, length us, event | category | flops | bytes accessed | tf_op | source)
XLA Modules:
  0.0 57.4 jit_solution(8134371436246609048)
XLA Ops:
  0.0 0.7 %bitcast_add_fusion = s32[64]{0:T(128)S(1)} fusion(s32[1,64]{1,0:T(1,128)} %param.16, s32[1,64,1]{1,2,0:T(1,128)} %param.15), kind=kLoop, calls=%fused_computation.1 | loop fusion | flops 128 | bytes 768 | tf_op jit(solution)/shard_map/add | solution.py:465
  0.7 0.7 %broadcast_add_fusion = s32[8,1,64]{2,1,0:T(1,128)} fusion(s32[64]{0:T(128)S(1)} %bitcast_add_fusion, s32[8]{0:T(128)S(1)} %iota_multiply_fusion), kind=kLoop, calls=%fused_computation | loop fusion | flops 512 | bytes 2336 | tf_op jit(solution)/shard_map/add | solution.py:466
  1.3 6.4 %all-to-all-start = ((s32[8,1,64]{2,1,0:T(1,128)}), s32[8,1,64]{2,1,0:T(1,128)S(1)}, u32[]{:S(2)}, u32[]{:S(2)}) async-start(s32[8,1,64]{2,1,0:T(1,128)} %broadcast_add_fusion), calls=%async_computation | async-start | bytes 8192 | tf_op jit(solution)/shard_map/all_to_all | solution.py:467
  7.7 0.0 copy-start
  7.7 2.3 %copy-done = f32[2,137,32,128]{3,2,1,0:T(8,128)S(1)} copy-done((f32[2,137,32,128]{3,2,1,0:T(8,128)S(1)}, f32[2,137,32,128]{3,2,1,0:T(8,128)}, u32[]{:S(2)}) %copy-start) | copy-done | bytes 4489240
  10.0 0.0 copy-start.7
  10.0 0.0 copy-start.8
  10.0 0.0 copy-start.6
  10.0 1.1 %lay_state.1 = bf16[137,32,256]{2,1,0:T(8,128)(2,1)S(1)} custom-call(f32[8768,128]{1,0:T(8,128)S(1)} %bitcast.22), custom_call_target="tpu_custom_call" | custom-call | bytes 6733824 | tf_op jit(solution)/shard_map/lay_state/pallas_call | solution.py:66
  11.1 1.9 %all-to-all-done = s32[8,1,64]{2,1,0:T(1,128)S(1)} async-done(((s32[8,1,64]{2,1,0:T(1,128)}), s32[8,1,64]{2,1,0:T(1,128)S(1)}, u32[]{:S(2)}, u32[]{:S(2)}) %all-to-all-start) | async-done | bytes 2080 | tf_op jit(solution)/shard_map/all_to_all | solution.py:467
  12.9 0.0 copy-start.2
  12.9 0.0 copy-start.3
  12.9 0.0 copy-start.4
  13.0 1.9 %gather_state.1.after_ref = bf16[128,384]{1,0:T(8,128)(2,1)} custom-call(s32[8,64]{1,0:T(8,128)S(1)} %bitcast.28, bf16[4384,256]{1,0:T(8,128)(2,1)S(1)} %bitcast.21), custom_call_target="tpu_custom_call" | custom-call | flops 287309824 | bytes 2244608 | tf_op jit(solution)/shard_map/gather_state/pallas_call | solution.py:121
  14.9 3.6 %all-to-all-start.1 = ((bf16[8,16,384]{2,1,0:T(8,128)(2,1)}), bf16[8,16,384]{2,1,0:T(8,128)(2,1)S(1)}, u32[]{:S(2)}, u32[]{:S(2)}) async-start(bf16[8,16,384]{2,1,0:T(8,128)(2,1)} %bitcast.9), calls=%async_computation.1 | async-start | bytes 196608 | tf_op jit(solution)/shard_map/all_to_all | solution.py:472
  18.5 0.0 copy-done.7
  18.5 0.1 reshape.106.lon_ref
  18.6 0.0 copy-done.8
  18.6 0.1 reshape.107.lat_ref
  18.7 0.0 copy-done.6
  18.7 0.2 reshape.105.vertical_ref
  18.9 1.0 %plan_points.1 = (bf16[384,512]{1,0:T(8,128)(2,1)S(1)}, s32[1,512]{1,0:T(1,128)S(1)}, bf16[2,144,384]{2,1,0:T(8,128)(2,1)S(1)}, f32[128,384]{1,0:T(8,128)S(1)}, f32[9,384]{1,0:T(8,128)S(1)}) custom-call(s32[8,64]{1,0:T(8,128)S(1)} %bitcast.29, bf16[274,137]{1,0:T(8,128)(2,1)S(1)} %reshape.105.vertical_ref, f32[9,274]{1,0:T(8,128)S(1)} %reshape.106.lon_ref, ...), custom_call_target="tpu_custom_call" | custom-call | flops 2097152 | bytes 393216 | tf_op jit(solution)/shard_map/plan_points/pallas_call | solution.py:479
  19.9 0.0 copy-start.1
  19.9 2.3 %copy-done.1 = bf16[1,64,2,137,128]{4,2,3,1,0:T(2,128)(2,1)S(1)} copy-done((bf16[1,64,2,137,128]{4,2,3,1,0:T(2,128)(2,1)S(1)}, bf16[1,64,2,137,128]{4,2,3,1,0:T(2,128)(2,1)}, u32[]{:S(2)}) %copy-start.1) | copy-done | bytes 4489240
  22.2 0.3 fetch_jacobian.1.jac_ref
  22.6 2.0 %all-to-all-done.1 = bf16[8,16,384]{2,1,0:T(8,128)(2,1)S(1)} async-done(((bf16[8,16,384]{2,1,0:T(8,128)(2,1)}), bf16[8,16,384]{2,1,0:T(8,128)(2,1)S(1)}, u32[]{:S(2)}, u32[]{:S(2)}) %all-to-all-start.1) | async-done | bytes 98336 | tf_op jit(solution)/shard_map/all_to_all | solution.py:472
  24.6 0.0 copy-done.2
  24.6 0.0 copy-done.3
  24.6 0.0 copy-done.4
  24.6 0.0 copy-done.5
  24.6 0.0 slice-start.1
  24.6 2.2 %first_departures.1 = (f32[288,128]{1,0:T(8,128)S(1)}, f32[64,384]{1,0:T(8,128)S(1)}, f32[64,128]{1,0:T(8,128)S(1)}) custom-call(s32[1,64]{1,0:T(1,128)S(1)} %bitcast.33, s32[1,64]{1,0:T(1,128)S(1)} %copy-done.5, bf16[128,384]{1,0:T(8,128)(2,1)S(1)} %bitcast.27, bf16[64,128]{1,0:T(8,128)(2,1)S(1)} %bitcast.31, bf16[64,128]{1,0:T(8,128)(2,1)S(1)} %bitcast.30, ...), custom_call_target="tpu_custom_call" | custom-call | flops 3000000000 | bytes 2244608 | tf_op jit(solution)/shard_map/first_departures/pallas_call | solution.py:245
  26.8 0.0 slice-done
  26.8 0.0 slice-done.1
  26.9 2.6 %last_departures.1 = bf16[8,144,128]{2,1,0:T(8,128)(2,1)} custom-call(f32[64,384]{1,0:T(8,128)S(1)} %get-tuple-element.14.columns_ref, f32[64,128]{1,0:T(8,128)S(1)} %get-tuple-element.15.weight_ref, bf16[64,128]{1,0:T(8,128)(2,1)S(1)} %bitcast.32, bf16[17536,128]{1,0:T(8,128)(2,1)S(1)} %bitcast.26, f32[288,128]{1,0:T(8,128)S(1)} %get-tuple-element.16.before_ref), custom_call_target="tpu_custom_call" | custom-call | flops 3000000000 | bytes 2244608 | tf_op jit(solution)/shard_map/last_departures/pallas_call | solution.py:257
  29.5 3.5 %all-to-all-start.2 = ((bf16[8,144,128]{2,1,0:T(8,128)(2,1)}), bf16[8,144,128]{2,1,0:T(8,128)(2,1)S(1)}, u32[]{:S(2)}, u32[]{:S(2)}) async-start(bf16[8,144,128]{2,1,0:T(8,128)(2,1)} %last_departures.1), calls=%async_computation.2 | async-start | bytes 589824 | tf_op jit(solution)/shard_map/all_to_all | solution.py:513
  32.9 5.9 %collective-permute-start.1 = (s32[1,512]{1,0:T(1,128)S(1)}, s32[1,512]{1,0:T(1,128)S(1)}, u32[]{:S(2)}, u32[]{:S(2)}) collective-permute-start(s32[1,512]{1,0:T(1,128)S(1)} %get-tuple-element.13.after_ref.refs_0_), channel_id=1, source_target_pairs={{1,2},{2,1},{5,6},{6,5},{9,10},{10,9},{13,14},{14,13},{17,18},{18,... | collective-permute-start | bytes 6152 | tf_op jit(solution)/shard_map/ppermute | solution.py:519
  38.8 0.1 collective-permute-start
  38.9 1.2 %collective-permute-done.1.far_ref.refs_4_ = s32[1,512]{1,0:T(1,128)S(1)} collective-permute-done((s32[1,512]{1,0:T(1,128)S(1)}, s32[1,512]{1,0:T(1,128)S(1)}, u32[]{:S(2)}, u32[]{:S(2)}) %collective-permute-start.1) | collective-permute-done | bytes 2080 | tf_op jit(solution)/shard_map/ppermute | solution.py:519
  40.1 0.0 collective-permute-done.near_ref.refs_2_
  40.1 0.2 all-to-all-done.2.products_ref
  40.3 0.4 impact_columns.1.refs_1_
  40.7 6.9 %collective-permute-start.3 = (bf16[144,768]{1,0:T(8,128)(2,1)S(1)}, bf16[144,768]{1,0:T(8,128)(2,1)S(1)}, u32[]{:S(2)}, u32[]{:S(2)}) collective-permute-start(bf16[144,768]{1,0:T(8,128)(2,1)S(1)} %impact_columns.1.refs_1_), channel_id=1, source_target_pairs={{1,2},{2,1},{5,6},{6,5},{9,10},{10,9},{13,14},{14,13},{17,18},{18,... | collective-permute-start | bytes 663560 | tf_op jit(solution)/shard_map/ppermute | solution.py:530
  47.6 0.1 collective-permute-start.2
  47.7 4.4 %inner_rows.1.refs_9_ = f32[274,32,128]{2,1,0:T(8,128)} custom-call(s32[1,512]{1,0:T(1,128)S(1)} %get-tuple-element.13.after_ref.refs_0_, bf16[144,768]{1,0:T(8,128)(2,1)S(1)} %impact_columns.1.refs_1_, bf16[2,144,384]{2,1,0:T(8,128)(2,1)S(1)} %get-tuple-element.18.refs_2_.refs_6_, f32[128,384]{1,0:T(8,128)S(1)} %get-tuple-element.19.refs_3_.refs_7_, ...), custom_call_target="tpu_custom_call" | custom-call | flops 44892160 | bytes 2244608 | tf_op jit(solution)/shard_map/inner_rows/pallas_call | solution.py:547
  52.1 0.0 collective-permute-done.3.refs_5_
  52.1 0.0 collective-permute-done.2.refs_3_
  52.2 5.2 %outer_rows.1 = f32[274,32,128]{2,1,0:T(8,128)} custom-call(s32[1,512]{1,0:T(1,128)S(1)} %get-tuple-element.13.after_ref.refs_0_, bf16[144,768]{1,0:T(8,128)(2,1)S(1)} %impact_columns.1.refs_1_, s32[1,512]{1,0:T(1,128)S(1)} %collective-permute-done.near_ref.refs_2_, ...), custom_call_target="tpu_custom_call", output_to_operand_aliasing={{}: (9, {})} | custom-call | flops 44892160 | bytes 2244608 | tf_op jit(solution)/shard_map/outer_rows/pallas_call | solution.py:547
  (4 shorter events, 0.0 us)
Async XLA Ops:
  1.3 11.6 %all-to-all-start = ((s32[8,1,64]{2,1,0:T(1,128)}), s32[8,1,64]{2,1,0:T(1,128)S(1)}, u32[]{:S(2)}, u32[]{:S(2)}) async-start(s32[8,1,64]{2,1,0:T(1,128)} %broadcast_add_fusion), calls=%async_computation | async-start | bytes 8192 | tf_op jit(solution)/shard_map/all_to_all | solution.py:467
  7.7 2.3 %copy-start = (f32[2,137,32,128]{3,2,1,0:T(8,128)S(1)}, f32[2,137,32,128]{3,2,1,0:T(8,128)}, u32[]{:S(2)}) copy-start(f32[2,137,32,128]{3,2,1,0:T(8,128)} %param.10) | copy-start | bytes 13467652
  10.0 8.5 %copy-start.7 = (f32[2,137,9]{1,0,2:T(2,128)S(1)}, f32[2,137,9]{1,0,2:T(2,128)}, u32[]{:S(2)}) copy-start(f32[2,137,9]{1,0,2:T(2,128)} %param.18) | copy-start | bytes 29596
  10.0 8.6 %copy-start.8 = (f32[2,137,9]{1,0,2:T(2,128)S(1)}, f32[2,137,9]{1,0,2:T(2,128)}, u32[]{:S(2)}) copy-start(f32[2,137,9]{1,0,2:T(2,128)} %param.19) | copy-start | bytes 29596
  10.0 8.7 %copy-start.6 = (bf16[2,137,137]{2,0,1:T(2,128)(2,1)S(1)}, bf16[2,137,137]{2,0,1:T(2,128)(2,1)}, u32[]{:S(2)}) copy-start(bf16[2,137,137]{2,0,1:T(2,128)(2,1)} %param.17) | copy-start | bytes 225232
  12.9 11.6 %copy-start.2 = (bf16[1,64,128]{2,1,0:T(8,128)(2,1)S(1)}, bf16[1,64,128]{2,1,0:T(8,128)(2,1)}, u32[]{:S(2)}) copy-start(bf16[1,64,128]{2,1,0:T(8,128)(2,1)} %param.13) | copy-start | bytes 49156
  12.9 11.6 %copy-start.3 = (bf16[1,64,128]{2,1,0:T(8,128)(2,1)S(1)}, bf16[1,64,128]{2,1,0:T(8,128)(2,1)}, u32[]{:S(2)}) copy-start(bf16[1,64,128]{2,1,0:T(8,128)(2,1)} %param.12) | copy-start | bytes 49156
  12.9 11.6 %copy-start.4 = (s32[1,64,1]{1,2,0:T(1,128)S(1)}, s32[1,64,1]{1,2,0:T(1,128)}, u32[]{:S(2)}) copy-start(s32[1,64,1]{1,2,0:T(1,128)} %param.15) | copy-start | bytes 772
  13.0 11.6 %copy-start.5 = (s32[1,64]{1,0:T(1,128)S(1)}, s32[1,64]{1,0:T(1,128)}, u32[]{:S(2)}) copy-start(s32[1,64]{1,0:T(1,128)} %valid_ref.1) | copy-start | bytes 772
  14.9 9.7 %all-to-all-start.1 = ((bf16[8,16,384]{2,1,0:T(8,128)(2,1)}), bf16[8,16,384]{2,1,0:T(8,128)(2,1)S(1)}, u32[]{:S(2)}, u32[]{:S(2)}) async-start(bf16[8,16,384]{2,1,0:T(8,128)(2,1)} %bitcast.9), calls=%async_computation.1 | async-start | bytes 196608 | tf_op jit(solution)/shard_map/all_to_all | solution.py:472
  19.9 2.3 %copy-start.1 = (bf16[1,64,2,137,128]{4,2,3,1,0:T(2,128)(2,1)S(1)}, bf16[1,64,2,137,128]{4,2,3,1,0:T(2,128)(2,1)}, u32[]{:S(2)}) copy-start(bf16[1,64,2,137,128]{4,2,3,1,0:T(2,128)(2,1)} %param.11) | copy-start | bytes 13467652
  22.2 4.6 %slice-start = ((s8[4489216]{0:T(1024)(128)(4,1)}), s8[294912]{0:T(1024)(128)(4,1)S(1)}, s32[]{:S(2)}) async-start(s8[4489216]{0:T(1024)(128)(4,1)} %bitcast.24), calls=%async_computation.3 | async-start | bytes 589824
  24.6 2.3 %slice-start.1 = ((s8[4489216]{0:T(1024)(128)(4,1)}), s8[4194304]{0:T(1024)(128)(4,1)S(1)}, s32[]{:S(2)}) async-start(s8[4489216]{0:T(1024)(128)(4,1)} %bitcast.24), calls=%async_computation.4 | async-start | bytes 8388608
  29.5 10.8 %all-to-all-start.2 = ((bf16[8,144,128]{2,1,0:T(8,128)(2,1)}), bf16[8,144,128]{2,1,0:T(8,128)(2,1)S(1)}, u32[]{:S(2)}, u32[]{:S(2)}) async-start(bf16[8,144,128]{2,1,0:T(8,128)(2,1)} %last_departures.1), calls=%async_computation.2 | async-start | bytes 589824 | tf_op jit(solution)/shard_map/all_to_all | solution.py:513
  32.9 7.1 %collective-permute-start.1 = (s32[1,512]{1,0:T(1,128)S(1)}, s32[1,512]{1,0:T(1,128)S(1)}, u32[]{:S(2)}, u32[]{:S(2)}) collective-permute-start(s32[1,512]{1,0:T(1,128)S(1)} %get-tuple-element.13.after_ref.refs_0_), channel_id=1, source_target_pairs={{1,2},{2,1},{5,6},{6,5},{9,10},{10,9},{13,14},{14,13},{17,18},{18,... | collective-permute-start | bytes 6152 | tf_op jit(solution)/shard_map/ppermute | solution.py:519
  38.8 1.3 %collective-permute-start = (s32[1,512]{1,0:T(1,128)S(1)}, s32[1,512]{1,0:T(1,128)S(1)}, u32[]{:S(2)}, u32[]{:S(2)}) collective-permute-start(s32[1,512]{1,0:T(1,128)S(1)} %get-tuple-element.13.after_ref.refs_0_), channel_id=1, source_target_pairs={{0,1},{2,3},{1,0},{3,2},{4,5},{6,7},{5,4},{7,6},{8,9},{10,11},{9,8... | collective-permute-start | bytes 6152 | tf_op jit(solution)/shard_map/ppermute | solution.py:518
  40.7 11.4 %collective-permute-start.3 = (bf16[144,768]{1,0:T(8,128)(2,1)S(1)}, bf16[144,768]{1,0:T(8,128)(2,1)S(1)}, u32[]{:S(2)}, u32[]{:S(2)}) collective-permute-start(bf16[144,768]{1,0:T(8,128)(2,1)S(1)} %impact_columns.1.refs_1_), channel_id=1, source_target_pairs={{1,2},{2,1},{5,6},{6,5},{9,10},{10,9},{13,14},{14,13},{17,18},{18,... | collective-permute-start | bytes 663560 | tf_op jit(solution)/shard_map/ppermute | solution.py:530
  47.6 4.5 %collective-permute-start.2 = (bf16[144,768]{1,0:T(8,128)(2,1)S(1)}, bf16[144,768]{1,0:T(8,128)(2,1)S(1)}, u32[]{:S(2)}, u32[]{:S(2)}) collective-permute-start(bf16[144,768]{1,0:T(8,128)(2,1)S(1)} %impact_columns.1.refs_1_), channel_id=1, source_target_pairs={{0,1},{2,3},{1,0},{3,2},{4,5},{6,7},{5,4},{7,6},{8,9},{10,11},{9,8... | collective-permute-start | bytes 663560 | tf_op jit(solution)/shard_map/ppermute | solution.py:529

commit v6 on v5

--- a/solution.py
+++ b/solution.py
@@ -155,19 +155,8 @@
     )(array, after)
 
 
-def first_departures(capacity, group, features, dest_ref, valid_ref, states_ref, obs_ref, inv_ref, jac_ref, after_ref, total_ref, columns_ref, weight_ref):
-    records = dest_ref.shape[1]
-    slots = states_ref.shape[0]
-    channels = jac_ref.shape[1]
-    dest = to_column(dest_ref[...])
-    named = (dest == lane_iota((records, LANES))).astype(F32)
-    before = jnp.dot(earlier_rows(records), named.astype(BF16), preferred_element_type=F32)
-    rank = jnp.sum(before * named, axis=1, keepdims=True).astype(jnp.int32)
-    chosen = (dest * capacity + rank == lane_iota((records, slots))).astype(F32).astype(BF16)
-    columns = jnp.dot(chosen, states_ref[...], preferred_element_type=F32)
-    alive = lane_iota((records, channels)) < to_column(valid_ref[...])
-    columns_ref[...] = columns
-    weight_ref[...] = jnp.where(alive, inv_ref[...].astype(F32), 0.0)
+def first_departures(group, features, chosen_ref, states_ref, weight_ref, obs_ref, jac_ref, after_ref, total_ref, columns_ref):
+    columns_ref[...] = jnp.dot(chosen_ref[...], states_ref[...], preferred_element_type=F32)
     total_ref[...] = jnp.zeros_like(total_ref)
     product_groups(group, features, 0, columns_ref, weight_ref, obs_ref, jac_ref, total_ref)
 
@@ -192,6 +181,7 @@
     reach = pl.cdiv(skip * (part - 1) + features, LANES)
     row = row_iota((group, LANES))
     index = jnp.bitwise_and(row, part - 1)
+    lows = {}
     for g in range(done, jac_ref.shape[0] // (group * features)):
         first = g * group * features
         mine = columns_ref[g * group : (g + 1) * group, :]
@@ -216,7 +206,9 @@
         model = jnp.where(row < part, both[:, :channels], both[:, channels:])
         own = slice(g * group, (g + 1) * group)
         misfit = weight_ref[own, :] * (model - obs_ref[own, :].astype(F32))
-        low = misfit.astype(BF16).astype(F32)
+        lows[g] = misfit.astype(BF16).astype(F32)
+    for g, low in lows.items():
+        first = g * group * features
         for r in range(part):
             against = jnp.concatenate([jnp.where(row == r, low, 0.0), jnp.where(row == r + part, low, 0.0)], axis=1)
             start = first + r * features
@@ -234,7 +226,7 @@
         total[0:features, g * group : (g + 1) * group] = sums
 
 
-def departures(dest, valid, states, obs, inv, jac, after, capacity, devices, tall):
+def departures(chosen, states, weight, obs, jac, after, devices, tall):
     records, channels = obs.shape
     features = jac.shape[0] // records
     group = 16
@@ -242,18 +234,17 @@
     vmem, anywhere = pl.BlockSpec(memory_space=pltpu.VMEM), pl.BlockSpec(memory_space=pl.ANY)
     params = pltpu.CompilerParams(vmem_limit_bytes=16 * 1024 * 1024)
     cost = pl.CostEstimate(flops=3_000_000_000, bytes_accessed=jac.size, transcendentals=0)
-    total, columns, weight = pl.pallas_call(
-        functools.partial(first_departures, capacity, group, features),
-        in_specs=[vmem] * 6 + [anywhere],
+    total, columns = pl.pallas_call(
+        functools.partial(first_departures, group, features),
+        in_specs=[vmem] * 5 + [anywhere],
         out_shape=(
             jax.ShapeDtypeStruct((2 * tall, 2 * records), F32),
             jax.ShapeDtypeStruct((records, states.shape[1]), F32),
-            jax.ShapeDtypeStruct((records, channels), F32),
         ),
         compiler_params=params,
         cost_estimate=cost,
         name="first_departures",
-    )(dest, valid, states, obs, inv, fetch(jac, after, done * group * features), after)
+    )(chosen, states, weight, obs, fetch(jac, after, done * group * features), after)
     return pl.pallas_call(
         functools.partial(last_departures, group, features, done),
         in_specs=[vmem] * 5,
@@ -276,7 +267,7 @@
     return jnp.where(key == NOWHERE, NOWHERE, key + row * STRIDE)
 
 
-def plan_kernel(records, points, reach, codes_ref, vertical_ref, lon_ref, lat_ref, after_ref, same_ref, info_ref, mixing_ref, table_ref, taps_ref, down, first):
+def plan_kernel(records, points, reach, capacity, codes_ref, dest_ref, valid_ref, inv_ref, vertical_ref, lon_ref, lat_ref, after_ref, chosen_ref, weight_ref, same_ref, info_ref, mixing_ref, table_ref, taps_ref, down, first):
     count = codes_ref.shape[0]
     span, listed = count * records, same_ref.shape[0]
     tile, column = split_codes(codes_ref, records, points)
@@ -316,6 +307,14 @@
     starts = jnp.where(down[...] < lane_iota((span, LANES)) * STRIDE, first[...], 0.0)
     info_ref[0:1, listed:] = jnp.sum(starts, axis=0, keepdims=True).astype(jnp.int32)
 
+    dest = to_column(dest_ref[...])
+    named = (dest == lane_iota((records, LANES))).astype(F32)
+    before = jnp.dot(earlier_rows(records), named.astype(BF16), preferred_element_type=F32)
+    rank = jnp.sum(before * named, axis=1, keepdims=True).astype(jnp.int32)
+    chosen_ref[...] = (dest * capacity + rank == lane_iota(chosen_ref.shape)).astype(F32).astype(BF16)
+    alive = lane_iota(weight_ref.shape) < to_column(valid_ref[...])
+    weight_ref[...] = jnp.where(alive, inv_ref[...].astype(F32), 0.0)
+
     features, levels = vertical_ref.shape
     wide = mixing_ref.shape[2]
     tall = mixing_ref.shape[1]
@@ -462,8 +461,10 @@
         span = records * lon_devices
         tall = pl.cdiv(features, 32) * 16
 
-        codes = destination.reshape(1, 1, records) * points + column.reshape(1, 1, records)
-        codes = codes + lax.broadcasted_iota(jnp.int32, (lon_devices, 1, records), 0) * NOWHERE
+        told = (lon_devices, 1, records)
+        codes = lax.broadcasted_iota(jnp.int32, told, 0) * (NOWHERE // points)
+        codes = (codes + jnp.broadcast_to(destination.reshape(1, 1, records), told)) * points
+        codes = codes + jnp.broadcast_to(column.reshape(1, 1, records), told)
         codes = lax.all_to_all(codes, "lon", split_axis=0, concat_axis=0, tiled=True)
         codes = codes.reshape(lon_devices, records)
         laid = lay_state(state_field)
@@ -476,10 +477,12 @@
         wide = pl.cdiv(features, LANES) * LANES
         taps = lon_taps.shape[-1]
         vmem, anywhere = pl.BlockSpec(memory_space=pltpu.VMEM), pl.BlockSpec(memory_space=pl.ANY)
-        same, info, mixing, lon_table, lat_flat = pl.pallas_call(
-            functools.partial(plan_kernel, records, points, reach),
-            in_specs=[vmem] * 4 + [anywhere],
+        chosen, weight, same, info, mixing, lon_table, lat_flat = pl.pallas_call(
+            functools.partial(plan_kernel, records, points, reach, capacity),
+            in_specs=[vmem] * 7 + [anywhere],
             out_shape=(
+                jax.ShapeDtypeStruct((records, lon_devices * capacity), BF16),
+                jax.ShapeDtypeStruct((records, channels), F32),
                 jax.ShapeDtypeStruct((listed, span), BF16),
                 jax.ShapeDtypeStruct((1, listed + LANES), jnp.int32),
                 jax.ShapeDtypeStruct((2, tall, wide), BF16),
@@ -492,6 +495,9 @@
             name="plan_points",
         )(
             codes,
+            destination.reshape(1, records),
+            valid_count.reshape(1, records),
+            inverse_var.reshape(records, channels),
             jnp.swapaxes(vertical, 0, 1).reshape(features, levels),
             jnp.moveaxis(lon_taps, 2, 0).reshape(taps, features),
             jnp.moveaxis(lat_taps, 2, 0).reshape(taps, features),
@@ -499,14 +505,12 @@
         )
         own = jnp.swapaxes(jacobian.reshape(records, variables, levels, channels), 1, 2).reshape(-1, channels)
         products = departures(
-            destination.reshape(1, records),
-            valid_count.reshape(1, records),
+            chosen,
             found_in.reshape(lon_devices * capacity, found.shape[-1]),
+            weight,
             observed.reshape(records, channels),
-            inverse_var.reshape(records, channels),
             own,
             info,
-            capacity,
             lon_devices,
             tall,
         )

time: 58 us -> 57.5 us (level)
  Pallas kernels: 19.3 us -> 18.4 us
  local copies, waits for them, and re-layouts: 4.95 us -> 5.55 us
    unnamed x22, local copies, waits for them, and re-layouts: 4.57 us -> 5.17 us
    add x2 -> x1, other arithmetic: 1.34 us -> 1.33 us  [body(): codes = codes + jnp.broadcast_to(column.reshape(1, 1, records), told)]
where the time goes in v6:
time: 57.5 us; the launch traced here: 56.9 us
  starting transfers between devices  26.2 us (46%)
  Pallas kernels  18.4 us (32%)
  local copies, waits for them, and re-layouts  5.55 us (10%)
  waiting for transfers between devices  5.27 us (9%)
  other arithmetic  1.34 us (2%)
    pallas_call x2, Pallas kernels, filtered(): pl.pallas_call(kernel, grid=(steps,), in_specs=held, out_specs=pl.BlockSp...  9.65 us
    ppermute x1, starting transfers between devices, body(): impact_far = lax.ppermute(impact, 'lat', swaps[1])  6.76 us
    all_to_all x1, starting transfers between devices, body(): lax.all_to_all(codes, 'lon', split_axis=0, concat_axis=0, tiled=True)  6.35 us
    ppermute x1, starting transfers between devices, body(): info_far = lax.ppermute(info, 'lat', swaps[1])  5.72 us
    unnamed x22, local copies, waits for them, and re-layouts  5.17 us
    all_to_all x1, starting transfers between devices, body(): lax.all_to_all(found.reshape(lon_devices, capacity, found.shape[-1]), 'lo...  3.63 us
    all_to_all x1, starting transfers between devices, body(): lax.all_to_all(products, 'lon', split_axis=0, concat_axis=0, tiled=True)  3.57 us
    pallas_call x1, Pallas kernels, departures(): pl.pallas_call(functools.partial(last_departures, group, features, done),...  2.25 us
  transfers between devices with their start and end apart: 7, of which 4 were waited for; matrix products, arithmetic and copies ran while one was open for 1% of the time, Pallas kernels for 12%

profile of v6, /device:TPU:1, one launch (start us, length us, event | category | flops | bytes accessed | tf_op | source)
XLA Modules:
  0.0 56.9 jit_solution(16145184748244666106)
XLA Ops:
  0.0 1.3 %multiply_add_fusion = s32[8,1,64]{2,0,1:T(8,128)} fusion(s32[64]{0:T(128)} %bitcast.37, s32[64]{0:T(128)} %bitcast.30, s32[8]{0:T(128)S(1)} %iota_multiply_fusion), kind=kLoop, calls=%fused_computation | loop fusion | flops 1536 | bytes 2592 | tf_op jit(solution)/shard_map/add | solution.py:467
  1.3 6.4 %all-to-all-start = ((s32[8,1,64]{2,1,0:T(1,128)}), s32[8,1,64]{2,1,0:T(1,128)S(1)}, u32[]{:S(2)}, u32[]{:S(2)}) async-start(s32[8,1,64]{2,1,0:T(1,128)} %bitcast.2), calls=%async_computation | async-start | bytes 8192 | tf_op jit(solution)/shard_map/all_to_all | solution.py:468
  7.7 0.0 copy-start
  7.7 2.3 %copy-done = f32[2,137,32,128]{3,2,1,0:T(8,128)S(1)} copy-done((f32[2,137,32,128]{3,2,1,0:T(8,128)S(1)}, f32[2,137,32,128]{3,2,1,0:T(8,128)}, u32[]{:S(2)}) %copy-start) | copy-done | bytes 4489240
  10.0 0.0 copy-start.7
  10.0 0.0 copy-start.8
  10.0 0.0 copy-start.6
  10.0 0.0 copy-start.2
  10.0 0.0 copy-start.3
  10.0 0.0 copy-start.4
  10.0 1.1 %lay_state.1 = bf16[137,32,256]{2,1,0:T(8,128)(2,1)S(1)} custom-call(f32[8768,128]{1,0:T(8,128)S(1)} %bitcast.21), custom_call_target="tpu_custom_call" | custom-call | bytes 6733824 | tf_op jit(solution)/shard_map/lay_state/pallas_call | solution.py:66
  11.1 1.8 %all-to-all-done = s32[8,1,64]{2,1,0:T(1,128)S(1)} async-done(((s32[8,1,64]{2,1,0:T(1,128)}), s32[8,1,64]{2,1,0:T(1,128)S(1)}, u32[]{:S(2)}, u32[]{:S(2)}) %all-to-all-start) | async-done | bytes 2080 | tf_op jit(solution)/shard_map/all_to_all | solution.py:468
  12.9 0.0 copy-start.5
  12.9 1.9 %gather_state.1.after_ref = bf16[128,384]{1,0:T(8,128)(2,1)} custom-call(s32[8,64]{1,0:T(8,128)S(1)} %bitcast.27, bf16[4384,256]{1,0:T(8,128)(2,1)S(1)} %bitcast.20), custom_call_target="tpu_custom_call" | custom-call | flops 287309824 | bytes 2244608 | tf_op jit(solution)/shard_map/gather_state/pallas_call | solution.py:121
  14.9 3.6 %all-to-all-start.1 = ((bf16[8,16,384]{2,1,0:T(8,128)(2,1)}), bf16[8,16,384]{2,1,0:T(8,128)(2,1)S(1)}, u32[]{:S(2)}, u32[]{:S(2)}) async-start(bf16[8,16,384]{2,1,0:T(8,128)(2,1)} %bitcast.11), calls=%async_computation.1 | async-start | bytes 196608 | tf_op jit(solution)/shard_map/all_to_all | solution.py:473
  18.5 0.0 copy-done.7
  18.5 0.1 reshape.134.lon_ref
  18.6 0.0 copy-done.8
  18.6 0.1 reshape.135.lat_ref
  18.7 0.0 copy-done.6
  18.7 0.2 reshape.133.vertical_ref
  18.9 0.0 copy-done.2
  18.9 0.0 copy-done.3
  18.9 0.0 copy-done.4
  18.9 1.1 %plan_points.1 = (bf16[64,128]{1,0:T(8,128)(2,1)S(1)}, f32[64,128]{1,0:T(8,128)S(1)}, bf16[384,512]{1,0:T(8,128)(2,1)S(1)}, s32[1,512]{1,0:T(1,128)S(1)}, bf16[2...) custom-call(s32[8,64]{1,0:T(8,128)S(1)} %bitcast.28, s32[1,64]{1,0:T(1,128)S(1)} %bitcast.31, ...), custom_call_target="tpu_custom_call" | custom-call | flops 2097152 | bytes 393216 | tf_op jit(solution)/shard_map/plan_points/pallas_call | solution.py:480
  20.0 0.0 copy-start.1
  20.0 2.3 %copy-done.1 = bf16[1,64,2,137,128]{4,2,3,1,0:T(2,128)(2,1)S(1)} copy-done((bf16[1,64,2,137,128]{4,2,3,1,0:T(2,128)(2,1)S(1)}, bf16[1,64,2,137,128]{4,2,3,1,0:T(2,128)(2,1)}, u32[]{:S(2)}) %copy-start.1) | copy-done | bytes 4489240
  22.3 0.0 slice-start
  22.3 0.3 fetch_jacobian.1.jac_ref
  22.7 1.9 %all-to-all-done.1 = bf16[8,16,384]{2,1,0:T(8,128)(2,1)S(1)} async-done(((bf16[8,16,384]{2,1,0:T(8,128)(2,1)}), bf16[8,16,384]{2,1,0:T(8,128)(2,1)S(1)}, u32[]{:S(2)}, u32[]{:S(2)}) %all-to-all-start.1) | async-done | bytes 98336 | tf_op jit(solution)/shard_map/all_to_all | solution.py:473
  24.6 0.0 copy-done.5
  24.6 1.6 %first_departures.1 = (f32[288,128]{1,0:T(8,128)S(1)}, f32[64,384]{1,0:T(8,128)S(1)}) custom-call(bf16[64,128]{1,0:T(8,128)(2,1)S(1)} %get-tuple-element.15.chosen_ref, bf16[128,384]{1,0:T(8,128)(2,1)S(1)} %bitcast.26, f32[64,128]{1,0:T(8,128)S(1)} %get-tuple-element.16.weight_ref, bf16[64,128]{1,0:T(8,128)(2,1)S(1)} %bitcast.32, ...), custom_call_target="tpu_custom_call" | custom-call | flops 3000000000 | bytes 2244608 | tf_op jit(solution)/shard_map/first_departures/pallas_call | solution.py:237
  26.1 0.0 slice-done
  26.2 0.6 %slice-done.1 = s8[4194304]{0:T(1024)(128)(4,1)S(1)} async-done(((s8[4489216]{0:T(1024)(128)(4,1)}), s8[4194304]{0:T(1024)(128)(4,1)S(1)}, s32[]{:S(2)}) %slice-start.1) | async-done | bytes 4194328
  26.8 2.2 %last_departures.1 = bf16[8,144,128]{2,1,0:T(8,128)(2,1)} custom-call(f32[64,384]{1,0:T(8,128)S(1)} %get-tuple-element.17.columns_ref, f32[64,128]{1,0:T(8,128)S(1)} %get-tuple-element.16.weight_ref, bf16[64,128]{1,0:T(8,128)(2,1)S(1)} %bitcast.33, bf16[17536,128]{1,0:T(8,128)(2,1)S(1)} %bitcast.25, f32[288,128]{1,0:T(8,128)S(1)} %get-tuple-element.18.before_ref), custom_call_target="tpu_custom_call" | custom-call | flops 3000000000 | bytes 2244608 | tf_op jit(solution)/shard_map/last_departures/pallas_call | solution.py:248
  29.0 3.6 %all-to-all-start.2 = ((bf16[8,144,128]{2,1,0:T(8,128)(2,1)}), bf16[8,144,128]{2,1,0:T(8,128)(2,1)S(1)}, u32[]{:S(2)}, u32[]{:S(2)}) async-start(bf16[8,144,128]{2,1,0:T(8,128)(2,1)} %last_departures.1), calls=%async_computation.2 | async-start | bytes 589824 | tf_op jit(solution)/shard_map/all_to_all | solution.py:517
  32.6 5.7 %collective-permute-start.1 = (s32[1,512]{1,0:T(1,128)S(1)}, s32[1,512]{1,0:T(1,128)S(1)}, u32[]{:S(2)}, u32[]{:S(2)}) collective-permute-start(s32[1,512]{1,0:T(1,128)S(1)} %get-tuple-element.14.after_ref.refs_0_), channel_id=1, source_target_pairs={{1,2},{2,1},{5,6},{6,5},{9,10},{10,9},{13,14},{14,13},{17,18},{18,... | collective-permute-start | bytes 6152 | tf_op jit(solution)/shard_map/ppermute | solution.py:523
  38.3 0.1 collective-permute-start
  38.4 1.3 %collective-permute-done.1.far_ref.refs_4_ = s32[1,512]{1,0:T(1,128)S(1)} collective-permute-done((s32[1,512]{1,0:T(1,128)S(1)}, s32[1,512]{1,0:T(1,128)S(1)}, u32[]{:S(2)}, u32[]{:S(2)}) %collective-permute-start.1) | collective-permute-done | bytes 2080 | tf_op jit(solution)/shard_map/ppermute | solution.py:523
  39.7 0.0 collective-permute-done.near_ref.refs_2_
  39.7 0.3 all-to-all-done.2.products_ref
  39.9 0.4 impact_columns.1.refs_1_
  40.3 6.8 %collective-permute-start.3 = (bf16[144,768]{1,0:T(8,128)(2,1)S(1)}, bf16[144,768]{1,0:T(8,128)(2,1)S(1)}, u32[]{:S(2)}, u32[]{:S(2)}) collective-permute-start(bf16[144,768]{1,0:T(8,128)(2,1)S(1)} %impact_columns.1.refs_1_), channel_id=1, source_target_pairs={{1,2},{2,1},{5,6},{6,5},{9,10},{10,9},{13,14},{14,13},{17,18},{18,... | collective-permute-start | bytes 663560 | tf_op jit(solution)/shard_map/ppermute | solution.py:534
  47.1 0.1 collective-permute-start.2
  47.2 4.5 %inner_rows.1.refs_9_ = f32[274,32,128]{2,1,0:T(8,128)} custom-call(s32[1,512]{1,0:T(1,128)S(1)} %get-tuple-element.14.after_ref.refs_0_, bf16[144,768]{1,0:T(8,128)(2,1)S(1)} %impact_columns.1.refs_1_, bf16[2,144,384]{2,1,0:T(8,128)(2,1)S(1)} %get-tuple-element.20.refs_2_.refs_6_, f32[128,384]{1,0:T(8,128)S(1)} %get-tuple-element.21.refs_3_.refs_7_, ...), custom_call_target="tpu_custom_call" | custom-call | flops 44892160 | bytes 2244608 | tf_op jit(solution)/shard_map/inner_rows/pallas_call | solution.py:551
  51.7 0.0 collective-permute-done.3.refs_5_
  51.7 0.0 collective-permute-done.2.refs_3_
  51.7 5.2 %outer_rows.1 = f32[274,32,128]{2,1,0:T(8,128)} custom-call(s32[1,512]{1,0:T(1,128)S(1)} %get-tuple-element.14.after_ref.refs_0_, bf16[144,768]{1,0:T(8,128)(2,1)S(1)} %impact_columns.1.refs_1_, s32[1,512]{1,0:T(1,128)S(1)} %collective-permute-done.near_ref.refs_2_, ...), custom_call_target="tpu_custom_call", output_to_operand_aliasing={{}: (9, {})} | custom-call | flops 44892160 | bytes 2244608 | tf_op jit(solution)/shard_map/outer_rows/pallas_call | solution.py:551
  (3 shorter events, 0.0 us)
Async XLA Ops:
  1.3 11.6 %all-to-all-start = ((s32[8,1,64]{2,1,0:T(1,128)}), s32[8,1,64]{2,1,0:T(1,128)S(1)}, u32[]{:S(2)}, u32[]{:S(2)}) async-start(s32[8,1,64]{2,1,0:T(1,128)} %bitcast.2), calls=%async_computation | async-start | bytes 8192 | tf_op jit(solution)/shard_map/all_to_all | solution.py:468
  7.7 2.3 %copy-start = (f32[2,137,32,128]{3,2,1,0:T(8,128)S(1)}, f32[2,137,32,128]{3,2,1,0:T(8,128)}, u32[]{:S(2)}) copy-start(f32[2,137,32,128]{3,2,1,0:T(8,128)} %param.10) | copy-start | bytes 13467652
  10.0 8.5 %copy-start.7 = (f32[2,137,9]{1,0,2:T(2,128)S(1)}, f32[2,137,9]{1,0,2:T(2,128)}, u32[]{:S(2)}) copy-start(f32[2,137,9]{1,0,2:T(2,128)} %param.18) | copy-start | bytes 29596
  10.0 8.6 %copy-start.8 = (f32[2,137,9]{1,0,2:T(2,128)S(1)}, f32[2,137,9]{1,0,2:T(2,128)}, u32[]{:S(2)}) copy-start(f32[2,137,9]{1,0,2:T(2,128)} %param.19) | copy-start | bytes 29596
  10.0 8.7 %copy-start.6 = (bf16[2,137,137]{2,0,1:T(2,128)(2,1)S(1)}, bf16[2,137,137]{2,0,1:T(2,128)(2,1)}, u32[]{:S(2)}) copy-start(bf16[2,137,137]{2,0,1:T(2,128)(2,1)} %param.17) | copy-start | bytes 225232
  10.0 8.9 %copy-start.2 = (bf16[1,64,128]{2,1,0:T(8,128)(2,1)S(1)}, bf16[1,64,128]{2,1,0:T(8,128)(2,1)}, u32[]{:S(2)}) copy-start(bf16[1,64,128]{2,1,0:T(8,128)(2,1)} %param.13) | copy-start | bytes 49156
  10.0 8.9 %copy-start.3 = (s32[1,64,1]{1,2,0:T(1,128)S(1)}, s32[1,64,1]{1,2,0:T(1,128)}, u32[]{:S(2)}) copy-start(s32[1,64,1]{1,2,0:T(1,128)} %param.15) | copy-start | bytes 772
  10.0 8.9 %copy-start.4 = (s32[1,64]{1,0:T(1,128)S(1)}, s32[1,64]{1,0:T(1,128)}, u32[]{:S(2)}) copy-start(s32[1,64]{1,0:T(1,128)} %valid_ref.1) | copy-start | bytes 772
  12.9 11.6 %copy-start.5 = (bf16[1,64,128]{2,1,0:T(8,128)(2,1)S(1)}, bf16[1,64,128]{2,1,0:T(8,128)(2,1)}, u32[]{:S(2)}) copy-start(bf16[1,64,128]{2,1,0:T(8,128)(2,1)} %param.12) | copy-start | bytes 49156
  14.9 9.7 %all-to-all-start.1 = ((bf16[8,16,384]{2,1,0:T(8,128)(2,1)}), bf16[8,16,384]{2,1,0:T(8,128)(2,1)S(1)}, u32[]{:S(2)}, u32[]{:S(2)}) async-start(bf16[8,16,384]{2,1,0:T(8,128)(2,1)} %bitcast.11), calls=%async_computation.1 | async-start | bytes 196608 | tf_op jit(solution)/shard_map/all_to_all | solution.py:473
  20.0 2.3 %copy-start.1 = (bf16[1,64,2,137,128]{4,2,3,1,0:T(2,128)(2,1)S(1)}, bf16[1,64,2,137,128]{4,2,3,1,0:T(2,128)(2,1)}, u32[]{:S(2)}) copy-start(bf16[1,64,2,137,128]{4,2,3,1,0:T(2,128)(2,1)} %param.11) | copy-start | bytes 13467652
  22.3 3.8 %slice-start = ((s8[4489216]{0:T(1024)(128)(4,1)}), s8[294912]{0:T(1024)(128)(4,1)S(1)}, s32[]{:S(2)}) async-start(s8[4489216]{0:T(1024)(128)(4,1)} %bitcast.23), calls=%async_computation.3 | async-start | bytes 589824
  24.6 2.2 %slice-start.1 = ((s8[4489216]{0:T(1024)(128)(4,1)}), s8[4194304]{0:T(1024)(128)(4,1)S(1)}, s32[]{:S(2)}) async-start(s8[4489216]{0:T(1024)(128)(4,1)} %bitcast.23), calls=%async_computation.4 | async-start | bytes 8388608
  29.0 10.9 %all-to-all-start.2 = ((bf16[8,144,128]{2,1,0:T(8,128)(2,1)}), bf16[8,144,128]{2,1,0:T(8,128)(2,1)S(1)}, u32[]{:S(2)}, u32[]{:S(2)}) async-start(bf16[8,144,128]{2,1,0:T(8,128)(2,1)} %last_departures.1), calls=%async_computation.2 | async-start | bytes 589824 | tf_op jit(solution)/shard_map/all_to_all | solution.py:517
  32.6 7.1 %collective-permute-start.1 = (s32[1,512]{1,0:T(1,128)S(1)}, s32[1,512]{1,0:T(1,128)S(1)}, u32[]{:S(2)}, u32[]{:S(2)}) collective-permute-start(s32[1,512]{1,0:T(1,128)S(1)} %get-tuple-element.14.after_ref.refs_0_), channel_id=1, source_target_pairs={{1,2},{2,1},{5,6},{6,5},{9,10},{10,9},{13,14},{14,13},{17,18},{18,... | collective-permute-start | bytes 6152 | tf_op jit(solution)/shard_map/ppermute | solution.py:523
  38.3 1.4 %collective-permute-start = (s32[1,512]{1,0:T(1,128)S(1)}, s32[1,512]{1,0:T(1,128)S(1)}, u32[]{:S(2)}, u32[]{:S(2)}) collective-permute-start(s32[1,512]{1,0:T(1,128)S(1)} %get-tuple-element.14.after_ref.refs_0_), channel_id=1, source_target_pairs={{0,1},{2,3},{1,0},{3,2},{4,5},{6,7},{5,4},{7,6},{8,9},{10,11},{9,8... | collective-permute-start | bytes 6152 | tf_op jit(solution)/shard_map/ppermute | solution.py:522
  40.3 11.3 %collective-permute-start.3 = (bf16[144,768]{1,0:T(8,128)(2,1)S(1)}, bf16[144,768]{1,0:T(8,128)(2,1)S(1)}, u32[]{:S(2)}, u32[]{:S(2)}) collective-permute-start(bf16[144,768]{1,0:T(8,128)(2,1)S(1)} %impact_columns.1.refs_1_), channel_id=1, source_target_pairs={{1,2},{2,1},{5,6},{6,5},{9,10},{10,9},{13,14},{14,13},{17,18},{18,... | collective-permute-start | bytes 663560 | tf_op jit(solution)/shard_map/ppermute | solution.py:534
  47.1 4.6 %collective-permute-start.2 = (bf16[144,768]{1,0:T(8,128)(2,1)S(1)}, bf16[144,768]{1,0:T(8,128)(2,1)S(1)}, u32[]{:S(2)}, u32[]{:S(2)}) collective-permute-start(bf16[144,768]{1,0:T(8,128)(2,1)S(1)} %impact_columns.1.refs_1_), channel_id=1, source_target_pairs={{0,1},{2,3},{1,0},{3,2},{4,5},{6,7},{5,4},{7,6},{8,9},{10,11},{9,8... | collective-permute-start | bytes 663560 | tf_op jit(solution)/shard_map/ppermute | solution.py:533

commit v7 on v6

--- a/solution.py
+++ b/solution.py
@@ -267,6 +267,12 @@
     return jnp.where(key == NOWHERE, NOWHERE, key + row * STRIDE)
 
 
+def twice(array, features):
+    left = features % LANES
+    lane = lane_iota(array.shape)
+    return jnp.where((lane >= features) & (lane < features + left), pltpu.roll(array, left, 1), array)
+
+
 def plan_kernel(records, points, reach, capacity, codes_ref, dest_ref, valid_ref, inv_ref, vertical_ref, lon_ref, lat_ref, after_ref, chosen_ref, weight_ref, same_ref, info_ref, mixing_ref, table_ref, taps_ref, down, first):
     count = codes_ref.shape[0]
     span, listed = count * records, same_ref.shape[0]
@@ -324,15 +330,16 @@
     spread = rows
     for v in range(1, variables):
         spread = jnp.where(row_iota(rows.shape) % variables == v, pltpu.roll(rows, v * levels, 1), spread)
+    spread = twice(spread, features)
     mixing_ref[0] = spread[:tall].astype(BF16)
     mixing_ref[1, 0 : features - tall, :] = spread[tall:].astype(BF16)
     taps = lon_ref.shape[0]
     spare = jnp.zeros((taps, wide - features), F32)
-    lon = jnp.concatenate([lon_ref[...], spare], axis=1)
+    lon = twice(jnp.concatenate([lon_ref[...], spare], axis=1), features)
     lon = jnp.concatenate([lon[k : k + 1] for k in reversed(range(taps))] + [jnp.zeros((16 - taps, wide), F32)], axis=0)
     for b in range(8):
         table_ref[16 * b : 16 * (b + 1), :] = pltpu.roll(lon, b, 0) if b else lon
-    taps_ref[...] = jnp.concatenate([lat_ref[...], spare], axis=1)
+    taps_ref[...] = twice(jnp.concatenate([lat_ref[...], spare], axis=1), features)
 
 
 def impact_kernel(records, products_ref, same_ref, near_ref, far_ref, out_ref, terms):
@@ -352,20 +359,29 @@
         ).astype(BF16)
 
 
-def filter_kernel(block_of, reach, rows, *refs):
-    (*lists, vertical_ref, lon_ref, lat_ref, out_ref, mixed, along, mean, ready, sent) = refs
+def filter_kernel(block_of, reach, rows, steps, inner, *refs):
+    if inner:
+        (*lists, vertical_ref, lon_ref, lat_ref, ready, mixed, along, mean) = refs
+    else:
+        (*lists, vertical_ref, lon_ref, lat_ref, inner_ref, out_ref, mixed, along, mean, ready, sent) = refs
     lists = [(lists[n], lists[n + 1]) for n in range(0, len(lists) // 2 * 2, 2)]
     listed = lists[0][1].shape[1] // vertical_ref.shape[0]
-    features = out_ref.shape[0]
+    features = ready.shape[0]
     wide = vertical_ref.shape[2]
-    height = ready.shape[2]
+    height = ready.shape[1] // steps
     window = height + 2 * reach
     pitch = along.shape[0] // window
     step = pl.program_id(0)
     base = block_of(step) * height - reach
 
+    def leave_inner():
+        there = pl.ds(height, inner_ref.shape[1])
+        return pltpu.make_async_copy(inner_ref, out_ref.at[:, there], sent.at[steps, 0])
+
     @pl.when(step == 0)
     def _():
+        if not inner:
+            leave_inner().start()
         along[...] = jnp.zeros_like(along)
         for n, (info, impact) in enumerate(lists):
             for part in range(0, listed, LANES):
@@ -382,6 +398,10 @@
                         )
                     mixed[n * listed + part : n * listed + part + LANES, :] = total
 
+    full, left = divmod(features, LANES)
+    lane = lane_iota((1, wide)) - full * LANES
+    mine = (lane < 0) | ((lane >= step * left) & (lane < (step + 1) * left))
+    mine = jnp.where(mine, 1.0, 0.0)
     for n, (info, _) in enumerate(lists):
         offset = -base
         if n:
@@ -404,7 +424,7 @@
                 spot = jnp.bitwise_and(place, 7)
                 at = pl.ds(pl.multiple_of(row * pitch + place - spot, 8), 16)
                 taps = lon_ref[pl.ds(pl.multiple_of(spot * 16, 16), 16), :]
-                column = mixed[pl.ds(n * listed + here, 1), :] * jnp.where(live, 1.0, 0.0)
+                column = mixed[pl.ds(n * listed + here, 1), :] * jnp.where(live, mine, 0.0)
                 pieces.append((at, taps * column))
             for at, piece in pieces:
                 along[at, :] += piece
@@ -412,40 +432,56 @@
 
         lax.fori_loop(0, lax.div(stop - start + SOME - 1, SOME), add_some, 0)
 
-    flat = ready.reshape(ready.shape[0] * features * height, LANES)
+    tall = steps * height
+    flat = ready.reshape(features * tall, LANES)
 
     def leave(at, t):
         here = pl.ds(t * LANES, min(LANES, features - t * LANES))
+        mine = pl.ds(pl.multiple_of(at * height, height), height)
         there = pl.ds(pl.multiple_of(block_of(at) * height, height), height)
-        return pltpu.make_async_copy(ready.at[at, here], out_ref.at[here, there], sent.at[at, t])
-
-    for t in range(wide // LANES):
+        return pltpu.make_async_copy(ready.at[here, mine], out_ref.at[here, there], sent.at[at, t])
+
+    def smooth(t, again):
         here = slice(t * LANES, (t + 1) * LANES)
         lat = [jnp.broadcast_to(lat_ref[k : k + 1, here], (8, LANES)) for k in range(2 * reach + 1)]
-
         for j in range(LANES // 8):
             sums = [None] * height
             for w in range(window):
                 spot = pl.ds(w * pitch + 8 + j * 8, 8)
                 part = along[spot, here]
-                along[spot, here] = jnp.zeros_like(part)
+                if again:
+                    along[spot, here] = jnp.zeros_like(part)
                 for row in range(max(0, w - 2 * reach), min(height, w + 1)):
                     term = lat[w - row] * part
                     sums[row] = term if sums[row] is None else sums[row] + term
             for row in range(height):
                 mean[t % 2, row, j * 8 : (j + 1) * 8, :] = sums[row]
 
-        kept = min(LANES, features - t * LANES)
+    for t in range(full):
+        smooth(t, True)
         for row in range(height):
-            turned = jnp.transpose(mean[t % 2, row])
-            flat[pl.ds((step * features + t * LANES) * height + row, kept, stride=height), :] = turned[0:kept]
-        leave(step, t).start()
-
-    @pl.when(step == ready.shape[0] - 1)
+            flat[pl.ds(t * LANES * tall + step * height + row, LANES, stride=tall), :] = jnp.transpose(
+                mean[t % 2, row]
+            )
+        if not inner:
+            leave(step, t).start()
+
+    @pl.when(step == steps - 1)
     def _():
-        for at in range(ready.shape[0]):
-            for t in range(wide // LANES):
-                leave(at, t).wait()
+        smooth(full, False)
+        for row in range(height):
+            turned = jnp.transpose(mean[full % 2, row])
+            for at in range(steps):
+                flat[pl.ds(full * LANES * tall + at * height + row, left, stride=tall), :] = turned[
+                    at * left : (at + 1) * left
+                ]
+        if not inner:
+            for at in range(steps):
+                leave(at, full).start()
+            for at in range(steps):
+                for t in range(full + 1):
+                    leave(at, t).wait()
+            leave_inner().wait()
 
 
 def solution(mesh):
@@ -538,30 +574,25 @@
         pitch = LANES + 16
 
         def filtered(lists, steps, block_of, before, name):
-            held = [pl.BlockSpec(memory_space=pltpu.SMEM), pl.BlockSpec(memory_space=pltpu.VMEM)] * (len(lists) // 2)
-            held += [pl.BlockSpec(memory_space=pltpu.VMEM)] * 3
+            held = [pl.BlockSpec(memory_space=pltpu.SMEM), vmem] * (len(lists) // 2) + [vmem] * 3
             given = list(lists) + [mixing, lon_table, lat_flat]
-            kernel = functools.partial(filter_kernel, block_of, reach, rows)
+            scratch = [
+                pltpu.VMEM((len(lists) // 2 * listed, wide), F32),
+                pltpu.VMEM(((height + 2 * reach) * pitch, wide), F32),
+                pltpu.VMEM((2, height, cols, LANES), F32),
+            ]
+            own_rows = (features, steps * height, cols)
             if before is not None:
                 given.append(before)
-                held.append(pl.BlockSpec(memory_space=pl.ANY))
-                at = len(lists) + 3
-                inner = kernel
-                kernel = lambda *refs: inner(*refs[:at], *refs[at + 1 :])
+                held.append(vmem)
+                scratch += [pltpu.VMEM(own_rows, F32), pltpu.SemaphoreType.DMA((steps + 1, wide // LANES))]
             return pl.pallas_call(
-                kernel,
+                functools.partial(filter_kernel, block_of, reach, rows, steps, before is None),
                 grid=(steps,),
                 in_specs=held,
-                out_specs=pl.BlockSpec(memory_space=pl.ANY),
-                out_shape=jax.ShapeDtypeStruct((features, rows, cols), F32),
-                scratch_shapes=[
-                    pltpu.VMEM((len(lists) // 2 * listed, wide), F32),
-                    pltpu.VMEM(((height + 2 * reach) * pitch, wide), F32),
-                    pltpu.VMEM((2, height, cols, LANES), F32),
-                    pltpu.VMEM((steps, features, height, cols), F32),
-                    pltpu.SemaphoreType.DMA((steps, wide // LANES)),
-                ],
-                input_output_aliases={} if before is None else {len(given) - 1: 0},
+                out_specs=vmem if before is None else anywhere,
+                out_shape=jax.ShapeDtypeStruct(own_rows if before is None else (features, rows, cols), F32),
+                scratch_shapes=scratch,
                 compiler_params=pltpu.CompilerParams(vmem_limit_bytes=24 * 1024 * 1024),
                 cost_estimate=pl.CostEstimate(
                     flops=40 * features * rows * cols, bytes_accessed=features * rows * cols * 2, transcendentals=0

time: 57.5 us -> 56.7 us (0.986)
    pallas_call x2, Pallas kernels: 9.65 us -> 8.83 us  [filtered(): pl.pallas_call(functools.partial(filter_kernel, block_of, reach, rows, st...]
where the time goes in v7:
time: 56.7 us; the launch traced here: 56.1 us
  starting transfers between devices  25.9 us (46%)
  Pallas kernels  17.9 us (32%)
  local copies, waits for them, and re-layouts  5.55 us (10%)
  waiting for transfers between devices  5.27 us (9%)
  other arithmetic  1.34 us (2%)
    pallas_call x2, Pallas kernels, filtered(): pl.pallas_call(functools.partial(filter_kernel, block_of, reach, rows, st...  8.83 us
    ppermute x1, starting transfers between devices, body(): impact_far = lax.ppermute(impact, 'lat', swaps[1])  6.48 us
    all_to_all x1, starting transfers between devices, body(): lax.all_to_all(codes, 'lon', split_axis=0, concat_axis=0, tiled=True)  6.35 us
    ppermute x1, starting transfers between devices, body(): info_far = lax.ppermute(info, 'lat', swaps[1])  5.4 us
    unnamed x22, local copies, waits for them, and re-layouts  5.17 us
    all_to_all x1, starting transfers between devices, body(): lax.all_to_all(products, 'lon', split_axis=0, concat_axis=0, tiled=True)  3.89 us
    all_to_all x1, starting transfers between devices, body(): lax.all_to_all(found.reshape(lon_devices, capacity, found.shape[-1]), 'lo...  3.63 us
    pallas_call x1, Pallas kernels, departures(): pl.pallas_call(functools.partial(last_departures, group, features, done),...  2.25 us
  transfers between devices with their start and end apart: 7, of which 4 were waited for; matrix products, arithmetic and copies ran while one was open for 1% of the time, Pallas kernels for 12%

profile of v7, /device:TPU:1, one launch (start us, length us, event | category | flops | bytes accessed | tf_op | source)
XLA Modules:
  0.0 56.1 jit_solution(3777631978247412732)
XLA Ops:
  0.0 1.3 %multiply_add_fusion = s32[8,1,64]{2,0,1:T(8,128)} fusion(s32[64]{0:T(128)} %bitcast.37, s32[64]{0:T(128)} %bitcast.30, s32[8]{0:T(128)S(1)} %iota_multiply_fusion), kind=kLoop, calls=%fused_computation | loop fusion | flops 1536 | bytes 2592 | tf_op jit(solution)/shard_map/add | solution.py:503
  1.3 6.4 %all-to-all-start = ((s32[8,1,64]{2,1,0:T(1,128)}), s32[8,1,64]{2,1,0:T(1,128)S(1)}, u32[]{:S(2)}, u32[]{:S(2)}) async-start(s32[8,1,64]{2,1,0:T(1,128)} %bitcast.2), calls=%async_computation | async-start | bytes 8192 | tf_op jit(solution)/shard_map/all_to_all | solution.py:504
  7.7 0.0 copy-start
  7.7 2.3 %copy-done = f32[2,137,32,128]{3,2,1,0:T(8,128)S(1)} copy-done((f32[2,137,32,128]{3,2,1,0:T(8,128)S(1)}, f32[2,137,32,128]{3,2,1,0:T(8,128)}, u32[]{:S(2)}) %copy-start) | copy-done | bytes 4489240
  10.0 0.0 copy-start.7
  10.0 0.0 copy-start.8
  10.0 0.0 copy-start.6
  10.0 0.0 copy-start.2
  10.0 0.0 copy-start.3
  10.0 0.0 copy-start.4
  10.0 1.1 %lay_state.1 = bf16[137,32,256]{2,1,0:T(8,128)(2,1)S(1)} custom-call(f32[8768,128]{1,0:T(8,128)S(1)} %bitcast.21), custom_call_target="tpu_custom_call" | custom-call | bytes 6733824 | tf_op jit(solution)/shard_map/lay_state/pallas_call | solution.py:66
  11.1 1.8 %all-to-all-done = s32[8,1,64]{2,1,0:T(1,128)S(1)} async-done(((s32[8,1,64]{2,1,0:T(1,128)}), s32[8,1,64]{2,1,0:T(1,128)S(1)}, u32[]{:S(2)}, u32[]{:S(2)}) %all-to-all-start) | async-done | bytes 2080 | tf_op jit(solution)/shard_map/all_to_all | solution.py:504
  12.9 0.0 copy-start.5
  12.9 1.9 %gather_state.1.after_ref = bf16[128,384]{1,0:T(8,128)(2,1)} custom-call(s32[8,64]{1,0:T(8,128)S(1)} %bitcast.27, bf16[4384,256]{1,0:T(8,128)(2,1)S(1)} %bitcast.20), custom_call_target="tpu_custom_call" | custom-call | flops 287309824 | bytes 2244608 | tf_op jit(solution)/shard_map/gather_state/pallas_call | solution.py:121
  14.9 3.6 %all-to-all-start.1 = ((bf16[8,16,384]{2,1,0:T(8,128)(2,1)}), bf16[8,16,384]{2,1,0:T(8,128)(2,1)S(1)}, u32[]{:S(2)}, u32[]{:S(2)}) async-start(bf16[8,16,384]{2,1,0:T(8,128)(2,1)} %bitcast.11), calls=%async_computation.1 | async-start | bytes 196608 | tf_op jit(solution)/shard_map/all_to_all | solution.py:509
  18.5 0.0 copy-done.7
  18.5 0.1 reshape.134.lon_ref
  18.6 0.0 copy-done.8
  18.6 0.1 reshape.135.lat_ref
  18.7 0.0 copy-done.6
  18.7 0.2 reshape.133.vertical_ref
  18.9 0.0 copy-done.2
  18.9 0.0 copy-done.3
  18.9 0.0 copy-done.4
  18.9 1.4 %plan_points.1 = (bf16[64,128]{1,0:T(8,128)(2,1)S(1)}, f32[64,128]{1,0:T(8,128)S(1)}, bf16[384,512]{1,0:T(8,128)(2,1)S(1)}, s32[1,512]{1,0:T(1,128)S(1)}, bf16[2...) custom-call(s32[8,64]{1,0:T(8,128)S(1)} %bitcast.28, s32[1,64]{1,0:T(1,128)S(1)} %bitcast.31, ...), custom_call_target="tpu_custom_call" | custom-call | flops 2097152 | bytes 393216 | tf_op jit(solution)/shard_map/plan_points/pallas_call | solution.py:516
  20.4 0.0 copy-start.1
  20.4 2.3 %copy-done.1 = bf16[1,64,2,137,128]{4,2,3,1,0:T(2,128)(2,1)S(1)} copy-done((bf16[1,64,2,137,128]{4,2,3,1,0:T(2,128)(2,1)S(1)}, bf16[1,64,2,137,128]{4,2,3,1,0:T(2,128)(2,1)}, u32[]{:S(2)}) %copy-start.1) | copy-done | bytes 4489240
  22.6 0.0 slice-start
  22.6 0.3 fetch_jacobian.1.jac_ref
  23.0 1.6 %all-to-all-done.1 = bf16[8,16,384]{2,1,0:T(8,128)(2,1)S(1)} async-done(((bf16[8,16,384]{2,1,0:T(8,128)(2,1)}), bf16[8,16,384]{2,1,0:T(8,128)(2,1)S(1)}, u32[]{:S(2)}, u32[]{:S(2)}) %all-to-all-start.1) | async-done | bytes 98336 | tf_op jit(solution)/shard_map/all_to_all | solution.py:509
  24.6 0.0 copy-done.5
  24.6 1.6 %first_departures.1 = (f32[288,128]{1,0:T(8,128)S(1)}, f32[64,384]{1,0:T(8,128)S(1)}) custom-call(bf16[64,128]{1,0:T(8,128)(2,1)S(1)} %get-tuple-element.15.chosen_ref, bf16[128,384]{1,0:T(8,128)(2,1)S(1)} %bitcast.26, f32[64,128]{1,0:T(8,128)S(1)} %get-tuple-element.16.weight_ref, bf16[64,128]{1,0:T(8,128)(2,1)S(1)} %bitcast.32, ...), custom_call_target="tpu_custom_call" | custom-call | flops 3000000000 | bytes 2244608 | tf_op jit(solution)/shard_map/first_departures/pallas_call | solution.py:237
  26.1 0.0 slice-done
  26.2 0.6 %slice-done.1 = s8[4194304]{0:T(1024)(128)(4,1)S(1)} async-done(((s8[4489216]{0:T(1024)(128)(4,1)}), s8[4194304]{0:T(1024)(128)(4,1)S(1)}, s32[]{:S(2)}) %slice-start.1) | async-done | bytes 4194328
  26.8 2.2 %last_departures.1 = bf16[8,144,128]{2,1,0:T(8,128)(2,1)} custom-call(f32[64,384]{1,0:T(8,128)S(1)} %get-tuple-element.17.columns_ref, f32[64,128]{1,0:T(8,128)S(1)} %get-tuple-element.16.weight_ref, bf16[64,128]{1,0:T(8,128)(2,1)S(1)} %bitcast.33, bf16[17536,128]{1,0:T(8,128)(2,1)S(1)} %bitcast.25, f32[288,128]{1,0:T(8,128)S(1)} %get-tuple-element.18.before_ref), custom_call_target="tpu_custom_call" | custom-call | flops 3000000000 | bytes 2244608 | tf_op jit(solution)/shard_map/last_departures/pallas_call | solution.py:248
  29.0 3.9 %all-to-all-start.2 = ((bf16[8,144,128]{2,1,0:T(8,128)(2,1)}), bf16[8,144,128]{2,1,0:T(8,128)(2,1)S(1)}, u32[]{:S(2)}, u32[]{:S(2)}) async-start(bf16[8,144,128]{2,1,0:T(8,128)(2,1)} %last_departures.1), calls=%async_computation.2 | async-start | bytes 589824 | tf_op jit(solution)/shard_map/all_to_all | solution.py:553
  32.9 5.4 %collective-permute-start.1 = (s32[1,512]{1,0:T(1,128)S(1)}, s32[1,512]{1,0:T(1,128)S(1)}, u32[]{:S(2)}, u32[]{:S(2)}) collective-permute-start(s32[1,512]{1,0:T(1,128)S(1)} %get-tuple-element.14.after_ref.refs_0_), channel_id=1, source_target_pairs={{1,2},{2,1},{5,6},{6,5},{9,10},{10,9},{13,14},{14,13},{17,18},{18,... | collective-permute-start | bytes 6152 | tf_op jit(solution)/shard_map/ppermute | solution.py:559
  38.3 0.1 collective-permute-start
  38.4 1.5 %collective-permute-done.1.far_ref.refs_4_ = s32[1,512]{1,0:T(1,128)S(1)} collective-permute-done((s32[1,512]{1,0:T(1,128)S(1)}, s32[1,512]{1,0:T(1,128)S(1)}, u32[]{:S(2)}, u32[]{:S(2)}) %collective-permute-start.1) | collective-permute-done | bytes 2080 | tf_op jit(solution)/shard_map/ppermute | solution.py:559
  39.9 0.0 collective-permute-done.near_ref.refs_2_
  39.9 0.4 all-to-all-done.2.products_ref
  40.2 0.4 impact_columns.1.refs_1_
  40.7 6.5 %collective-permute-start.3 = (bf16[144,768]{1,0:T(8,128)(2,1)S(1)}, bf16[144,768]{1,0:T(8,128)(2,1)S(1)}, u32[]{:S(2)}, u32[]{:S(2)}) collective-permute-start(bf16[144,768]{1,0:T(8,128)(2,1)S(1)} %impact_columns.1.refs_1_), channel_id=1, source_target_pairs={{1,2},{2,1},{5,6},{6,5},{9,10},{10,9},{13,14},{14,13},{17,18},{18,... | collective-permute-start | bytes 663560 | tf_op jit(solution)/shard_map/ppermute | solution.py:570
  47.2 0.1 collective-permute-start.2
  47.2 3.7 %inner_rows.1.refs_9_ = f32[274,16,128]{2,1,0:T(8,128)S(1)} custom-call(s32[1,512]{1,0:T(1,128)S(1)} %get-tuple-element.14.after_ref.refs_0_, bf16[144,768]{1,0:T(8,128)(2,1)S(1)} %impact_columns.1.refs_1_, bf16[2,144,384]{2,1,0:T(8,128)(2,1)S(1)} %get-tuple-element.20.refs_2_.refs_6_, f32[128,384]{1,0:T(8,128)S(1)} %get-tuple-element.21.refs_3_.refs_7_, ...), custom_call_target="tpu_custom_call" | custom-call | flops 44892160 | bytes 2244608 | tf_op jit(solution)/shard_map/inner_rows/pallas_call | solution.py:589
  50.9 0.0 collective-permute-done.3.refs_5_
  50.9 0.0 collective-permute-done.2.refs_3_
  50.9 5.2 %outer_rows.1 = f32[274,32,128]{2,1,0:T(8,128)} custom-call(s32[1,512]{1,0:T(1,128)S(1)} %get-tuple-element.14.after_ref.refs_0_, bf16[144,768]{1,0:T(8,128)(2,1)S(1)} %impact_columns.1.refs_1_, s32[1,512]{1,0:T(1,128)S(1)} %collective-permute-done.near_ref.refs_2_, bf16[144,768]{1,0:T(8,128)(2,1)S(1)} %collective-permute-done.2.refs_3_, ...), custom_call_target="tpu_custom_call" | custom-call | flops 44892160 | bytes 2244608 | tf_op jit(solution)/shard_map/outer_rows/pallas_call | solution.py:589
  (3 shorter events, 0.0 us)
Async XLA Ops:
  1.3 11.6 %all-to-all-start = ((s32[8,1,64]{2,1,0:T(1,128)}), s32[8,1,64]{2,1,0:T(1,128)S(1)}, u32[]{:S(2)}, u32[]{:S(2)}) async-start(s32[8,1,64]{2,1,0:T(1,128)} %bitcast.2), calls=%async_computation | async-start | bytes 8192 | tf_op jit(solution)/shard_map/all_to_all | solution.py:504
  7.7 2.3 %copy-start = (f32[2,137,32,128]{3,2,1,0:T(8,128)S(1)}, f32[2,137,32,128]{3,2,1,0:T(8,128)}, u32[]{:S(2)}) copy-start(f32[2,137,32,128]{3,2,1,0:T(8,128)} %param.10) | copy-start | bytes 13467652
  10.0 8.5 %copy-start.7 = (f32[2,137,9]{1,0,2:T(2,128)S(1)}, f32[2,137,9]{1,0,2:T(2,128)}, u32[]{:S(2)}) copy-start(f32[2,137,9]{1,0,2:T(2,128)} %param.18) | copy-start | bytes 29596
  10.0 8.6 %copy-start.8 = (f32[2,137,9]{1,0,2:T(2,128)S(1)}, f32[2,137,9]{1,0,2:T(2,128)}, u32[]{:S(2)}) copy-start(f32[2,137,9]{1,0,2:T(2,128)} %param.19) | copy-start | bytes 29596
  10.0 8.7 %copy-start.6 = (bf16[2,137,137]{2,0,1:T(2,128)(2,1)S(1)}, bf16[2,137,137]{2,0,1:T(2,128)(2,1)}, u32[]{:S(2)}) copy-start(bf16[2,137,137]{2,0,1:T(2,128)(2,1)} %param.17) | copy-start | bytes 225232
  10.0 8.9 %copy-start.2 = (bf16[1,64,128]{2,1,0:T(8,128)(2,1)S(1)}, bf16[1,64,128]{2,1,0:T(8,128)(2,1)}, u32[]{:S(2)}) copy-start(bf16[1,64,128]{2,1,0:T(8,128)(2,1)} %param.13) | copy-start | bytes 49156
  10.0 8.9 %copy-start.3 = (s32[1,64,1]{1,2,0:T(1,128)S(1)}, s32[1,64,1]{1,2,0:T(1,128)}, u32[]{:S(2)}) copy-start(s32[1,64,1]{1,2,0:T(1,128)} %param.15) | copy-start | bytes 772
  10.0 8.9 %copy-start.4 = (s32[1,64]{1,0:T(1,128)S(1)}, s32[1,64]{1,0:T(1,128)}, u32[]{:S(2)}) copy-start(s32[1,64]{1,0:T(1,128)} %valid_ref.1) | copy-start | bytes 772
  12.9 11.6 %copy-start.5 = (bf16[1,64,128]{2,1,0:T(8,128)(2,1)S(1)}, bf16[1,64,128]{2,1,0:T(8,128)(2,1)}, u32[]{:S(2)}) copy-start(bf16[1,64,128]{2,1,0:T(8,128)(2,1)} %param.12) | copy-start | bytes 49156
  14.9 9.7 %all-to-all-start.1 = ((bf16[8,16,384]{2,1,0:T(8,128)(2,1)}), bf16[8,16,384]{2,1,0:T(8,128)(2,1)S(1)}, u32[]{:S(2)}, u32[]{:S(2)}) async-start(bf16[8,16,384]{2,1,0:T(8,128)(2,1)} %bitcast.11), calls=%async_computation.1 | async-start | bytes 196608 | tf_op jit(solution)/shard_map/all_to_all | solution.py:509
  20.4 2.3 %copy-start.1 = (bf16[1,64,2,137,128]{4,2,3,1,0:T(2,128)(2,1)S(1)}, bf16[1,64,2,137,128]{4,2,3,1,0:T(2,128)(2,1)}, u32[]{:S(2)}) copy-start(bf16[1,64,2,137,128]{4,2,3,1,0:T(2,128)(2,1)} %param.11) | copy-start | bytes 13467652
  22.6 3.5 %slice-start = ((s8[4489216]{0:T(1024)(128)(4,1)}), s8[294912]{0:T(1024)(128)(4,1)S(1)}, s32[]{:S(2)}) async-start(s8[4489216]{0:T(1024)(128)(4,1)} %bitcast.23), calls=%async_computation.3 | async-start | bytes 589824
  24.6 2.2 %slice-start.1 = ((s8[4489216]{0:T(1024)(128)(4,1)}), s8[4194304]{0:T(1024)(128)(4,1)S(1)}, s32[]{:S(2)}) async-start(s8[4489216]{0:T(1024)(128)(4,1)} %bitcast.23), calls=%async_computation.4 | async-start | bytes 8388608
  29.0 11.2 %all-to-all-start.2 = ((bf16[8,144,128]{2,1,0:T(8,128)(2,1)}), bf16[8,144,128]{2,1,0:T(8,128)(2,1)S(1)}, u32[]{:S(2)}, u32[]{:S(2)}) async-start(bf16[8,144,128]{2,1,0:T(8,128)(2,1)} %last_departures.1), calls=%async_computation.2 | async-start | bytes 589824 | tf_op jit(solution)/shard_map/all_to_all | solution.py:553
  32.9 7.0 %collective-permute-start.1 = (s32[1,512]{1,0:T(1,128)S(1)}, s32[1,512]{1,0:T(1,128)S(1)}, u32[]{:S(2)}, u32[]{:S(2)}) collective-permute-start(s32[1,512]{1,0:T(1,128)S(1)} %get-tuple-element.14.after_ref.refs_0_), channel_id=1, source_target_pairs={{1,2},{2,1},{5,6},{6,5},{9,10},{10,9},{13,14},{14,13},{17,18},{18,... | collective-permute-start | bytes 6152 | tf_op jit(solution)/shard_map/ppermute | solution.py:559
  38.3 1.6 %collective-permute-start = (s32[1,512]{1,0:T(1,128)S(1)}, s32[1,512]{1,0:T(1,128)S(1)}, u32[]{:S(2)}, u32[]{:S(2)}) collective-permute-start(s32[1,512]{1,0:T(1,128)S(1)} %get-tuple-element.14.after_ref.refs_0_), channel_id=1, source_target_pairs={{0,1},{2,3},{1,0},{3,2},{4,5},{6,7},{5,4},{7,6},{8,9},{10,11},{9,8... | collective-permute-start | bytes 6152 | tf_op jit(solution)/shard_map/ppermute | solution.py:558
  40.7 10.2 %collective-permute-start.3 = (bf16[144,768]{1,0:T(8,128)(2,1)S(1)}, bf16[144,768]{1,0:T(8,128)(2,1)S(1)}, u32[]{:S(2)}, u32[]{:S(2)}) collective-permute-start(bf16[144,768]{1,0:T(8,128)(2,1)S(1)} %impact_columns.1.refs_1_), channel_id=1, source_target_pairs={{1,2},{2,1},{5,6},{6,5},{9,10},{10,9},{13,14},{14,13},{17,18},{18,... | collective-permute-start | bytes 663560 | tf_op jit(solution)/shard_map/ppermute | solution.py:570
  47.2 3.8 %collective-permute-start.2 = (bf16[144,768]{1,0:T(8,128)(2,1)S(1)}, bf16[144,768]{1,0:T(8,128)(2,1)S(1)}, u32[]{:S(2)}, u32[]{:S(2)}) collective-permute-start(bf16[144,768]{1,0:T(8,128)(2,1)S(1)} %impact_columns.1.refs_1_), channel_id=1, source_target_pairs={{0,1},{2,3},{1,0},{3,2},{4,5},{6,7},{5,4},{7,6},{8,9},{10,11},{9,8... | collective-permute-start | bytes 663560 | tf_op jit(solution)/shard_map/ppermute | solution.py:569

commit v8 on v6

--- a/solution.py
+++ b/solution.py
@@ -267,7 +267,13 @@
     return jnp.where(key == NOWHERE, NOWHERE, key + row * STRIDE)
 
 
-def plan_kernel(records, points, reach, capacity, codes_ref, dest_ref, valid_ref, inv_ref, vertical_ref, lon_ref, lat_ref, after_ref, chosen_ref, weight_ref, same_ref, info_ref, mixing_ref, table_ref, taps_ref, down, first):
+def twice(array, features):
+    left = features % LANES
+    lane = lane_iota(array.shape)
+    return jnp.where((lane >= features) & (lane < features + left), pltpu.roll(array, left, 1), array)
+
+
+def plan_kernel(records, points, reach, capacity, codes_ref, dest_ref, valid_ref, inv_ref, after_ref, chosen_ref, weight_ref, same_ref, info_ref, down, first):
     count = codes_ref.shape[0]
     span, listed = count * records, same_ref.shape[0]
     tile, column = split_codes(codes_ref, records, points)
@@ -315,6 +321,8 @@
     alive = lane_iota(weight_ref.shape) < to_column(valid_ref[...])
     weight_ref[...] = jnp.where(alive, inv_ref[...].astype(F32), 0.0)
 
+
+def tables_kernel(vertical_ref, lon_ref, lat_ref, after_ref, mixing_ref, table_ref, taps_ref):
     features, levels = vertical_ref.shape
     wide = mixing_ref.shape[2]
     tall = mixing_ref.shape[1]
@@ -324,18 +332,19 @@
     spread = rows
     for v in range(1, variables):
         spread = jnp.where(row_iota(rows.shape) % variables == v, pltpu.roll(rows, v * levels, 1), spread)
+    spread = twice(spread, features)
     mixing_ref[0] = spread[:tall].astype(BF16)
     mixing_ref[1, 0 : features - tall, :] = spread[tall:].astype(BF16)
     taps = lon_ref.shape[0]
     spare = jnp.zeros((taps, wide - features), F32)
-    lon = jnp.concatenate([lon_ref[...], spare], axis=1)
+    lon = twice(jnp.concatenate([lon_ref[...], spare], axis=1), features)
     lon = jnp.concatenate([lon[k : k + 1] for k in reversed(range(taps))] + [jnp.zeros((16 - taps, wide), F32)], axis=0)
     for b in range(8):
         table_ref[16 * b : 16 * (b + 1), :] = pltpu.roll(lon, b, 0) if b else lon
-    taps_ref[...] = jnp.concatenate([lat_ref[...], spare], axis=1)
-
-
-def impact_kernel(records, products_ref, same_ref, near_ref, far_ref, out_ref, terms):
+    taps_ref[...] = twice(jnp.concatenate([lat_ref[...], spare], axis=1), features)
+
+
+def impact_kernel(records, products_ref, same_ref, near_ref, far_ref, tables_ref, out_ref, terms):
     count, tall, width = products_ref.shape
     listed = same_ref.shape[0]
     lane = lane_iota((tall, width))
@@ -382,11 +391,16 @@
                         )
                     mixed[n * listed + part : n * listed + part + LANES, :] = total
 
+    steps = ready.shape[0]
+    full, left = divmod(features, LANES)
+    lane = lane_iota((1, wide)) - full * LANES
+    mine = (lane < 0) | ((lane >= step * left) & (lane < (step + 1) * left))
+    mine = jnp.where(mine, 1.0, 0.0)
     for n, (info, _) in enumerate(lists):
         offset = -base
         if n:
             side = 1 - 2 * lax.rem(lax.axis_index("lat"), 2)
-            offset += (rows if n == 1 else -rows) * side
+            offset += (rows if n == 2 else -rows) * side
         low = jnp.clip(-offset, 0, rows)
         high = jnp.clip(window - offset, 0, rows)
 
@@ -404,7 +418,7 @@
                 spot = jnp.bitwise_and(place, 7)
                 at = pl.ds(pl.multiple_of(row * pitch + place - spot, 8), 16)
                 taps = lon_ref[pl.ds(pl.multiple_of(spot * 16, 16), 16), :]
-                column = mixed[pl.ds(n * listed + here, 1), :] * jnp.where(live, 1.0, 0.0)
+                column = mixed[pl.ds(n * listed + here, 1), :] * jnp.where(live, mine, 0.0)
                 pieces.append((at, taps * column))
             for at, piece in pieces:
                 along[at, :] += piece
@@ -419,32 +433,43 @@
         there = pl.ds(pl.multiple_of(block_of(at) * height, height), height)
         return pltpu.make_async_copy(ready.at[at, here], out_ref.at[here, there], sent.at[at, t])
 
-    for t in range(wide // LANES):
+    def smooth(t, again):
         here = slice(t * LANES, (t + 1) * LANES)
         lat = [jnp.broadcast_to(lat_ref[k : k + 1, here], (8, LANES)) for k in range(2 * reach + 1)]
-
         for j in range(LANES // 8):
             sums = [None] * height
             for w in range(window):
                 spot = pl.ds(w * pitch + 8 + j * 8, 8)
                 part = along[spot, here]
-                along[spot, here] = jnp.zeros_like(part)
+                if again:
+                    along[spot, here] = jnp.zeros_like(part)
                 for row in range(max(0, w - 2 * reach), min(height, w + 1)):
                     term = lat[w - row] * part
                     sums[row] = term if sums[row] is None else sums[row] + term
             for row in range(height):
                 mean[t % 2, row, j * 8 : (j + 1) * 8, :] = sums[row]
 
-        kept = min(LANES, features - t * LANES)
+    for t in range(full):
+        smooth(t, True)
         for row in range(height):
-            turned = jnp.transpose(mean[t % 2, row])
-            flat[pl.ds((step * features + t * LANES) * height + row, kept, stride=height), :] = turned[0:kept]
+            flat[pl.ds((step * features + t * LANES) * height + row, LANES, stride=height), :] = jnp.transpose(
+                mean[t % 2, row]
+            )
         leave(step, t).start()
 
-    @pl.when(step == ready.shape[0] - 1)
+    @pl.when(step == steps - 1)
     def _():
-        for at in range(ready.shape[0]):
-            for t in range(wide // LANES):
+        smooth(full, False)
+        for row in range(height):
+            turned = jnp.transpose(mean[full % 2, row])
+            for at in range(steps):
+                flat[pl.ds((at * features + full * LANES) * height + row, left, stride=height), :] = turned[
+                    at * left : (at + 1) * left
+                ]
+        for at in range(steps):
+            leave(at, full).start()
+        for at in range(steps):
+            for t in range(full + 1):
                 leave(at, t).wait()
 
 
@@ -477,17 +502,14 @@
         wide = pl.cdiv(features, LANES) * LANES
         taps = lon_taps.shape[-1]
         vmem, anywhere = pl.BlockSpec(memory_space=pltpu.VMEM), pl.BlockSpec(memory_space=pl.ANY)
-        chosen, weight, same, info, mixing, lon_table, lat_flat = pl.pallas_call(
+        chosen, weight, same, info = pl.pallas_call(
             functools.partial(plan_kernel, records, points, reach, capacity),
-            in_specs=[vmem] * 7 + [anywhere],
+            in_specs=[vmem] * 4 + [anywhere],
             out_shape=(
                 jax.ShapeDtypeStruct((records, lon_devices * capacity), BF16),
                 jax.ShapeDtypeStruct((records, channels), F32),
                 jax.ShapeDtypeStruct((listed, span), BF16),
                 jax.ShapeDtypeStruct((1, listed + LANES), jnp.int32),
-                jax.ShapeDtypeStruct((2, tall, wide), BF16),
-                jax.ShapeDtypeStruct((8 * 16, wide), F32),
-                jax.ShapeDtypeStruct((taps, wide), F32),
             ),
             scratch_shapes=[pltpu.VMEM((span, LANES), jnp.int32), pltpu.VMEM((span, LANES), F32)],
             compiler_params=pltpu.CompilerParams(vmem_limit_bytes=16 * 1024 * 1024),
@@ -498,9 +520,6 @@
             destination.reshape(1, records),
             valid_count.reshape(1, records),
             inverse_var.reshape(records, channels),
-            jnp.swapaxes(vertical, 0, 1).reshape(features, levels),
-            jnp.moveaxis(lon_taps, 2, 0).reshape(taps, features),
-            jnp.moveaxis(lat_taps, 2, 0).reshape(taps, features),
             found,
         )
         own = jnp.swapaxes(jacobian.reshape(records, variables, levels, channels), 1, 2).reshape(-1, channels)
@@ -516,6 +535,23 @@
         )
         products_in = lax.all_to_all(products, "lon", split_axis=0, concat_axis=0, tiled=True)
 
+        mixing, lon_table, lat_flat = pl.pallas_call(
+            tables_kernel,
+            in_specs=[vmem] * 3 + [anywhere],
+            out_shape=(
+                jax.ShapeDtypeStruct((2, tall, wide), BF16),
+                jax.ShapeDtypeStruct((8 * 16, wide), F32),
+                jax.ShapeDtypeStruct((taps, wide), F32),
+            ),
+            compiler_params=pltpu.CompilerParams(vmem_limit_bytes=16 * 1024 * 1024),
+            cost_estimate=pl.CostEstimate(flops=0, bytes_accessed=4 * features * wide, transcendentals=0),
+            name="tables",
+        )(
+            jnp.swapaxes(vertical, 0, 1).reshape(features, levels),
+            jnp.moveaxis(lon_taps, 2, 0).reshape(taps, features),
+            jnp.moveaxis(lat_taps, 2, 0).reshape(taps, features),
+            products,
+        )
         pairs = [(i, i + 1) for i in range(0, lat_devices - 1, 2)]
         between = [(i, i + 1) for i in range(1, lat_devices - 1, 2)]
         swaps = [[(a, b) for a, b in some] + [(b, a) for a, b in some] for some in (pairs, between)]
@@ -524,12 +560,12 @@
 
         impact = pl.pallas_call(
             functools.partial(impact_kernel, records),
-            in_specs=[vmem] * 2 + [anywhere] * 2,
+            in_specs=[vmem] * 2 + [anywhere] * 3,
             out_shape=jax.ShapeDtypeStruct((tall, 2 * listed), BF16),
             scratch_shapes=[pltpu.VMEM((2, tall, span), BF16)],
             compiler_params=pltpu.CompilerParams(vmem_limit_bytes=16 * 1024 * 1024),
             name="impact_columns",
-        )(products_in, same, info_near, info_far)
+        )(products_in, same, info_near, info_far, mixing)
         impact_near = lax.ppermute(impact, "lat", swaps[0])
         impact_far = lax.ppermute(impact, "lat", swaps[1])
 
@@ -571,7 +607,7 @@
 
         inner = filtered([info, impact], blocks - 2, lambda s: s + 1, None, "inner_rows")
         result = filtered(
-            [info, impact, info_near, impact_near, info_far, impact_far],
+            [info, impact, info_far, impact_far, info_near, impact_near],
             2,
             lambda s: s * (blocks - 1),
             inner,

time: 57.5 us -> 57.5 us (level)
    ppermute x1, starting transfers between devices: 0.07 us -> 3.97 us  [body(): impact_near = lax.ppermute(impact, 'lat', swaps[0])]
    ppermute x1, starting transfers between devices: 6.76 us -> 3.04 us  [body(): impact_far = lax.ppermute(impact, 'lat', swaps[1])]
    ppermute x1, waiting for transfers between devices: 1.28 us -> 0.52 us  [body(): info_far = lax.ppermute(info, 'lat', swaps[1])]
where the time goes in v8:
time: 57.5 us; the launch traced here: 56.6 us
  starting transfers between devices  26.4 us (46%)
  Pallas kernels  18.3 us (32%)
  local copies, waits for them, and re-layouts  5.56 us (10%)
  waiting for transfers between devices  4.95 us (9%)
  other arithmetic  1.34 us (2%)
    pallas_call x2, Pallas kernels, filtered(): pl.pallas_call(kernel, grid=(steps,), in_specs=held, out_specs=pl.BlockSp...  9.42 us
    all_to_all x1, starting transfers between devices, body(): lax.all_to_all(codes, 'lon', split_axis=0, concat_axis=0, tiled=True)  6.35 us
    ppermute x1, starting transfers between devices, body(): info_far = lax.ppermute(info, 'lat', swaps[1])  5.9 us
    unnamed x22, local copies, waits for them, and re-layouts  5.18 us
    ppermute x1, starting transfers between devices, body(): impact_near = lax.ppermute(impact, 'lat', swaps[0])  3.97 us
    all_to_all x1, starting transfers between devices, body(): lax.all_to_all(found.reshape(lon_devices, capacity, found.shape[-1]), 'lo...  3.59 us
    all_to_all x1, starting transfers between devices, body(): lax.all_to_all(products, 'lon', split_axis=0, concat_axis=0, tiled=True)  3.42 us
    ppermute x1, starting transfers between devices, body(): impact_far = lax.ppermute(impact, 'lat', swaps[1])  3.04 us
  transfers between devices with their start and end apart: 7, of which 4 were waited for; matrix products, arithmetic and copies ran while one was open for 1% of the time, Pallas kernels for 12%

profile of v8, /device:TPU:1, one launch (start us, length us, event | category | flops | bytes accessed | tf_op | source)
XLA Modules:
  0.0 56.6 jit_solution(12576305104724679736)
XLA Ops:
  0.0 1.3 %multiply_add_fusion = s32[8,1,64]{2,0,1:T(8,128)} fusion(s32[64]{0:T(128)} %bitcast.37, s32[64]{0:T(128)} %bitcast.30, s32[8]{0:T(128)S(1)} %iota_multiply_fusion), kind=kLoop, calls=%fused_computation | loop fusion | flops 1536 | bytes 2592 | tf_op jit(solution)/shard_map/add | solution.py:492
  1.3 6.4 %all-to-all-start = ((s32[8,1,64]{2,1,0:T(1,128)}), s32[8,1,64]{2,1,0:T(1,128)S(1)}, u32[]{:S(2)}, u32[]{:S(2)}) async-start(s32[8,1,64]{2,1,0:T(1,128)} %bitcast.2), calls=%async_computation | async-start | bytes 8192 | tf_op jit(solution)/shard_map/all_to_all | solution.py:493
  7.7 0.0 copy-start
  7.7 2.3 %copy-done = f32[2,137,32,128]{3,2,1,0:T(8,128)S(1)} copy-done((f32[2,137,32,128]{3,2,1,0:T(8,128)S(1)}, f32[2,137,32,128]{3,2,1,0:T(8,128)}, u32[]{:S(2)}) %copy-start) | copy-done | bytes 4489240
  10.0 0.0 copy-start.2
  10.0 0.0 copy-start.3
  10.0 0.0 copy-start.4
  10.0 1.1 %lay_state.1 = bf16[137,32,256]{2,1,0:T(8,128)(2,1)S(1)} custom-call(f32[8768,128]{1,0:T(8,128)S(1)} %bitcast.21), custom_call_target="tpu_custom_call" | custom-call | bytes 6733824 | tf_op jit(solution)/shard_map/lay_state/pallas_call | solution.py:66
  11.1 1.9 %all-to-all-done = s32[8,1,64]{2,1,0:T(1,128)S(1)} async-done(((s32[8,1,64]{2,1,0:T(1,128)}), s32[8,1,64]{2,1,0:T(1,128)S(1)}, u32[]{:S(2)}, u32[]{:S(2)}) %all-to-all-start) | async-done | bytes 2080 | tf_op jit(solution)/shard_map/all_to_all | solution.py:493
  12.9 0.0 copy-start.5
  12.9 1.9 %gather_state.1.after_ref = bf16[128,384]{1,0:T(8,128)(2,1)} custom-call(s32[8,64]{1,0:T(8,128)S(1)} %bitcast.27, bf16[4384,256]{1,0:T(8,128)(2,1)S(1)} %bitcast.20), custom_call_target="tpu_custom_call" | custom-call | flops 287309824 | bytes 2244608 | tf_op jit(solution)/shard_map/gather_state/pallas_call | solution.py:121
  14.9 3.6 %all-to-all-start.1 = ((bf16[8,16,384]{2,1,0:T(8,128)(2,1)}), bf16[8,16,384]{2,1,0:T(8,128)(2,1)S(1)}, u32[]{:S(2)}, u32[]{:S(2)}) async-start(bf16[8,16,384]{2,1,0:T(8,128)(2,1)} %bitcast.8), calls=%async_computation.1 | async-start | bytes 196608 | tf_op jit(solution)/shard_map/all_to_all | solution.py:498
  18.4 0.0 copy-done.2
  18.5 0.0 copy-done.3
  18.5 0.0 copy-done.4
  18.5 1.0 %plan_points.1 = (bf16[64,128]{1,0:T(8,128)(2,1)S(1)}, f32[64,128]{1,0:T(8,128)S(1)}, bf16[384,512]{1,0:T(8,128)(2,1)S(1)}, s32[1,512]{1,0:T(1,128)S(1)}) custom-call(s32[8,64]{1,0:T(8,128)S(1)} %bitcast.28, s32[1,64]{1,0:T(1,128)S(1)} %bitcast.31, s32[1,64]{1,0:T(1,128)S(1)} %copy-done.4, bf16[64,128]{1,0:T(8,128)(2,1)S(1)} %bitcast.29, ...), custom_call_target="tpu_custom_call" | custom-call | flops 2097152 | bytes 393216 | tf_op jit(solution)/shard_map/plan_points/pallas_call | solution.py:505
  19.5 0.0 copy-start.1
  19.5 2.3 %copy-done.1 = bf16[1,64,2,137,128]{4,2,3,1,0:T(2,128)(2,1)S(1)} copy-done((bf16[1,64,2,137,128]{4,2,3,1,0:T(2,128)(2,1)S(1)}, bf16[1,64,2,137,128]{4,2,3,1,0:T(2,128)(2,1)}, u32[]{:S(2)}) %copy-start.1) | copy-done | bytes 4489240
  21.8 0.0 slice-start
  21.8 0.3 fetch_jacobian.1.jac_ref
  22.1 2.4 %all-to-all-done.1 = bf16[8,16,384]{2,1,0:T(8,128)(2,1)S(1)} async-done(((bf16[8,16,384]{2,1,0:T(8,128)(2,1)}), bf16[8,16,384]{2,1,0:T(8,128)(2,1)S(1)}, u32[]{:S(2)}, u32[]{:S(2)}) %all-to-all-start.1) | async-done | bytes 98336 | tf_op jit(solution)/shard_map/all_to_all | solution.py:498
  24.5 0.0 copy-done.5
  24.5 0.0 slice-start.1
  24.5 1.6 %first_departures.1 = (f32[288,128]{1,0:T(8,128)S(1)}, f32[64,384]{1,0:T(8,128)S(1)}) custom-call(bf16[64,128]{1,0:T(8,128)(2,1)S(1)} %get-tuple-element.15.chosen_ref, bf16[128,384]{1,0:T(8,128)(2,1)S(1)} %bitcast.26, f32[64,128]{1,0:T(8,128)S(1)} %get-tuple-element.16.weight_ref, bf16[64,128]{1,0:T(8,128)(2,1)S(1)} %bitcast.32, ...), custom_call_target="tpu_custom_call" | custom-call | flops 3000000000 | bytes 2244608 | tf_op jit(solution)/shard_map/first_departures/pallas_call | solution.py:237
  26.1 0.0 slice-done
  26.1 0.6 %slice-done.1 = s8[4194304]{0:T(1024)(128)(4,1)S(1)} async-done(((s8[4489216]{0:T(1024)(128)(4,1)}), s8[4194304]{0:T(1024)(128)(4,1)S(1)}, s32[]{:S(2)}) %slice-start.1) | async-done | bytes 4194328
  26.7 0.0 copy-start.8
  26.7 2.2 %last_departures.1.after_ref = bf16[8,144,128]{2,1,0:T(8,128)(2,1)} custom-call(f32[64,384]{1,0:T(8,128)S(1)} %get-tuple-element.17.columns_ref, f32[64,128]{1,0:T(8,128)S(1)} %get-tuple-element.16.weight_ref, bf16[64,128]{1,0:T(8,128)(2,1)S(1)} %bitcast.33, bf16[17536,128]{1,0:T(8,128)(2,1)S(1)} %bitcast.25, f32[288,128]{1,0:T(8,128)S(1)} %get-tuple-element.18.before_ref), custom_call_target="tpu_custom_call" | custom-call | flops 3000000000 | bytes 2244608 | tf_op jit(solution)/shard_map/last_departures/pallas_call | solution.py:248
  29.0 3.4 %all-to-all-start.2 = ((bf16[8,144,128]{2,1,0:T(8,128)(2,1)}), bf16[8,144,128]{2,1,0:T(8,128)(2,1)S(1)}, u32[]{:S(2)}, u32[]{:S(2)}) async-start(bf16[8,144,128]{2,1,0:T(8,128)(2,1)} %last_departures.1.after_ref), calls=%async_computation.2 | async-start | bytes 589824 | tf_op jit(solution)/shard_map/all_to_all | solution.py:536
  32.4 5.9 %collective-permute-start.1 = (s32[1,512]{1,0:T(1,128)S(1)}, s32[1,512]{1,0:T(1,128)S(1)}, u32[]{:S(2)}, u32[]{:S(2)}) collective-permute-start(s32[1,512]{1,0:T(1,128)S(1)} %get-tuple-element.14.after_ref.refs_0_), channel_id=1, source_target_pairs={{1,2},{2,1},{5,6},{6,5},{9,10},{10,9},{13,14},{14,13},{17,18},{18,... | collective-permute-start | bytes 6152 | tf_op jit(solution)/shard_map/ppermute | solution.py:559
  38.3 0.1 collective-permute-start
  38.4 0.0 copy-done.7
  38.4 0.1 reshape.141.lon_ref
  38.5 0.0 copy-done.8
  38.5 0.1 reshape.142.lat_ref
  38.6 0.0 copy-done.6
  38.6 0.2 reshape.140.vertical_ref
  38.8 0.3 tables.1
  39.0 0.5 collective-permute-done.1.far_ref.refs_2_
  39.6 0.0 collective-permute-done.near_ref.refs_4_
  39.6 0.2 all-to-all-done.2.products_ref
  39.7 0.4 impact_columns.1.refs_1_
  40.2 4.0 %collective-permute-start.3 = (bf16[144,768]{1,0:T(8,128)(2,1)S(1)}, bf16[144,768]{1,0:T(8,128)(2,1)S(1)}, u32[]{:S(2)}, u32[]{:S(2)}) collective-permute-start(bf16[144,768]{1,0:T(8,128)(2,1)S(1)} %impact_columns.1.refs_1_), channel_id=1, source_target_pairs={{0,1},{2,3},{1,0},{3,2},{4,5},{6,7},{5,4},{7,6},{8,9},{10,11},{9,8... | collective-permute-start | bytes 663560 | tf_op jit(solution)/shard_map/ppermute | solution.py:569
  44.1 3.0 %collective-permute-start.2 = (bf16[144,768]{1,0:T(8,128)(2,1)S(1)}, bf16[144,768]{1,0:T(8,128)(2,1)S(1)}, u32[]{:S(2)}, u32[]{:S(2)}) collective-permute-start(bf16[144,768]{1,0:T(8,128)(2,1)S(1)} %impact_columns.1.refs_1_), channel_id=1, source_target_pairs={{1,2},{2,1},{5,6},{6,5},{9,10},{10,9},{13,14},{14,13},{17,18},{18,... | collective-permute-start | bytes 663560 | tf_op jit(solution)/shard_map/ppermute | solution.py:570
  47.2 4.3 %inner_rows.1.refs_9_ = f32[274,32,128]{2,1,0:T(8,128)} custom-call(s32[1,512]{1,0:T(1,128)S(1)} %get-tuple-element.14.after_ref.refs_0_, bf16[144,768]{1,0:T(8,128)(2,1)S(1)} %impact_columns.1.refs_1_, bf16[2,144,384]{2,1,0:T(8,128)(2,1)S(1)} %get-tuple-element.20.tables_ref.refs_2_.refs_6_, f32[128,384]{1,0:T(8,128)S(1)} %get-tuple-element.21.refs_3_.refs_7_, ...), custom_call_target="tpu_custom_call" | custom-call | flops 44892160 | bytes 2244608 | tf_op jit(solution)/shard_map/inner_rows/pallas_call | solution.py:587
  51.5 0.0 collective-permute-done.3.refs_5_
  51.5 0.0 collective-permute-done.2.refs_3_
  51.5 5.1 %outer_rows.1 = f32[274,32,128]{2,1,0:T(8,128)} custom-call(s32[1,512]{1,0:T(1,128)S(1)} %get-tuple-element.14.after_ref.refs_0_, bf16[144,768]{1,0:T(8,128)(2,1)S(1)} %impact_columns.1.refs_1_, s32[1,512]{1,0:T(1,128)S(1)} %collective-permute-done.1.far_ref.refs_2_, ...), custom_call_target="tpu_custom_call", output_to_operand_aliasing={{}: (9, {})} | custom-call | flops 44892160 | bytes 2244608 | tf_op jit(solution)/shard_map/outer_rows/pallas_call | solution.py:587
  (4 shorter events, 0.0 us)
Async XLA Ops:
  1.3 11.6 %all-to-all-start = ((s32[8,1,64]{2,1,0:T(1,128)}), s32[8,1,64]{2,1,0:T(1,128)S(1)}, u32[]{:S(2)}, u32[]{:S(2)}) async-start(s32[8,1,64]{2,1,0:T(1,128)} %bitcast.2), calls=%async_computation | async-start | bytes 8192 | tf_op jit(solution)/shard_map/all_to_all | solution.py:493
  7.7 2.3 %copy-start = (f32[2,137,32,128]{3,2,1,0:T(8,128)S(1)}, f32[2,137,32,128]{3,2,1,0:T(8,128)}, u32[]{:S(2)}) copy-start(f32[2,137,32,128]{3,2,1,0:T(8,128)} %param.10) | copy-start | bytes 13467652
  10.0 8.5 %copy-start.2 = (bf16[1,64,128]{2,1,0:T(8,128)(2,1)S(1)}, bf16[1,64,128]{2,1,0:T(8,128)(2,1)}, u32[]{:S(2)}) copy-start(bf16[1,64,128]{2,1,0:T(8,128)(2,1)} %param.13) | copy-start | bytes 49156
  10.0 8.5 %copy-start.3 = (s32[1,64,1]{1,2,0:T(1,128)S(1)}, s32[1,64,1]{1,2,0:T(1,128)}, u32[]{:S(2)}) copy-start(s32[1,64,1]{1,2,0:T(1,128)} %param.15) | copy-start | bytes 772
  10.0 8.5 %copy-start.4 = (s32[1,64]{1,0:T(1,128)S(1)}, s32[1,64]{1,0:T(1,128)}, u32[]{:S(2)}) copy-start(s32[1,64]{1,0:T(1,128)} %valid_ref.1) | copy-start | bytes 772
  12.9 11.6 %copy-start.5 = (bf16[1,64,128]{2,1,0:T(8,128)(2,1)S(1)}, bf16[1,64,128]{2,1,0:T(8,128)(2,1)}, u32[]{:S(2)}) copy-start(bf16[1,64,128]{2,1,0:T(8,128)(2,1)} %param.12) | copy-start | bytes 49156
  14.9 9.7 %all-to-all-start.1 = ((bf16[8,16,384]{2,1,0:T(8,128)(2,1)}), bf16[8,16,384]{2,1,0:T(8,128)(2,1)S(1)}, u32[]{:S(2)}, u32[]{:S(2)}) async-start(bf16[8,16,384]{2,1,0:T(8,128)(2,1)} %bitcast.8), calls=%async_computation.1 | async-start | bytes 196608 | tf_op jit(solution)/shard_map/all_to_all | solution.py:498
  19.5 2.3 %copy-start.1 = (bf16[1,64,2,137,128]{4,2,3,1,0:T(2,128)(2,1)S(1)}, bf16[1,64,2,137,128]{4,2,3,1,0:T(2,128)(2,1)}, u32[]{:S(2)}) copy-start(bf16[1,64,2,137,128]{4,2,3,1,0:T(2,128)(2,1)} %param.11) | copy-start | bytes 13467652
  21.8 4.3 %slice-start = ((s8[4489216]{0:T(1024)(128)(4,1)}), s8[294912]{0:T(1024)(128)(4,1)S(1)}, s32[]{:S(2)}) async-start(s8[4489216]{0:T(1024)(128)(4,1)} %bitcast.23), calls=%async_computation.3 | async-start | bytes 589824
  24.5 2.2 %slice-start.1 = ((s8[4489216]{0:T(1024)(128)(4,1)}), s8[4194304]{0:T(1024)(128)(4,1)S(1)}, s32[]{:S(2)}) async-start(s8[4489216]{0:T(1024)(128)(4,1)} %bitcast.23), calls=%async_computation.4 | async-start | bytes 8388608
  26.7 11.7 %copy-start.7 = (f32[2,137,9]{1,0,2:T(2,128)S(1)}, f32[2,137,9]{1,0,2:T(2,128)}, u32[]{:S(2)}) copy-start(f32[2,137,9]{1,0,2:T(2,128)} %param.18) | copy-start | bytes 29596
  26.7 11.8 %copy-start.8 = (f32[2,137,9]{1,0,2:T(2,128)S(1)}, f32[2,137,9]{1,0,2:T(2,128)}, u32[]{:S(2)}) copy-start(f32[2,137,9]{1,0,2:T(2,128)} %param.19) | copy-start | bytes 29596
  26.7 11.9 %copy-start.6 = (bf16[2,137,137]{2,0,1:T(2,128)(2,1)S(1)}, bf16[2,137,137]{2,0,1:T(2,128)(2,1)}, u32[]{:S(2)}) copy-start(bf16[2,137,137]{2,0,1:T(2,128)(2,1)} %param.17) | copy-start | bytes 225232
  29.0 10.8 %all-to-all-start.2 = ((bf16[8,144,128]{2,1,0:T(8,128)(2,1)}), bf16[8,144,128]{2,1,0:T(8,128)(2,1)S(1)}, u32[]{:S(2)}, u32[]{:S(2)}) async-start(bf16[8,144,128]{2,1,0:T(8,128)(2,1)} %last_departures.1.after_ref), calls=%async_computation.2 | async-start | bytes 589824 | tf_op jit(solution)/shard_map/all_to_all | solution.py:536
  32.4 7.2 %collective-permute-start.1 = (s32[1,512]{1,0:T(1,128)S(1)}, s32[1,512]{1,0:T(1,128)S(1)}, u32[]{:S(2)}, u32[]{:S(2)}) collective-permute-start(s32[1,512]{1,0:T(1,128)S(1)} %get-tuple-element.14.after_ref.refs_0_), channel_id=1, source_target_pairs={{1,2},{2,1},{5,6},{6,5},{9,10},{10,9},{13,14},{14,13},{17,18},{18,... | collective-permute-start | bytes 6152 | tf_op jit(solution)/shard_map/ppermute | solution.py:559
  38.3 1.3 %collective-permute-start = (s32[1,512]{1,0:T(1,128)S(1)}, s32[1,512]{1,0:T(1,128)S(1)}, u32[]{:S(2)}, u32[]{:S(2)}) collective-permute-start(s32[1,512]{1,0:T(1,128)S(1)} %get-tuple-element.14.after_ref.refs_0_), channel_id=1, source_target_pairs={{0,1},{2,3},{1,0},{3,2},{4,5},{6,7},{5,4},{7,6},{8,9},{10,11},{9,8... | collective-permute-start | bytes 6152 | tf_op jit(solution)/shard_map/ppermute | solution.py:558
  40.2 11.3 %collective-permute-start.3 = (bf16[144,768]{1,0:T(8,128)(2,1)S(1)}, bf16[144,768]{1,0:T(8,128)(2,1)S(1)}, u32[]{:S(2)}, u32[]{:S(2)}) collective-permute-start(bf16[144,768]{1,0:T(8,128)(2,1)S(1)} %impact_columns.1.refs_1_), channel_id=1, source_target_pairs={{0,1},{2,3},{1,0},{3,2},{4,5},{6,7},{5,4},{7,6},{8,9},{10,11},{9,8... | collective-permute-start | bytes 663560 | tf_op jit(solution)/shard_map/ppermute | solution.py:569
  44.1 7.4 %collective-permute-start.2 = (bf16[144,768]{1,0:T(8,128)(2,1)S(1)}, bf16[144,768]{1,0:T(8,128)(2,1)S(1)}, u32[]{:S(2)}, u32[]{:S(2)}) collective-permute-start(bf16[144,768]{1,0:T(8,128)(2,1)S(1)} %impact_columns.1.refs_1_), channel_id=1, source_target_pairs={{1,2},{2,1},{5,6},{6,5},{9,10},{10,9},{13,14},{14,13},{17,18},{18,... | collective-permute-start | bytes 663560 | tf_op jit(solution)/shard_map/ppermute | solution.py:570
